TPU v7x, 32 devices: a whole 2x2x4 slice. The times are simulated.
32 devices in a mesh: tm: 8 (over y, x, core), tile: 4 (over z).
Axes of the slice: x: 2, y: 2, z: 4, core: 2. Of those that a mesh axis runs over, the one named last changes fastest.
Arguments:
- latent: bfloat16 [16, 16, 128, 16], P('tm', 'tile'), may hold values from -6 to 6
- cache_lat: bfloat16 [2, 16, 128, 16], P(None, 'tile'), may hold values from -6 to 6
- cache_one: bfloat16 [2, 16, 128, 384], P(None, 'tile'), may hold values from -6 to 6
- cache_two: bfloat16 [2, 16, 128, 384], P(None, 'tile'), may hold values from -6 to 6
- w_in: bfloat16 [3, 3, 3, 16, 384], replicated, may hold values from -0.3125 to 0.3125
- b_in: float32 [384], replicated, may hold values from -3 to 3
- gain_one: float32 [384], replicated, may hold values from 0.1 to 1.9
- w_one: bfloat16 [3, 3, 3, 384, 384], replicated, may hold values from -0.0625 to 0.0625
- b_one: float32 [384], replicated, may hold values from -3 to 3
- gain_two: float32 [384], replicated, may hold values from 0.1 to 1.9
- w_two: bfloat16 [3, 3, 3, 384, 384], replicated, may hold values from -0.0625 to 0.0625
- b_two: float32 [384], replicated, may hold values from -3 to 3
Outputs:
- decoded: bfloat16 [16, 16, 128, 384], P('tm', 'tile')
All inputs are finite; a program needn't handle non-finite values.
Results may differ from a plain program's by a relative error of at most 0.0051.
Values may be sent and summed in bfloat16 or wider, within the bound.
No kernel may reach another device: no remote copies, remote signals or barrier semaphores. Data moves between devices by JAX's collectives and lax.ppermute only.
A program may use at most 320 MiB of HBM per device.

v0:
```python
import jax
import jax.numpy as jnp
from jax import lax
from jax.sharding import PartitionSpec as P


def from_behind(x, axis, by):
    peers = lax.axis_size(axis)
    pairs = [(i, i + by) for i in range(peers) if 0 <= i + by < peers]
    return lax.ppermute(x, axis, pairs)


def padded_2(cells, sides, width):
    for axis, dim in sides:
        count = lax.axis_size(axis)
        ends = count - 1
        head = lax.slice_in_dim(cells, 0, width, axis=dim)
        tail = lax.slice_in_dim(cells, cells.shape[dim] - width, cells.shape[dim], axis=dim)
        cells = jnp.concatenate(
            [
                lax.ppermute(tail, axis, [(i, (i + 1) % count) for i in range(ends)]),
                cells,
                lax.ppermute(head, axis, [((i + 1) % count, i) for i in range(ends)]),
            ],
            axis=dim,
        )
    return cells


def framed(values, cache):
    starting = lax.axis_index("tm") == 0
    earlier = from_behind(values, "tm", 1)
    earlier = jnp.where(starting, cache, earlier)
    extended = jnp.concatenate([earlier, values], 0)
    extended = padded_2(extended, (("tile", 1),), 1)
    return extended


def conv_local(extended, kernel, bias):
    padded = jnp.pad(extended, ((0, 0), (0, 0), (1, 1), (0, 0)))
    frames = padded.shape[0] - 2
    height = padded.shape[1] - 2
    width = padded.shape[2] - 2
    chan = padded.shape[3]
    outc = kernel.shape[-1]
    if chan < 128:
        windows = []
        for dt in range(3):
            for dy in range(3):
                for dx in range(3):
                    windows.append(padded[dt : dt + frames, dy : dy + height, dx : dx + width])
        stacked = jnp.concatenate(windows, -1).reshape(-1, 27 * chan)
        total = jnp.dot(
            stacked, kernel.reshape(27 * chan, outc), preferred_element_type=jnp.float32
        )
        return total.reshape(frames, height, width, outc) + bias
    total = jnp.zeros((frames * height * width, outc), jnp.float32)
    for dt in range(3):
        windows = []
        for dy in range(3):
            for dx in range(3):
                windows.append(padded[dt : dt + frames, dy : dy + height, dx : dx + width])
        stacked = jnp.concatenate(windows, -1).reshape(-1, 9 * chan)
        total = total + jnp.dot(
            stacked, kernel[dt].reshape(9 * chan, outc), preferred_element_type=jnp.float32
        )
    return total.reshape(frames, height, width, outc) + bias


def rms_norm(values, gain):
    return values * lax.rsqrt(jnp.mean(values * values, -1, keepdims=True) + 1e-06) * gain


def on_device(
    latent,
    cache_lat,
    cache_one,
    cache_two,
    w_in,
    b_in,
    gain_one,
    w_one,
    b_one,
    gain_two,
    w_two,
    b_two,
):
    first = conv_local(framed(latent, cache_lat), w_in, b_in).astype(jnp.bfloat16)
    normed = jax.nn.silu(rms_norm(first.astype(jnp.float32), gain_one)).astype(jnp.bfloat16)
    middle = conv_local(framed(normed, cache_one), w_one, b_one)
    normed_two = jax.nn.silu(rms_norm(middle, gain_two)).astype(jnp.bfloat16)
    last = conv_local(framed(normed_two, cache_two), w_two, b_two)
    return (first.astype(jnp.float32) + last).astype(jnp.bfloat16)


def solution(mesh):
    return jax.shard_map(
        on_device,
        mesh=mesh,
        in_specs=(
            P("tm", "tile", None, None),
            P(None, "tile", None, None),
            P(None, "tile", None, None),
            P(None, "tile", None, None),
            P(),
            P(),
            P(),
            P(),
            P(),
            P(),
            P(),
            P(),
        ),
        out_specs=P("tm", "tile", None, None),
        check_vma=False,
    )
```

profile of v0, /device:TPU:2, one launch (start us, length us, event | category | flops | bytes accessed | tf_op | source)
XLA Modules:
  0.0 131.7 jit_solution(17782479042298627931)
XLA Ops:
  0.0 2.0 %collective-permute-start = (bf16[2,4,128,16]{2,3,1,0:T(8,128)(2,1)}, bf16[2,4,128,16]{2,3,1,0:T(8,128)(2,1)S(1)}, u32[]{:S(2)}, u32[]{:S(2)}) collective-permute-start(bf16[2,4,128,16]{2,3,1,0:T(8,128)(2,1)} %param.12), channel_id=1, source_target_pairs={{0,4},{4,8},{8,12},{12,16},{16,20},{20,24},{24,28},{1,5},{5,9},{9,... | collective-permute-start | bytes 98312 | tf_op jit(solution)/shard_map/ppermute | solution.py:10
  2.1 3.5 %collective-permute-done = bf16[2,4,128,16]{2,3,1,0:T(8,128)(2,1)S(1)} collective-permute-done((bf16[2,4,128,16]{2,3,1,0:T(8,128)(2,1)}, bf16[2,4,128,16]{2,3,1,0:T(8,128)(2,1)S(1)}, u32[]{:S(2)}, u32[]{:S(2)}) %collective-permute-start) | collective-permute-done | bytes 32800 | tf_op jit(solution)/shard_map/ppermute | solution.py:10
  6.3 3.5 %collective-permute-start.1 = (bf16[4,1,128,16]{2,3,1,0:T(8,128)(2,1)S(1)}, bf16[4,1,128,16]{2,3,1,0:T(8,128)(2,1)S(1)}, u32[]{:S(2)}, u32[]{:S(2)}) collective-permute-start(bf16[4,1,128,16]{2,3,1,0:T(8,128)(2,1)S(1)} %get-tuple-element.75), channel_id=1, source_target_pairs={{0,1},{1,2},{2,3},{4,5},{5,6},{6,7},{8,9},{9,10},{10,11},{12,13},{... | collective-permute-start | bytes 49160 | tf_op jit(solution)/shard_map/ppermute | solution.py:21
  11.2 4.2 %collective-permute-done.2 = bf16[4,1,128,16]{2,3,1,0:T(8,128)(2,1)S(1)} collective-permute-done((bf16[4,1,128,16]{2,3,1,0:T(8,128)(2,1)S(1)}, bf16[4,1,128,16]{2,3,1,0:T(8,128)(2,1)S(1)}, u32[]{:S(2)}, u32[]{:S(2)}) %collective-permute-start.2) | collective-permute-done | bytes 16416 | tf_op jit(solution)/shard_map/ppermute | solution.py:23
  19.8 1.5 %fusion.11 = (f32[2,4,128]{2,1,0:T(4,128)S(1)}, bf16[2,4,128,384]{3,2,1,0:T(8,128)(2,1)S(1)}) fusion(f32[384]{0:T(512)} %param.17, bf16[2,4,128,432]{2,3,1,0:T(8,128)(2,1)S(1)} %constant_dynamic-update-slice_fusion, bf16[432,384,1,1]{1,0,3,2:T(8,128)(2,1)S(1)} %bitcast.34), kind=kOutput, calls=%fused_computation.22 | convolution fusion | flops 341703680 | bytes 2008576 | tf_op jit(solution)/shard_map/dot_general | solution.py:53
  22.5 1.9 %collective-permute-start.3 = (bf16[2,4,128,384]{3,2,1,0:T(8,128)(2,1)S(1)}, bf16[2,4,128,384]{3,2,1,0:T(8,128)(2,1)S(1)}, u32[]{:S(2)}, u32[]{:S(2)}) collective-permute-start(bf16[2,4,128,384]{3,2,1,0:T(8,128)(2,1)S(1)} %fusion.18), channel_id=1, source_target_pairs={{0,4},{4,8},{8,12},{12,16},{16,20},{20,24},{24,28},{1,5},{5,9},{9,... | collective-permute-start | bytes 2359304 | tf_op jit(solution)/shard_map/ppermute | solution.py:10
  24.5 11.4 %collective-permute-done.3 = bf16[2,4,128,384]{3,2,1,0:T(8,128)(2,1)S(1)} collective-permute-done((bf16[2,4,128,384]{3,2,1,0:T(8,128)(2,1)S(1)}, bf16[2,4,128,384]{3,2,1,0:T(8,128)(2,1)S(1)}, u32[]{:S(2)}, u32[]{:S(2)}) %collective-permute-start.3) | collective-permute-done | bytes 786464 | tf_op jit(solution)/shard_map/ppermute | solution.py:10
  36.1 3.5 %collective-permute-start.4 = (bf16[4,1,128,384]{3,2,1,0:T(8,128)(2,1)S(1)}, bf16[4,1,128,384]{3,2,1,0:T(8,128)(2,1)S(1)}, u32[]{:S(2)}, u32[]{:S(2)}) collective-permute-start(bf16[4,1,128,384]{3,2,1,0:T(8,128)(2,1)S(1)} %get-tuple-element.65), channel_id=1, source_target_pairs={{0,1},{1,2},{2,3},{4,5},{5,6},{6,7},{8,9},{9,10},{10,11},{12,13},{... | collective-permute-start | bytes 1179656 | tf_op jit(solution)/shard_map/ppermute | solution.py:21
  40.9 1.4 %fusion.27 = (bf16[1,3,3,384,384]{4,3,2,1,0:T(8,128)(2,1)S(1)}, bf16[1,3,3,384,384]{4,3,2,1,0:T(8,128)(2,1)S(1)}, bf16[1,3,3,384,384]{4,3,2,1,0:T(8,128)(2,1)S(1)}) fusion(bf16[3,3,3,384,384]{4,3,2,1,0:T(8,128)(2,1)S(1)} %copy-done.2), kind=kLoop, calls=%fused_computation.142 | loop fusion | bytes 15925248 | tf_op jit(solution)/shard_map/slice | solution.py:65
  42.3 5.8 %collective-permute-done.4 = bf16[4,1,128,384]{3,2,1,0:T(8,128)(2,1)S(1)} collective-permute-done((bf16[4,1,128,384]{3,2,1,0:T(8,128)(2,1)S(1)}, bf16[4,1,128,384]{3,2,1,0:T(8,128)(2,1)S(1)}, u32[]{:S(2)}, u32[]{:S(2)}) %collective-permute-start.4) | collective-permute-done | bytes 393248 | tf_op jit(solution)/shard_map/ppermute | solution.py:21
  48.1 4.1 %collective-permute-done.5 = bf16[4,1,128,384]{3,2,1,0:T(8,128)(2,1)S(1)} collective-permute-done((bf16[4,1,128,384]{3,2,1,0:T(8,128)(2,1)S(1)}, bf16[4,1,128,384]{3,2,1,0:T(8,128)(2,1)S(1)}, u32[]{:S(2)}, u32[]{:S(2)}) %collective-permute-start.5) | collective-permute-done | bytes 393248 | tf_op jit(solution)/shard_map/ppermute | solution.py:23
  52.2 1.7 %fusion.8 = bf16[4,6,130,384]{3,2,1,0:T(8,128)(2,1)S(1)} fusion(bf16[4,1,128,384]{3,2,1,0:T(8,128)(2,1)S(1)} %collective-permute-done.5, bf16[4,1,128,384]{3,2,1,0:T(8,128)(2,1)S(1)} %collective-permute-done.4, bf16[2,4,128,384]{3,2,1,0:T(8,128)(2,1)S(1)} %fusion.18, bf16[2,4,128,384]{3,2,1,0:T(8,128)(2,1)S(1)} %broadcast_select_fusion.1), kind=kLoop, calls=%fused_computation.12 | loop fusion | flops 17971200 | bytes 4755456 | tf_op jit(solution)/shard_map/concatenate | solution.py:19
  60.9 3.9 %fusion.28 = f32[1024,384]{1,0:T(8,128)S(1)} fusion(bf16[1024,3456]{1,0:T(8,128)(2,1)S(1)} %bitcast.47, bf16[3456,384]{1,0:T(8,128)(2,1)S(1)} %bitcast.41), kind=kOutput, calls=%fused_computation.143 | convolution fusion | flops 2717908992 | bytes 11304960 | tf_op jit(solution)/shard_map/dot_general | solution.py:64
  64.7 3.9 %fusion.29 = f32[1024,384]{1,0:T(8,128)S(1)} fusion(bf16[1024,3456]{1,0:T(8,128)(2,1)S(1)} %bitcast.46, bf16[3456,384]{1,0:T(8,128)(2,1)S(1)} %bitcast.39), kind=kOutput, calls=%fused_computation.144 | convolution fusion | flops 2717908992 | bytes 11304960 | tf_op jit(solution)/shard_map/dot_general | solution.py:64
  68.7 4.1 %multiply_reduce_fusion = (f32[1024]{0:T(1024)S(1)}, f32[1024,384]{1,0:T(8,128)S(1)}) fusion(f32[384]{0:T(512)S(1)} %copy-done.5, bf16[1024,3456]{1,0:T(8,128)(2,1)S(1)} %bitcast.45, bf16[3456,384]{1,0:T(8,128)(2,1)S(1)} %bitcast.37, f32[1024,384]{1,0:T(8,128)S(1)} %fusion.28, f32[1024,384]{1,0:T(8,128)S(1)} %fusion.29), kind=kOutput, calls=%fused_computation.33 | convolution fusion | flops 2719874048 | bytes 14456320 | tf_op jit(solution)/shard_map/dot_general | solution.py:64
  73.3 2.1 %collective-permute-start.6 = (bf16[2,4,128,384]{3,2,1,0:T(8,128)(2,1)S(1)}, bf16[2,4,128,384]{3,2,1,0:T(8,128)(2,1)S(1)}, u32[]{:S(2)}, u32[]{:S(2)}) collective-permute-start(bf16[2,4,128,384]{3,2,1,0:T(8,128)(2,1)S(1)} %multiply_convert_fusion), channel_id=1, source_target_pairs={{0,4},{4,8},{8,12},{12,16},{16,20},{20,24},{24,28},{1,5},{5,9},{9,... | collective-permute-start | bytes 2359304 | tf_op jit(solution)/shard_map/ppermute | solution.py:10
  75.5 11.2 %collective-permute-done.6 = bf16[2,4,128,384]{3,2,1,0:T(8,128)(2,1)S(1)} collective-permute-done((bf16[2,4,128,384]{3,2,1,0:T(8,128)(2,1)S(1)}, bf16[2,4,128,384]{3,2,1,0:T(8,128)(2,1)S(1)}, u32[]{:S(2)}, u32[]{:S(2)}) %collective-permute-start.6) | collective-permute-done | bytes 786464 | tf_op jit(solution)/shard_map/ppermute | solution.py:10
  86.8 3.5 %collective-permute-start.7 = (bf16[4,1,128,384]{3,2,1,0:T(8,128)(2,1)S(1)}, bf16[4,1,128,384]{3,2,1,0:T(8,128)(2,1)S(1)}, u32[]{:S(2)}, u32[]{:S(2)}) collective-permute-start(bf16[4,1,128,384]{3,2,1,0:T(8,128)(2,1)S(1)} %get-tuple-element.61), channel_id=1, source_target_pairs={{0,1},{1,2},{2,3},{4,5},{5,6},{6,7},{8,9},{9,10},{10,11},{12,13},{... | collective-permute-start | bytes 1179656 | tf_op jit(solution)/shard_map/ppermute | solution.py:21
  91.6 1.4 %fusion.26 = (bf16[1,3,3,384,384]{4,3,2,1,0:T(8,128)(2,1)S(1)}, bf16[1,3,3,384,384]{4,3,2,1,0:T(8,128)(2,1)S(1)}, bf16[1,3,3,384,384]{4,3,2,1,0:T(8,128)(2,1)S(1)}) fusion(bf16[3,3,3,384,384]{4,3,2,1,0:T(8,128)(2,1)S(1)} %bitcast.36), kind=kLoop, calls=%fused_computation.141 | loop fusion | bytes 15925248 | tf_op jit(solution)/shard_map/slice | solution.py:65
  93.0 4.0 %collective-permute-done.7 = bf16[4,1,128,384]{3,2,1,0:T(8,128)(2,1)S(1)} collective-permute-done((bf16[4,1,128,384]{3,2,1,0:T(8,128)(2,1)S(1)}, bf16[4,1,128,384]{3,2,1,0:T(8,128)(2,1)S(1)}, u32[]{:S(2)}, u32[]{:S(2)}) %collective-permute-start.7) | collective-permute-done | bytes 393248 | tf_op jit(solution)/shard_map/ppermute | solution.py:21
  97.0 4.1 %collective-permute-done.8 = bf16[4,1,128,384]{3,2,1,0:T(8,128)(2,1)S(1)} collective-permute-done((bf16[4,1,128,384]{3,2,1,0:T(8,128)(2,1)S(1)}, bf16[4,1,128,384]{3,2,1,0:T(8,128)(2,1)S(1)}, u32[]{:S(2)}, u32[]{:S(2)}) %collective-permute-start.8) | collective-permute-done | bytes 393248 | tf_op jit(solution)/shard_map/ppermute | solution.py:23
  101.2 1.7 %select_maximum_fusion = bf16[4,6,130,384]{3,2,1,0:T(8,128)(2,1)S(1)} fusion(bf16[4,1,128,384]{3,2,1,0:T(8,128)(2,1)S(1)} %collective-permute-done.8, bf16[4,1,128,384]{3,2,1,0:T(8,128)(2,1)S(1)} %collective-permute-done.7, bf16[2,4,128,384]{3,2,1,0:T(8,128)(2,1)S(1)} %multiply_convert_fusion, bf16[2,4,128,384]{3,2,1,0:T(8,128)(2,1)S(1)} %broadcast_select_fusion), kind=kLoop, calls=%fused_computation.3 | loop fusion | flops 17971200 | bytes 4755456 | tf_op jit(solution)/shard_map/concatenate | solution.py:19
  104.8 1.4 %slice_dynamic-update-slice_fusion.6 = (bf16[2,4,128,3456]{3,2,1,0:T(8,128)(2,1)S(1)}, bf16[2,4,128,3456]{3,2,1,0:T(8,128)(2,1)S(1)}, bf16[2,4,128,3456]{3,2,1,0:T(8,128)(2,1)}) fusion(bf16[2,4,128,3456]{3,2,1,0:T(8,128)(2,1)S(1)} %get-tuple-element.26, bf16[4,5,128,384]{3,2,1,0:T(8,128)(2,1)S(1)} %get-tuple-element.60, ...), kind=kLoop, calls=%fused_computation.42 | loop fusion | bytes 4718592
  106.2 1.7 %slice_dynamic-update-slice_fusion.5 = (bf16[2,4,128,3456]{3,2,1,0:T(8,128)(2,1)S(1)}, bf16[2,4,128,3456]{3,2,1,0:T(8,128)(2,1)S(1)}, bf16[2,4,128,3456]{3,2,1,0:T(8,128)(2,1)}) fusion(bf16[2,4,128,3456]{3,2,1,0:T(8,128)(2,1)S(1)} %get-tuple-element.50, bf16[4,6,130,384]{3,2,1,0:T(8,128)(2,1)S(1)} %select_maximum_fusion, ...), kind=kLoop, calls=%fused_computation.41 | loop fusion | bytes 4718592
  109.2 1.4 %constant_dynamic-update-slice_fusion.30 = (bf16[2,4,128,3456]{3,2,1,0:T(8,128)(2,1)S(1)}, bf16[2,4,128,3456]{3,2,1,0:T(8,128)(2,1)S(1)}, bf16[2,4,128,3456]{3,2,1,0:T(8,128)(2,1)}) fusion(bf16[2,4,128,3456]{3,2,1,0:T(8,128)(2,1)S(1)} %get-tuple-element.20, bf16[2,4,128,384]{3,2,1,0:T(8,128)(2,1)S(1)} %multiply_convert_fusion, ...), kind=kLoop, calls=%fused_computation.132 | loop fusion | flops 1572864 | bytes 3932160
  110.6 1.7 %slice_dynamic-update-slice_fusion.3 = (bf16[2,4,128,3456]{3,2,1,0:T(8,128)(2,1)S(1)}, bf16[2,4,128,3456]{3,2,1,0:T(8,128)(2,1)S(1)}, bf16[2,4,128,3456]{3,2,1,0:T(8,128)(2,1)}) fusion(bf16[2,4,128,3456]{3,2,1,0:T(8,128)(2,1)S(1)} %get-tuple-element.67, bf16[4,6,130,384]{3,2,1,0:T(8,128)(2,1)S(1)} %select_maximum_fusion, ...), kind=kLoop, calls=%fused_computation.39 | loop fusion | bytes 4718592
  112.3 1.4 %slice_dynamic-update-slice_fusion.2 = (bf16[2,4,128,3456]{3,2,1,0:T(8,128)(2,1)S(1)}, bf16[2,4,128,3456]{3,2,1,0:T(8,128)(2,1)S(1)}, bf16[2,4,128,3456]{3,2,1,0:T(8,128)(2,1)}) fusion(bf16[2,4,128,3456]{3,2,1,0:T(8,128)(2,1)S(1)} %get-tuple-element.17, bf16[4,6,130,384]{3,2,1,0:T(8,128)(2,1)S(1)} %select_maximum_fusion, ...), kind=kLoop, calls=%fused_computation.38 | loop fusion | bytes 4718592
  113.7 1.4 %slice_dynamic-update-slice_fusion.1 = (bf16[2,4,128,3456]{3,2,1,0:T(8,128)(2,1)S(1)}, bf16[2,4,128,3456]{3,2,1,0:T(8,128)(2,1)S(1)}, bf16[2,4,128,3456]{3,2,1,0:T(8,128)(2,1)}) fusion(bf16[2,4,128,3456]{3,2,1,0:T(8,128)(2,1)S(1)} %get-tuple-element.14, bf16[4,5,128,384]{3,2,1,0:T(8,128)(2,1)S(1)} %get-tuple-element.59, ...), kind=kLoop, calls=%fused_computation.37 | loop fusion | bytes 4718592
  115.1 1.7 %slice_dynamic-update-slice_fusion = (bf16[2,4,128,3456]{3,2,1,0:T(8,128)(2,1)S(1)}, bf16[2,4,128,3456]{3,2,1,0:T(8,128)(2,1)S(1)}, bf16[2,4,128,3456]{3,2,1,0:T(8,128)(2,1)}) fusion(bf16[2,4,128,3456]{3,2,1,0:T(8,128)(2,1)S(1)} %get-tuple-element.47, bf16[4,6,130,384]{3,2,1,0:T(8,128)(2,1)S(1)} %select_maximum_fusion, ...), kind=kLoop, calls=%fused_computation.36 | loop fusion | bytes 4718592 | tf_op jit(solution)/shard_map/concatenate | solution.py:63
  116.8 6.1 %fusion.30 = f32[1024,384]{1,0:T(8,128)S(1)} fusion(bf16[1024,3456]{1,0:T(8,128)(2,1)} %bitcast.50, bf16[3456,384]{1,0:T(8,128)(2,1)S(1)} %bitcast.42), kind=kOutput, calls=%fused_computation.145 | convolution fusion | flops 2717908992 | bytes 11304960 | tf_op jit(solution)/shard_map/dot_general | solution.py:64
  122.8 3.9 %fusion.31 = f32[1024,384]{1,0:T(8,128)S(1)} fusion(bf16[1024,3456]{1,0:T(8,128)(2,1)S(1)} %bitcast.49, bf16[3456,384]{1,0:T(8,128)(2,1)S(1)} %bitcast.40), kind=kOutput, calls=%fused_computation.146 | convolution fusion | flops 2717908992 | bytes 11304960 | tf_op jit(solution)/shard_map/dot_general | solution.py:64
  126.7 3.9 %add_add_fusion = f32[1024,384]{1,0:T(8,128)S(1)} fusion(f32[1024,384]{1,0:T(8,128)S(1)} %fusion.30, f32[1024,384]{1,0:T(8,128)S(1)} %fusion.31, bf16[1024,3456]{1,0:T(8,128)(2,1)S(1)} %bitcast.48, bf16[3456,384]{1,0:T(8,128)(2,1)S(1)} %bitcast.38), kind=kOutput, calls=%fused_computation.31 | convolution fusion | flops 2718695424 | bytes 14450688 | tf_op jit(solution)/shard_map/dot_general | solution.py:64
  (78 shorter events, 22.3 us)
Async XLA Ops:
  0.0 19.8 %copy-start = (bf16[3,3,3,16,384]{4,3,2,1,0:T(8,128)(2,1)S(1)}, bf16[3,3,3,16,384]{4,3,2,1,0:T(8,128)(2,1)}, u32[]{:S(2)}) copy-start(bf16[3,3,3,16,384]{4,3,2,1,0:T(8,128)(2,1)} %param.16) | copy-start | bytes 995332
  0.0 35.9 %copy-start.3 = (bf16[2,4,128,384]{3,2,1,0:T(8,128)(2,1)S(1)}, bf16[2,4,128,384]{3,2,1,0:T(8,128)(2,1)}, u32[]{:S(2)}) copy-start(bf16[2,4,128,384]{3,2,1,0:T(8,128)(2,1)} %param.14) | copy-start | bytes 2359300
  0.0 5.6 %collective-permute-start = (bf16[2,4,128,16]{2,3,1,0:T(8,128)(2,1)}, bf16[2,4,128,16]{2,3,1,0:T(8,128)(2,1)S(1)}, u32[]{:S(2)}, u32[]{:S(2)}) collective-permute-start(bf16[2,4,128,16]{2,3,1,0:T(8,128)(2,1)} %param.12), channel_id=1, source_target_pairs={{0,4},{4,8},{8,12},{12,16},{16,20},{20,24},{24,28},{1,5},{5,9},{9,... | collective-permute-start | bytes 98312 | tf_op jit(solution)/shard_map/ppermute | solution.py:10
  2.1 38.8 %copy-start.2 = (bf16[3,3,3,384,384]{4,3,2,1,0:T(8,128)(2,1)S(1)}, bf16[3,3,3,384,384]{4,3,2,1,0:T(8,128)(2,1)}, u32[]{:S(2)}) copy-start(bf16[3,3,3,384,384]{4,3,2,1,0:T(8,128)(2,1)} %param.19) | copy-start | bytes 23887876
  6.3 4.9 %collective-permute-start.1 = (bf16[4,1,128,16]{2,3,1,0:T(8,128)(2,1)S(1)}, bf16[4,1,128,16]{2,3,1,0:T(8,128)(2,1)S(1)}, u32[]{:S(2)}, u32[]{:S(2)}) collective-permute-start(bf16[4,1,128,16]{2,3,1,0:T(8,128)(2,1)S(1)} %get-tuple-element.75), channel_id=1, source_target_pairs={{0,1},{1,2},{2,3},{4,5},{5,6},{6,7},{8,9},{9,10},{10,11},{12,13},{... | collective-permute-start | bytes 49160 | tf_op jit(solution)/shard_map/ppermute | solution.py:21
  9.8 5.6 %collective-permute-start.2 = (bf16[4,1,128,16]{2,3,1,0:T(8,128)(2,1)S(1)}, bf16[4,1,128,16]{2,3,1,0:T(8,128)(2,1)S(1)}, u32[]{:S(2)}, u32[]{:S(2)}) collective-permute-start(bf16[4,1,128,16]{2,3,1,0:T(8,128)(2,1)S(1)} %get-tuple-element.76), channel_id=1, source_target_pairs={{1,0},{2,1},{3,2},{5,4},{6,5},{7,6},{9,8},{10,9},{11,10},{13,12},{... | collective-permute-start | bytes 49160 | tf_op jit(solution)/shard_map/ppermute | solution.py:23
  22.5 13.3 %collective-permute-start.3 = (bf16[2,4,128,384]{3,2,1,0:T(8,128)(2,1)S(1)}, bf16[2,4,128,384]{3,2,1,0:T(8,128)(2,1)S(1)}, u32[]{:S(2)}, u32[]{:S(2)}) collective-permute-start(bf16[2,4,128,384]{3,2,1,0:T(8,128)(2,1)S(1)} %fusion.18), channel_id=1, source_target_pairs={{0,4},{4,8},{8,12},{12,16},{16,20},{20,24},{24,28},{1,5},{5,9},{9,... | collective-permute-start | bytes 2359304 | tf_op jit(solution)/shard_map/ppermute | solution.py:10
  36.1 12.0 %collective-permute-start.4 = (bf16[4,1,128,384]{3,2,1,0:T(8,128)(2,1)S(1)}, bf16[4,1,128,384]{3,2,1,0:T(8,128)(2,1)S(1)}, u32[]{:S(2)}, u32[]{:S(2)}) collective-permute-start(bf16[4,1,128,384]{3,2,1,0:T(8,128)(2,1)S(1)} %get-tuple-element.65), channel_id=1, source_target_pairs={{0,1},{1,2},{2,3},{4,5},{5,6},{6,7},{8,9},{9,10},{10,11},{12,13},{... | collective-permute-start | bytes 1179656 | tf_op jit(solution)/shard_map/ppermute | solution.py:21
  39.6 12.7 %collective-permute-start.5 = (bf16[4,1,128,384]{3,2,1,0:T(8,128)(2,1)S(1)}, bf16[4,1,128,384]{3,2,1,0:T(8,128)(2,1)S(1)}, u32[]{:S(2)}, u32[]{:S(2)}) collective-permute-start(bf16[4,1,128,384]{3,2,1,0:T(8,128)(2,1)S(1)} %get-tuple-element.66), channel_id=1, source_target_pairs={{1,0},{2,1},{3,2},{5,4},{6,5},{7,6},{9,8},{10,9},{11,10},{13,12},{... | collective-permute-start | bytes 1179656 | tf_op jit(solution)/shard_map/ppermute | solution.py:23
  64.7 3.9 %copy-start.5 = (f32[384]{0:T(512)S(1)}, f32[384]{0:T(512)}, u32[]{:S(2)}) copy-start(f32[384]{0:T(512)} %param.20) | copy-start | bytes 4612
  68.6 23.0 %slice-start = ((s8[7962624]{0:T(1024)(128)(4,1)}), s8[4194304]{0:T(1024)(128)(4,1)S(1)}, s32[]{:S(2)}) async-start(s8[7962624]{0:T(1024)(128)(4,1)} %bitcast.35), calls=%async_computation | async-start | bytes 8388608
  68.6 4.1 %copy-start.6 = (f32[384]{0:T(512)S(1)}, f32[384]{0:T(512)}, u32[]{:S(2)}) copy-start(f32[384]{0:T(512)} %param.21) | copy-start | bytes 4612
  68.6 18.0 %copy-start.4 = (bf16[2,4,128,384]{3,2,1,0:T(8,128)(2,1)S(1)}, bf16[2,4,128,384]{3,2,1,0:T(8,128)(2,1)}, u32[]{:S(2)}) copy-start(bf16[2,4,128,384]{3,2,1,0:T(8,128)(2,1)} %param.15) | copy-start | bytes 2359300
  68.7 23.0 %slice-start.1 = ((s8[7962624]{0:T(1024)(128)(4,1)}), s8[3768320]{0:T(1024)(128)(4,1)S(1)}, s32[]{:S(2)}) async-start(s8[7962624]{0:T(1024)(128)(4,1)} %bitcast.35), calls=%async_computation.1 | async-start | bytes 7536640
  73.3 13.3 %collective-permute-start.6 = (bf16[2,4,128,384]{3,2,1,0:T(8,128)(2,1)S(1)}, bf16[2,4,128,384]{3,2,1,0:T(8,128)(2,1)S(1)}, u32[]{:S(2)}, u32[]{:S(2)}) collective-permute-start(bf16[2,4,128,384]{3,2,1,0:T(8,128)(2,1)S(1)} %multiply_convert_fusion), channel_id=1, source_target_pairs={{0,4},{4,8},{8,12},{12,16},{16,20},{20,24},{24,28},{1,5},{5,9},{9,... | collective-permute-start | bytes 2359304 | tf_op jit(solution)/shard_map/ppermute | solution.py:10
  86.8 10.2 %collective-permute-start.7 = (bf16[4,1,128,384]{3,2,1,0:T(8,128)(2,1)S(1)}, bf16[4,1,128,384]{3,2,1,0:T(8,128)(2,1)S(1)}, u32[]{:S(2)}, u32[]{:S(2)}) collective-permute-start(bf16[4,1,128,384]{3,2,1,0:T(8,128)(2,1)S(1)} %get-tuple-element.61), channel_id=1, source_target_pairs={{0,1},{1,2},{2,3},{4,5},{5,6},{6,7},{8,9},{9,10},{10,11},{12,13},{... | collective-permute-start | bytes 1179656 | tf_op jit(solution)/shard_map/ppermute | solution.py:21
  90.3 10.9 %collective-permute-start.8 = (bf16[4,1,128,384]{3,2,1,0:T(8,128)(2,1)S(1)}, bf16[4,1,128,384]{3,2,1,0:T(8,128)(2,1)S(1)}, u32[]{:S(2)}, u32[]{:S(2)}) collective-permute-start(bf16[4,1,128,384]{3,2,1,0:T(8,128)(2,1)S(1)} %get-tuple-element.62), channel_id=1, source_target_pairs={{1,0},{2,1},{3,2},{5,4},{6,5},{7,6},{9,8},{10,9},{11,10},{13,12},{... | collective-permute-start | bytes 1179656 | tf_op jit(solution)/shard_map/ppermute | solution.py:23
  126.7 5.0 %copy-start.1 = (bf16[3,3,3,16,384]{4,3,2,1,0:T(8,128)(2,1)S(1)}, bf16[3,3,3,16,384]{4,3,2,1,0:T(8,128)(2,1)}, u32[]{:S(2)}) copy-start(bf16[3,3,3,16,384]{4,3,2,1,0:T(8,128)(2,1)} %param.16) | copy-start | bytes 995332
  126.7 3.9 %copy-start.7 = (f32[384]{0:T(512)S(1)}, f32[384]{0:T(512)}, u32[]{:S(2)}) copy-start(f32[384]{0:T(512)} %param.23) | copy-start | bytes 4612
where the time goes:
time: 132 us
  waiting for transfers between devices  48.5 us (37%)
  matrix products  27.1 us (21%)
  local copies, waits for them, and re-layouts  21.9 us (17%)
  starting transfers between devices  20.4 us (15%)
  other arithmetic  13.2 us (10%)
    ppermute x3, waiting for transfers between devices, from_behind(): return lax.ppermute(x, axis, pairs)  26 us
    dot_general x6, matrix products, conv_local(): jnp.dot(stacked, kernel[dt].reshape(9 * chan, outc), preferred_element_ty...  25.6 us
    unnamed x59, local copies, waits for them, and re-layouts  16.5 us
    ppermute x3, waiting for transfers between devices, padded_2(): lax.ppermute(head, axis, [((i + 1) % count, i) for i in range(ends)])  12.5 us
    ppermute x3, starting transfers between devices, padded_2(): lax.ppermute(tail, axis, [(i, (i + 1) % count) for i in range(ends)])  10.5 us
    ppermute x3, waiting for transfers between devices, padded_2(): lax.ppermute(tail, axis, [(i, (i + 1) % count) for i in range(ends)])  9.98 us
    concatenate x6, other arithmetic, padded_2(): jnp.concatenate([lax.ppermute(tail, axis, [(i, (i + 1) % count) for i in...  6.57 us
    ppermute x3, starting transfers between devices, from_behind(): return lax.ppermute(x, axis, pairs)  6.1 us
  transfers between devices with their start and end apart: 9, of which 9 were waited for; matrix products, arithmetic and copies ran while one was open for 2% of the time, Pallas kernels for 0%

commit v1 on v0

v1 whole, which is shorter than its diff:
```python
import functools

import jax
import jax.numpy as jnp
from jax import lax
from jax.experimental import pallas as pl
from jax.experimental.pallas import tpu as pltpu
from jax.sharding import PartitionSpec as P

BF = jnp.bfloat16
F32 = jnp.float32
VMEM = pltpu.VMEM


def shifted(x, axis, by):
    count = lax.axis_size(axis)
    return lax.ppermute(x, axis, [(i, i + by) for i in range(count) if 0 <= i + by < count])


def first_frames_only(x, by):
    rows = lax.axis_size("tile")
    return lax.ppermute(
        x, ("tm", "tile"), [(i, i + by) for i in range(rows) if 0 <= i + by < rows]
    )


def column_of(place, width):
    half = width // 2
    return jnp.where(place < half, 2 * place, 2 * (place - half) + 1)


def silu(v):
    return 0.5 * v * (1.0 + jnp.tanh(0.5 * v))


def rms(v, gain):
    return v * lax.rsqrt(jnp.mean(v * v, -1, keepdims=True) + 1e-6) * gain


def filtered(even, odd):
    half = even.shape[0]
    place = lax.broadcasted_iota(jnp.int32, even.shape, 0)
    odd_before = jnp.where(place == 0, 0.0, pltpu.roll(odd, 1, 0))
    even_after = jnp.where(place == half - 1, 0.0, pltpu.roll(even, half - 1, 0))
    return (
        (odd_before - odd).astype(BF),
        (even + odd).astype(BF),
        (odd - even).astype(BF),
        (even - even_after).astype(BF),
    )


def kernel_sums(w_ref, u_ref):
    g0 = w_ref[0, 0].astype(F32)
    g1 = w_ref[0, 1].astype(F32)
    g2 = w_ref[0, 2].astype(F32)
    s = 0.5 * (g0 + g2)
    h = 0.5 * g1
    u_ref[0, 0] = (s + h).astype(BF)
    u_ref[1, 0] = (s - h).astype(BF)


def summed_kernels(w):
    c, o = w.shape[-2:]
    return pl.pallas_call(
        kernel_sums,
        grid=(9,),
        in_specs=[pl.BlockSpec((1, 3, c, o), lambda i: (i, 0, 0, 0))],
        out_specs=pl.BlockSpec((2, 1, c, o), lambda i: (0, i, 0, 0)),
        out_shape=jax.ShapeDtypeStruct((2, 9, c, o), BF),
        name="kernel_sums",
        cost_estimate=pl.CostEstimate(flops=6 * 9 * c * o, bytes_accessed=10 * 9 * c * o, transcendentals=0),
    )(w.reshape(9, 3, c, o))


def weight_copies(w_hbm, u_hbm, w_v, sems, dts):
    out = []
    for j in range(4):
        row = []
        for dt in dts:
            taps = pl.ds(3 * dt, 3)
            if j == 0:
                src = w_hbm.at[taps, 0]
            elif j == 3:
                src = w_hbm.at[taps, 2]
            else:
                src = u_hbm.at[j - 1, taps]
            row.append(pltpu.make_async_copy(src, w_v.at[j, taps], sems.at[j, dt]))
        out.append(row)
    return out


def taps_of(w_v, j, dt):
    return jnp.concatenate([w_v[j, 3 * dt + dy] for dy in range(3)], 0)


def both(w_v, j, dt_a, dt_b):
    return jnp.concatenate([taps_of(w_v, j, dt_a), taps_of(w_v, j, dt_b)], 1)


def rows_of(v, f, j, rows):
    half, c = v.shape[-2:]
    return jnp.concatenate(
        [v[f, j, dy : dy + rows].reshape(rows * half, c) for dy in range(3)], 1
    )


def dot(a, b):
    return jnp.dot(a, b, preferred_element_type=F32)


def first_conv_body(
    tiles,
    own, prev1, prev2, cache_lat, cache_one, cache_up, cache_dn,
    w_in, b_in, gain_one, w_hbm, u_hbm, b_one, gain_two,
    n2_ref, h0_ref,
    lats, v, w_v, acc, sems,
):
    tm = lax.axis_index("tm")
    tile = lax.axis_index("tile")
    width = own.shape[-1]
    half = width // 2
    chan = w_in.shape[0] // 27
    lat_rows = own.shape[0] // (2 * chan)
    rows1 = lat_rows - 2
    rows2 = rows1 - 2
    rows = rows2 - 2
    c = w_in.shape[1]
    copies = weight_copies(w_hbm, u_hbm, w_v, sems, (0, 1, 2))
    for row in copies:
        for copy in row:
            copy.start()

    to = column_of(lax.broadcasted_iota(jnp.int32, (width, width), 1), width)
    at = lax.broadcasted_iota(jnp.int32, (width, width), 0)
    frame = 2 * lat_rows * chan
    for dx in range(3):
        place = jnp.where(at == to + (dx - 1), 1.0, 0.0).astype(BF)
        two = jnp.where(tm == 1, cache_lat[...], prev2[...])
        one = jnp.where(tm == 0, cache_lat[...], prev1[...])
        lats[dx, 0:frame] = dot(two, place).astype(BF)
        lats[dx, frame : 2 * frame] = dot(one, place).astype(BF)
        lats[dx, 2 * frame : 3 * frame] = dot(own[...], place).astype(BF)

    def valid(r, margin):
        at_row = tile * rows + r - margin
        return jnp.logical_and(at_row >= 0, at_row < tiles * rows)

    def put(f, r, n1):
        parts = filtered(n1[:half], n1[half:])
        for j in range(4):
            v[f, j, r] = parts[j]

    def normed(i, _):
        f = i // (rows1 // 2)
        r0 = 2 * (i % (rows1 // 2))
        patches = []
        for k in range(2):
            pieces = []
            for dt in range(3):
                for dy in range(3):
                    start = pl.multiple_of(((f + dt) * lat_rows + r0 + k + dy) * chan, chan)
                    for dx in range(3):
                        pieces.append(lats[dx, pl.ds(start, chan)])
            patches.append(jnp.concatenate(pieces, 0))
        patches = jnp.concatenate(patches, 1)
        h0 = lax.dot_general(
            patches, w_in[...], (((0,), (0,)), ((), ())), preferred_element_type=F32
        )
        h0 = (h0 + b_in[...]).astype(BF)
        own_rows = jnp.logical_and(f >= 2, jnp.logical_and(r0 >= 2, r0 < 2 + rows))

        @pl.when(own_rows)
        def _():
            for k in range(2):
                h0_ref[f - 2, r0 - 2 + k] = h0[k * width : (k + 1) * width]

        n1 = silu(rms(h0.astype(F32), gain_one[...])).astype(BF).astype(F32)
        for k in range(2):
            here = jnp.where(valid(r0 + k, 2), n1[k * width : (k + 1) * width], 0.0)
            put(f, r0 + k, here)
        return 0

    lax.fori_loop(jnp.where(tm == 0, rows1, 0), 2 * rows1, normed, 0)

    @pl.when(tm == 0)
    def _():
        to = column_of(lax.broadcasted_iota(jnp.int32, (width, width), 0), width)
        at = lax.broadcasted_iota(jnp.int32, (width, width), 1)
        place = jnp.where(at == to, 1.0, 0.0).astype(BF)
        for f in range(2):
            for r in range(rows1):
                if r < 2:
                    row = cache_up[f, r]
                elif r < 2 + rows:
                    row = cache_one[f, r - 2]
                else:
                    row = cache_dn[f, r - 2 - rows]
                put(f, r, dot(place, row))

    for j in range(4):
        for copy in copies[j]:
            copy.wait()
        pair = dot(
            jnp.concatenate([rows_of(v, 1, j, rows2), rows_of(v, 2, j, rows2)], 1),
            jnp.concatenate([both(w_v, j, 1, 0), both(w_v, j, 2, 1)], 0),
        )
        acc[j, 0] = pair[:, :c] + dot(rows_of(v, 0, j, rows2), taps_of(w_v, j, 0))
        acc[j, 1] = pair[:, c:] + dot(rows_of(v, 3, j, rows2), taps_of(w_v, j, 2))

    def finish(i, _):
        t = i // rows2
        r = i % rows2
        m = [acc[j, t, pl.ds(pl.multiple_of(r * half, half), half)] for j in range(4)]
        even = m[0] + m[1] + m[2] + b_one[...]
        odd = m[1] - m[2] - m[3] + b_one[...]
        keep = valid(r, 1)
        for k, part in enumerate((even, odd)):
            n2 = silu(rms(part, gain_two[...]))
            n2_ref[t, r, k * half : (k + 1) * half] = jnp.where(keep, n2, 0.0).astype(BF)
        return 0

    lax.fori_loop(0, 2 * rows2, finish, 0)


def own_frames_body(n2, w_hbm, u_hbm, acc_ref, v, w_v, sems):
    rows2, width, c = n2.shape[1:]
    half = width // 2
    rows = rows2 - 2
    copies = weight_copies(w_hbm, u_hbm, w_v, sems, (1, 2))
    for row in copies:
        for copy in row:
            copy.start()

    def split(i, _):
        f = i // rows2
        r = i % rows2
        row = n2[f, r].astype(F32)
        parts = filtered(row[:half], row[half:])
        for j in range(4):
            v[f, j, r] = parts[j]
        return 0

    lax.fori_loop(0, 2 * rows2, split, 0)
    for j in range(4):
        for copy in copies[j]:
            copy.wait()
        pair = dot(rows_of(v, 0, j, rows), both(w_v, j, 2, 1))
        acc_ref[j, 0] = pair[:, :c]
        acc_ref[j, 1] = pair[:, c:] + dot(rows_of(v, 1, j, rows), taps_of(w_v, j, 2))


def earlier_frames_body(
    earlier, cache_two, cache_up, cache_dn, w_hbm, u_hbm, acc_in, h0, b_two,
    out_ref, v, w_v, acc, sems,
):
    tm = lax.axis_index("tm")
    rows2, width, c = earlier.shape[1:]
    half = width // 2
    rows = rows2 - 2
    copies = weight_copies(w_hbm, u_hbm, w_v, sems, (0, 1))
    for row in copies:
        for copy in row:
            copy.start()

    def put(f, r, row):
        parts = filtered(row[:half], row[half:])
        for j in range(4):
            v[f, j, r] = parts[j]

    @pl.when(tm > 0)
    def _():
        def split(i, _):
            f = i // rows2
            r = i % rows2
            put(f, r, earlier[f, r].astype(F32))
            return 0

        lax.fori_loop(0, 2 * rows2, split, 0)

    @pl.when(tm == 0)
    def _():
        to = column_of(lax.broadcasted_iota(jnp.int32, (width, width), 0), width)
        at = lax.broadcasted_iota(jnp.int32, (width, width), 1)
        place = jnp.where(at == to, 1.0, 0.0).astype(BF)
        for f in range(2):
            for r in range(rows2):
                if r < 1:
                    row = cache_up[f, 2]
                elif r < 1 + rows:
                    row = cache_two[f, r - 1]
                else:
                    row = cache_dn[f, 2]
                put(f, r, dot(place, row))

    for j in range(4):
        for copy in copies[j]:
            copy.wait()
        pair = dot(rows_of(v, 1, j, rows), both(w_v, j, 1, 0))
        acc[j, 0] = acc_in[j, 0] + pair[:, :c] + dot(rows_of(v, 0, j, rows), taps_of(w_v, j, 0))
        acc[j, 1] = acc_in[j, 1] + pair[:, c:]

    frm = lax.broadcasted_iota(jnp.int32, (width, width), 0)
    at = column_of(lax.broadcasted_iota(jnp.int32, (width, width), 1), width)
    back = jnp.where(at == frm, 1.0, 0.0).astype(BF)

    def finish(i, _):
        t = i // rows
        r = i % rows
        m = [acc[j, t, pl.ds(pl.multiple_of(r * half, half), half)] for j in range(4)]
        even = m[0] + m[1] + m[2] + b_two[...]
        odd = m[1] - m[2] - m[3] + b_two[...]
        both_cols = jnp.concatenate([even, odd], 0) + h0[t, r].astype(F32)
        out_ref[t, r] = dot(back, both_cols.astype(BF)).astype(BF)
        return 0

    lax.fori_loop(0, 2 * rows, finish, 0)


def in_vmem(count):
    return [pl.BlockSpec(memory_space=VMEM)] * count


IN_HBM = [pl.BlockSpec(memory_space=pl.ANY)]


def on_device(
    latent, cache_lat, cache_one, cache_two, w_in, b_in, gain_one, w_one, b_one, gain_two, w_two, b_two
):
    tiles = lax.axis_size("tile")
    frames, rows, width, chan = latent.shape
    c = w_in.shape[-1]
    half = width // 2
    params = pltpu.CompilerParams(vmem_limit_bytes=48 << 20)

    lat = jnp.concatenate([jnp.swapaxes(latent, 2, 3), jnp.swapaxes(cache_lat, 2, 3)], 0)
    from_up = shifted(lat[:, rows - 3 :], "tile", 1)
    from_dn = shifted(lat[:, :3], "tile", -1)
    caches = jnp.concatenate([cache_one[:, rows - 2 :], cache_two[:, rows - 1 :]], 1)
    cache_up = first_frames_only(caches, 1)
    caches = jnp.concatenate([cache_one[:, :2], cache_two[:, :1]], 1)
    cache_dn = first_frames_only(caches, -1)
    u_one = summed_kernels(w_one)
    lat = jnp.concatenate([from_up, lat, from_dn], 1)
    own = lat[:frames].reshape(-1, width)
    prev1 = shifted(own, "tm", 1)
    prev2 = shifted(own, "tm", 2)
    u_two = summed_kernels(w_two)
    w1 = w_one.reshape(9, 3, c, c)
    w2 = w_two.reshape(9, 3, c, c)

    def row(x):
        return x.reshape(1, c)

    n2, h0 = pl.pallas_call(
        functools.partial(first_conv_body, tiles),
        out_shape=[
            jax.ShapeDtypeStruct((2, rows + 2, width, c), BF),
            jax.ShapeDtypeStruct((2, rows, width, c), BF),
        ],
        in_specs=in_vmem(10) + IN_HBM * 2 + in_vmem(2),
        out_specs=in_vmem(2),
        scratch_shapes=[
            VMEM((3, 6 * (rows + 6) * chan, width), BF),
            VMEM((4, 4, rows + 4, half, c), BF),
            VMEM((4, 9, c, c), BF),
            VMEM((4, 2, (rows + 2) * half, c), F32),
            pltpu.SemaphoreType.DMA((4, 3)),
        ],
        compiler_params=params,
        name="first_conv",
        cost_estimate=pl.CostEstimate(flops=14_000_000_000, bytes_accessed=14_000_000, transcendentals=0),
    )(
        own, prev1, prev2, lat[frames:].reshape(-1, width), cache_one, cache_up, cache_dn,
        w_in.reshape(-1, c), row(b_in), row(gain_one), w1, u_one, row(b_one), row(gain_two),
    )
    earlier = shifted(n2, "tm", 1)
    acc = pl.pallas_call(
        own_frames_body,
        out_shape=jax.ShapeDtypeStruct((4, 2, rows * half, c), F32),
        in_specs=in_vmem(1) + IN_HBM * 2,
        out_specs=pl.BlockSpec(memory_space=VMEM),
        scratch_shapes=[
            VMEM((2, 4, rows + 2, half, c), BF),
            VMEM((4, 9, c, c), BF),
            pltpu.SemaphoreType.DMA((4, 3)),
        ],
        compiler_params=params,
        name="own_frames",
        cost_estimate=pl.CostEstimate(flops=4_000_000_000, bytes_accessed=14_000_000, transcendentals=0),
    )(n2, w2, u_two)
    return pl.pallas_call(
        earlier_frames_body,
        out_shape=jax.ShapeDtypeStruct((2, rows, width, c), BF),
        in_specs=in_vmem(4) + IN_HBM * 2 + in_vmem(3),
        out_specs=pl.BlockSpec(memory_space=VMEM),
        scratch_shapes=[
            VMEM((2, 4, rows + 2, half, c), BF),
            VMEM((4, 9, c, c), BF),
            VMEM((4, 2, rows * half, c), F32),
            pltpu.SemaphoreType.DMA((4, 3)),
        ],
        compiler_params=params,
        name="earlier_frames",
        cost_estimate=pl.CostEstimate(flops=4_000_000_000, bytes_accessed=14_000_000, transcendentals=0),
    )(earlier, cache_two, cache_up, cache_dn, w2, u_two, acc, h0, row(b_two))


def solution(mesh):
    return jax.shard_map(
        on_device,
        mesh=mesh,
        in_specs=(
            P("tm", "tile", None, None),
            P(None, "tile", None, None),
            P(None, "tile", None, None),
            P(None, "tile", None, None),
            P(),
            P(),
            P(),
            P(),
            P(),
            P(),
            P(),
            P(),
        ),
        out_specs=P("tm", "tile", None, None),
        check_vma=False,
    )
```

time: 132 us -> 88.5 us (0.67)
  the two profiles are of different devices: /device:TPU:2 before, /device:TPU:0 now
where the time goes in v1:
time: 88.5 us; the launch traced here: 87.6 us
  Pallas kernels  53.1 us (60%)
  starting transfers between devices  19.7 us (22%)
  local copies, waits for them, and re-layouts  7.93 us (9%)
  waiting for transfers between devices  3.9 us (4%)
  other arithmetic  2.59 us (3%)
    pallas_call x1, Pallas kernels, on_device(): pl.pallas_call(functools.partial(first_conv_body, tiles), out_shape=[jax....  18.5 us
    pallas_call x2, Pallas kernels, summed_kernels(): pl.pallas_call(kernel_sums, grid=(9,), in_specs=[pl.BlockSpec((1, 3, c, o...  18.3 us
    ppermute x5, starting transfers between devices, shifted(): lax.ppermute(x, axis, [(i, i + by) for i in range(count) if 0 <= i + by <...  13.4 us
    pallas_call x1, Pallas kernels, on_device(): pl.pallas_call(earlier_frames_body, out_shape=jax.ShapeDtypeStruct((2, ro...  10.5 us
    ppermute x2, starting transfers between devices, first_frames_only(): lax.ppermute(x, ('tm', 'tile'), [(i, i + by) for i in range(rows) if 0 <=...  6.24 us
    pallas_call x1, Pallas kernels, on_device(): pl.pallas_call(own_frames_body, out_shape=jax.ShapeDtypeStruct((4, 2, row...  5.75 us
    unnamed x30, local copies, waits for them, and re-layouts  5.58 us
    ppermute x5, waiting for transfers between devices, shifted(): lax.ppermute(x, axis, [(i, i + by) for i in range(count) if 0 <= i + by <...  3.9 us
  transfers between devices with their start and end apart: 7, of which 1 were waited for; matrix products, arithmetic and copies ran while one was open for 3% of the time, Pallas kernels for 28%

profile of v1, /device:TPU:0, one launch (start us, length us, event | category | flops | bytes accessed | tf_op | source)
XLA Modules:
  0.0 87.6 jit_solution(11637213264656414323)
XLA Ops:
  0.0 1.1 %fusion.2 = (bf16[2,1,128,384]{3,2,1,0:T(8,128)(2,1)S(1)}, bf16[2,1,128,384]{3,2,1,0:T(8,128)(2,1)S(1)}) fusion(bf16[2,4,128,384]{3,2,1,0:T(8,128)(2,1)} %cache_two.1), kind=kLoop, calls=%fused_computation.8 | loop fusion | bytes 786432 | tf_op jit(solution)/shard_map/slice | solution.py:341
  1.1 1.2 %fusion.1 = (bf16[2,2,128,384]{3,2,1,0:T(8,128)(2,1)S(1)}, bf16[2,2,128,384]{3,2,1,0:T(8,128)(2,1)S(1)}) fusion(bf16[2,4,128,384]{3,2,1,0:T(8,128)(2,1)} %cache_one.1), kind=kLoop, calls=%fused_computation.7 | loop fusion | bytes 1572864 | tf_op jit(solution)/shard_map/slice | solution.py:341
  2.3 0.1 pad_maximum_fusion
  2.4 5.0 %collective-permute-start.4 = (bf16[2,3,128,384]{3,2,1,0:T(8,128)(2,1)S(1)}, bf16[2,3,128,384]{3,2,1,0:T(8,128)(2,1)S(1)}, u32[]{:S(2)}, u32[]{:S(2)}) collective-permute-start(bf16[2,3,128,384]{3,2,1,0:T(8,128)(2,1)S(1)} %pad_maximum_fusion), channel_id=1, source_target_pairs={{0,1},{1,2},{2,3}} | collective-permute-start | bytes 1769480 | tf_op jit(solution)/shard_map/ppermute | solution.py:22
  7.4 0.9 %pad_maximum_fusion.1 = bf16[2,3,128,384]{3,2,1,0:T(8,128)(2,1)} fusion(bf16[2,1,128,384]{3,2,1,0:T(8,128)(2,1)S(1)} %get-tuple-element.11, bf16[2,2,128,384]{3,2,1,0:T(8,128)(2,1)S(1)} %get-tuple-element.9), kind=kLoop, calls=%fused_computation.1 | loop fusion | flops 294912 | bytes 1179648 | tf_op jit(solution)/shard_map/concatenate | solution.py:341
  8.3 1.3 %collective-permute-start.5 = (bf16[2,3,128,384]{3,2,1,0:T(8,128)(2,1)}, bf16[2,3,128,384]{3,2,1,0:T(8,128)(2,1)S(1)}, u32[]{:S(2)}, u32[]{:S(2)}) collective-permute-start(bf16[2,3,128,384]{3,2,1,0:T(8,128)(2,1)} %pad_maximum_fusion.1), channel_id=1, source_target_pairs={{1,0},{2,1},{3,2}} | collective-permute-start | bytes 1769480 | tf_op jit(solution)/shard_map/ppermute | solution.py:22
  9.6 0.8 fusion
  10.4 1.3 %collective-permute-start.1 = (bf16[4,3,16,128]{3,2,1,0:T(8,128)(2,1)S(1)}, bf16[4,3,16,128]{3,2,1,0:T(8,128)(2,1)S(1)}, u32[]{:S(2)}, u32[]{:S(2)}) collective-permute-start(bf16[4,3,16,128]{3,2,1,0:T(8,128)(2,1)S(1)} %get-tuple-element.16), channel_id=1, source_target_pairs={{1,0},{2,1},{3,2},{5,4},{6,5},{7,6},{9,8},{10,9},{11,10},{13,12},{... | collective-permute-start | bytes 147464 | tf_op jit(solution)/shard_map/ppermute | solution.py:17
  11.7 5.2 %collective-permute-start = (bf16[4,3,16,128]{3,2,1,0:T(8,128)(2,1)S(1)}, bf16[4,3,16,128]{3,2,1,0:T(8,128)(2,1)S(1)}, u32[]{:S(2)}, u32[]{:S(2)}) collective-permute-start(bf16[4,3,16,128]{3,2,1,0:T(8,128)(2,1)S(1)} %get-tuple-element.15), channel_id=1, source_target_pairs={{0,1},{1,2},{2,3},{4,5},{5,6},{6,7},{8,9},{9,10},{10,11},{12,13},{... | collective-permute-start | bytes 147464 | tf_op jit(solution)/shard_map/ppermute | solution.py:17
  16.9 3.9 %collective-permute-done.1 = bf16[4,3,16,128]{3,2,1,0:T(8,128)(2,1)S(1)} collective-permute-done((bf16[4,3,16,128]{3,2,1,0:T(8,128)(2,1)S(1)}, bf16[4,3,16,128]{3,2,1,0:T(8,128)(2,1)S(1)}, u32[]{:S(2)}, u32[]{:S(2)}) %collective-permute-start.1) | collective-permute-done | bytes 49184 | tf_op jit(solution)/shard_map/ppermute | solution.py:17
  20.8 0.0 collective-permute-done
  20.8 0.8 pad_maximum_fusion.2
  21.6 1.3 %collective-permute-start.2 = (bf16[320,128]{1,0:T(8,128)(2,1)S(1)}, bf16[320,128]{1,0:T(8,128)(2,1)S(1)}, u32[]{:S(2)}, u32[]{:S(2)}) collective-permute-start(bf16[320,128]{1,0:T(8,128)(2,1)S(1)} %bitcast.8), channel_id=1, source_target_pairs={{0,4},{4,8},{8,12},{12,16},{16,20},{20,24},{24,28},{1,5},{5,9},{9,... | collective-permute-start | bytes 245768 | tf_op jit(solution)/shard_map/ppermute | solution.py:17
  22.9 1.3 %collective-permute-start.3 = (bf16[320,128]{1,0:T(8,128)(2,1)S(1)}, bf16[320,128]{1,0:T(8,128)(2,1)S(1)}, u32[]{:S(2)}, u32[]{:S(2)}) collective-permute-start(bf16[320,128]{1,0:T(8,128)(2,1)S(1)} %bitcast.9), channel_id=1, source_target_pairs={{0,8},{4,12},{8,16},{12,20},{16,24},{20,28},{1,9},{5,13},{9,17},{1... | collective-permute-start | bytes 245768 | tf_op jit(solution)/shard_map/ppermute | solution.py:17
  24.3 0.0 copy-start.2
  24.3 0.0 copy-start.9
  24.3 9.2 %kernel_sums.2.u_hbm = bf16[2,9,384,384]{3,2,1,0:T(8,128)(2,1)} custom-call(bf16[9,3,384,384]{3,2,1,0:T(8,128)(2,1)} %bitcast.15), custom_call_target="tpu_custom_call" | custom-call | flops 7962624 | bytes 13271040 | tf_op jit(solution)/shard_map/kernel_sums/pallas_call | solution.py:65
  33.5 0.0 collective-permute-done.2.prev1
  33.5 0.0 collective-permute-done.3.prev2
  33.5 0.0 collective-permute-done.4.cache_up
  33.5 0.0 copy-start.3
  33.5 0.8 copy-done.3
  34.4 0.0 collective-permute-done.5.cache_dn
  34.4 0.9 %copy-done.6 = bf16[2,3,128,384]{3,2,1,0:T(8,128)(2,1)} copy-done((bf16[2,3,128,384]{3,2,1,0:T(8,128)(2,1)}, bf16[2,3,128,384]{3,2,1,0:T(8,128)(2,1)S(1)}, u32[]{:S(2)}) %copy-start.6) | copy-done | bytes 589848
  35.3 1.1 %copy-done.4 = bf16[2,3,128,384]{3,2,1,0:T(8,128)(2,1)S(1)} copy-done((bf16[2,3,128,384]{3,2,1,0:T(8,128)(2,1)S(1)}, bf16[2,3,128,384]{3,2,1,0:T(8,128)(2,1)}, u32[]{:S(2)}) %copy-start.4) | copy-done | bytes 589848
  36.3 1.1 %copy-done.7 = bf16[2,3,128,384]{3,2,1,0:T(8,128)(2,1)S(1)} copy-done((bf16[2,3,128,384]{3,2,1,0:T(8,128)(2,1)S(1)}, bf16[2,3,128,384]{3,2,1,0:T(8,128)(2,1)}, u32[]{:S(2)}) %copy-start.7) | copy-done | bytes 589848
  37.4 18.5 %first_conv.1 = (bf16[2,6,128,384]{3,2,1,0:T(8,128)(2,1)S(1)}, bf16[2,4,128,384]{3,2,1,0:T(8,128)(2,1)S(1)}) custom-call(bf16[320,128]{1,0:T(8,128)(2,1)S(1)} %bitcast.10, bf16[320,128]{1,0:T(8,128)(2,1)S(1)} %collective-permute-done.2.prev1, bf16[320,128]{1,0:T(8,128)(2,1)S(1)} %collective-permute-done.3.prev2, bf16[320,128]{1,0:T(8,128)(2,1)S(1)} %bitcast.7, ...), custom_call_target="tpu_custom_call" | custom-call | flops 14000000000 | bytes 14000000 | tf_op jit(solution)/shard_map/first_conv/pallas_call | solution.py:355
  55.9 4.4 %collective-permute-start.6 = (bf16[2,6,128,384]{3,2,1,0:T(8,128)(2,1)S(1)}, bf16[2,6,128,384]{3,2,1,0:T(8,128)(2,1)S(1)}, u32[]{:S(2)}, u32[]{:S(2)}) collective-permute-start(bf16[2,6,128,384]{3,2,1,0:T(8,128)(2,1)S(1)} %get-tuple-element.7.n2), channel_id=1, source_target_pairs={{0,4},{4,8},{8,12},{12,16},{16,20},{20,24},{24,28},{1,5},{5,9},{9,... | collective-permute-start | bytes 3538952 | tf_op jit(solution)/shard_map/ppermute | solution.py:17
  60.3 9.1 %kernel_sums.3.u_hbm = bf16[2,9,384,384]{3,2,1,0:T(8,128)(2,1)} custom-call(bf16[9,3,384,384]{3,2,1,0:T(8,128)(2,1)} %bitcast.12), custom_call_target="tpu_custom_call" | custom-call | flops 7962624 | bytes 13271040 | tf_op jit(solution)/shard_map/kernel_sums/pallas_call | solution.py:65
  69.4 5.8 %own_frames.1.acc_in = f32[4,2,256,384]{3,2,1,0:T(8,128)S(1)} custom-call(bf16[2,6,128,384]{3,2,1,0:T(8,128)(2,1)S(1)} %get-tuple-element.7.n2, bf16[9,3,384,384]{3,2,1,0:T(8,128)(2,1)} %bitcast.13, bf16[2,9,384,384]{3,2,1,0:T(8,128)(2,1)} %kernel_sums.3.u_hbm), custom_call_target="tpu_custom_call" | custom-call | flops 4000000000 | bytes 14000000 | tf_op jit(solution)/shard_map/own_frames/pallas_call | solution.py:378
  75.2 1.7 %copy-done = f32[4,2,256,384]{3,2,1,0:T(8,128)} copy-done((f32[4,2,256,384]{3,2,1,0:T(8,128)}, f32[4,2,256,384]{3,2,1,0:T(8,128)S(1)}, u32[]{:S(2)}) %copy-start) | copy-done | bytes 3145752
  76.9 10.5 %earlier_frames.1 = bf16[2,4,128,384]{3,2,1,0:T(8,128)(2,1)} custom-call(bf16[2,6,128,384]{3,2,1,0:T(8,128)(2,1)S(1)} %collective-permute-done.6.earlier, bf16[2,4,128,384]{3,2,1,0:T(8,128)(2,1)S(1)} %copy-done.1, bf16[2,3,128,384]{3,2,1,0:T(8,128)(2,1)S(1)} %copy-done.5, bf16[2,3,128,384]{3,2,1,0:T(8,128)(2,1)S(1)} %copy-done.8, ...), custom_call_target="tpu_custom_call" | custom-call | flops 4000000000 | bytes 14000000 | tf_op jit(solution)/shard_map/earlier_frames/pallas_call | solution.py:392
  (29 shorter events, 0.1 us)
Async XLA Ops:
  0.0 24.2 %copy-start.10 = (f32[384]{0:T(512)S(1)}, f32[384]{0:T(512)}, u32[]{:S(2)}) copy-start(f32[384]{0:T(512)} %param.17) | copy-start | bytes 4612
  0.0 24.2 %copy-start.11 = (f32[384]{0:T(512)S(1)}, f32[384]{0:T(512)}, u32[]{:S(2)}) copy-start(f32[384]{0:T(512)} %param.18) | copy-start | bytes 4612
  0.0 24.2 %copy-start.12 = (f32[384]{0:T(512)S(1)}, f32[384]{0:T(512)}, u32[]{:S(2)}) copy-start(f32[384]{0:T(512)} %param.20) | copy-start | bytes 4612
  0.0 24.3 %copy-start.13 = (f32[384]{0:T(512)S(1)}, f32[384]{0:T(512)}, u32[]{:S(2)}) copy-start(f32[384]{0:T(512)} %param.21) | copy-start | bytes 4612
  2.4 31.1 %collective-permute-start.4 = (bf16[2,3,128,384]{3,2,1,0:T(8,128)(2,1)S(1)}, bf16[2,3,128,384]{3,2,1,0:T(8,128)(2,1)S(1)}, u32[]{:S(2)}, u32[]{:S(2)}) collective-permute-start(bf16[2,3,128,384]{3,2,1,0:T(8,128)(2,1)S(1)} %pad_maximum_fusion), channel_id=1, source_target_pairs={{0,1},{1,2},{2,3}} | collective-permute-start | bytes 1769480 | tf_op jit(solution)/shard_map/ppermute | solution.py:22
  8.3 26.1 %collective-permute-start.5 = (bf16[2,3,128,384]{3,2,1,0:T(8,128)(2,1)}, bf16[2,3,128,384]{3,2,1,0:T(8,128)(2,1)S(1)}, u32[]{:S(2)}, u32[]{:S(2)}) collective-permute-start(bf16[2,3,128,384]{3,2,1,0:T(8,128)(2,1)} %pad_maximum_fusion.1), channel_id=1, source_target_pairs={{1,0},{2,1},{3,2}} | collective-permute-start | bytes 1769480 | tf_op jit(solution)/shard_map/ppermute | solution.py:22
  10.4 10.4 %collective-permute-start.1 = (bf16[4,3,16,128]{3,2,1,0:T(8,128)(2,1)S(1)}, bf16[4,3,16,128]{3,2,1,0:T(8,128)(2,1)S(1)}, u32[]{:S(2)}, u32[]{:S(2)}) collective-permute-start(bf16[4,3,16,128]{3,2,1,0:T(8,128)(2,1)S(1)} %get-tuple-element.16), channel_id=1, source_target_pairs={{1,0},{2,1},{3,2},{5,4},{6,5},{7,6},{9,8},{10,9},{11,10},{13,12},{... | collective-permute-start | bytes 147464 | tf_op jit(solution)/shard_map/ppermute | solution.py:17
  11.7 9.1 %collective-permute-start = (bf16[4,3,16,128]{3,2,1,0:T(8,128)(2,1)S(1)}, bf16[4,3,16,128]{3,2,1,0:T(8,128)(2,1)S(1)}, u32[]{:S(2)}, u32[]{:S(2)}) collective-permute-start(bf16[4,3,16,128]{3,2,1,0:T(8,128)(2,1)S(1)} %get-tuple-element.15), channel_id=1, source_target_pairs={{0,1},{1,2},{2,3},{4,5},{5,6},{6,7},{8,9},{9,10},{10,11},{12,13},{... | collective-permute-start | bytes 147464 | tf_op jit(solution)/shard_map/ppermute | solution.py:17
  21.6 11.9 %collective-permute-start.2 = (bf16[320,128]{1,0:T(8,128)(2,1)S(1)}, bf16[320,128]{1,0:T(8,128)(2,1)S(1)}, u32[]{:S(2)}, u32[]{:S(2)}) collective-permute-start(bf16[320,128]{1,0:T(8,128)(2,1)S(1)} %bitcast.8), channel_id=1, source_target_pairs={{0,4},{4,8},{8,12},{12,16},{16,20},{20,24},{24,28},{1,5},{5,9},{9,... | collective-permute-start | bytes 245768 | tf_op jit(solution)/shard_map/ppermute | solution.py:17
  22.9 10.6 %collective-permute-start.3 = (bf16[320,128]{1,0:T(8,128)(2,1)S(1)}, bf16[320,128]{1,0:T(8,128)(2,1)S(1)}, u32[]{:S(2)}, u32[]{:S(2)}) collective-permute-start(bf16[320,128]{1,0:T(8,128)(2,1)S(1)} %bitcast.9), channel_id=1, source_target_pairs={{0,8},{4,12},{8,16},{12,20},{16,24},{20,28},{1,9},{5,13},{9,17},{1... | collective-permute-start | bytes 245768 | tf_op jit(solution)/shard_map/ppermute | solution.py:17
  24.3 11.0 %copy-start.2 = (bf16[2,4,128,384]{3,2,1,0:T(8,128)(2,1)S(1)}, bf16[2,4,128,384]{3,2,1,0:T(8,128)(2,1)}, u32[]{:S(2)}) copy-start(bf16[2,4,128,384]{3,2,1,0:T(8,128)(2,1)} %cache_one.1) | copy-start | bytes 2359300
  24.3 11.0 %copy-start.9 = (bf16[3,3,3,16,384]{4,3,2,1,0:T(8,128)(2,1)S(1)}, bf16[3,3,3,16,384]{4,3,2,1,0:T(8,128)(2,1)}, u32[]{:S(2)}) copy-start(bf16[3,3,3,16,384]{4,3,2,1,0:T(8,128)(2,1)} %param.16) | copy-start | bytes 995332
  33.5 0.8 copy-start.3
  34.4 0.9 %copy-start.6 = (bf16[2,3,128,384]{3,2,1,0:T(8,128)(2,1)}, bf16[2,3,128,384]{3,2,1,0:T(8,128)(2,1)S(1)}, u32[]{:S(2)}) copy-start(bf16[2,3,128,384]{3,2,1,0:T(8,128)(2,1)S(1)} %collective-permute-done.5.cache_dn) | copy-start | bytes 1769476
  35.3 1.1 %copy-start.4 = (bf16[2,3,128,384]{3,2,1,0:T(8,128)(2,1)S(1)}, bf16[2,3,128,384]{3,2,1,0:T(8,128)(2,1)}, u32[]{:S(2)}) copy-start(bf16[2,3,128,384]{3,2,1,0:T(8,128)(2,1)} %copy-done.3) | copy-start | bytes 1769476
  36.3 1.1 %copy-start.7 = (bf16[2,3,128,384]{3,2,1,0:T(8,128)(2,1)S(1)}, bf16[2,3,128,384]{3,2,1,0:T(8,128)(2,1)}, u32[]{:S(2)}) copy-start(bf16[2,3,128,384]{3,2,1,0:T(8,128)(2,1)} %copy-done.6) | copy-start | bytes 1769476
  37.4 22.9 %copy-start.14 = (f32[384]{0:T(512)S(1)}, f32[384]{0:T(512)}, u32[]{:S(2)}) copy-start(f32[384]{0:T(512)} %param.23) | copy-start | bytes 4612
  55.9 21.0 %collective-permute-start.6 = (bf16[2,6,128,384]{3,2,1,0:T(8,128)(2,1)S(1)}, bf16[2,6,128,384]{3,2,1,0:T(8,128)(2,1)S(1)}, u32[]{:S(2)}, u32[]{:S(2)}) collective-permute-start(bf16[2,6,128,384]{3,2,1,0:T(8,128)(2,1)S(1)} %get-tuple-element.7.n2), channel_id=1, source_target_pairs={{0,4},{4,8},{8,12},{12,16},{16,20},{20,24},{24,28},{1,5},{5,9},{9,... | collective-permute-start | bytes 3538952 | tf_op jit(solution)/shard_map/ppermute | solution.py:17
  69.4 7.5 %copy-start.1 = (bf16[2,4,128,384]{3,2,1,0:T(8,128)(2,1)S(1)}, bf16[2,4,128,384]{3,2,1,0:T(8,128)(2,1)}, u32[]{:S(2)}) copy-start(bf16[2,4,128,384]{3,2,1,0:T(8,128)(2,1)} %cache_two.1) | copy-start | bytes 2359300
  69.4 7.5 %copy-start.5 = (bf16[2,3,128,384]{3,2,1,0:T(8,128)(2,1)S(1)}, bf16[2,3,128,384]{3,2,1,0:T(8,128)(2,1)}, u32[]{:S(2)}) copy-start(bf16[2,3,128,384]{3,2,1,0:T(8,128)(2,1)} %copy-done.3) | copy-start | bytes 1769476
  69.4 7.5 %copy-start.8 = (bf16[2,3,128,384]{3,2,1,0:T(8,128)(2,1)S(1)}, bf16[2,3,128,384]{3,2,1,0:T(8,128)(2,1)}, u32[]{:S(2)}) copy-start(bf16[2,3,128,384]{3,2,1,0:T(8,128)(2,1)} %copy-done.6) | copy-start | bytes 1769476
  75.2 1.7 %copy-start = (f32[4,2,256,384]{3,2,1,0:T(8,128)}, f32[4,2,256,384]{3,2,1,0:T(8,128)S(1)}, u32[]{:S(2)}) copy-start(f32[4,2,256,384]{3,2,1,0:T(8,128)S(1)} %own_frames.1.acc_in) | copy-start | bytes 9437188

commit v2 on v1

v2 whole, which is shorter than its diff:
```python
import functools

import jax
import jax.numpy as jnp
from jax import lax
from jax.experimental import pallas as pl
from jax.experimental.pallas import tpu as pltpu
from jax.sharding import PartitionSpec as P

BF = jnp.bfloat16
F32 = jnp.float32
VMEM = pltpu.VMEM


def shifted(x, axis, by):
    count = lax.axis_size(axis)
    return lax.ppermute(x, axis, [(i, i + by) for i in range(count) if 0 <= i + by < count])


def first_frames_only(x, by):
    rows = lax.axis_size("tile")
    return lax.ppermute(
        x, ("tm", "tile"), [(i, i + by) for i in range(rows) if 0 <= i + by < rows]
    )


def column_of(place, width):
    half = width // 2
    return jnp.where(place < half, 2 * place, 2 * (place - half) + 1)


def silu(v):
    return 0.5 * v * (1.0 + jnp.tanh(0.5 * v))


def rms(v, gain):
    return v * lax.rsqrt(jnp.mean(v * v, -1, keepdims=True) + 1e-6) * gain


def filtered(even, odd):
    half = even.shape[0]
    place = lax.broadcasted_iota(jnp.int32, even.shape, 0)
    odd_before = jnp.where(place == 0, 0.0, pltpu.roll(odd, 1, 0))
    even_after = jnp.where(place == half - 1, 0.0, pltpu.roll(even, half - 1, 0))
    return (
        (odd_before - odd).astype(BF),
        (even + odd).astype(BF),
        (odd - even).astype(BF),
        (even - even_after).astype(BF),
    )


def summed_kernels_body(w, u):
    def tap(i, _):
        g0 = w[i, 0].astype(F32)
        g1 = w[i, 1].astype(F32)
        g2 = w[i, 2].astype(F32)
        s = 0.5 * (g0 + g2)
        h = 0.5 * g1
        u[0, i] = (s + h).astype(BF)
        u[1, i] = (s - h).astype(BF)
        return 0

    lax.fori_loop(0, w.shape[0], tap, 0)


def summed_kernels(w):
    taps, _, c, o = w.shape
    return pl.pallas_call(
        summed_kernels_body,
        in_specs=in_vmem(1),
        out_specs=in_vmem(1)[0],
        out_shape=jax.ShapeDtypeStruct((2, taps, c, o), BF),
        compiler_params=limit(16),
        name="summed_kernels",
        cost_estimate=pl.CostEstimate(flops=6 * taps * c * o, bytes_accessed=10 * taps * c * o, transcendentals=0),
    )(w)


def taps_of(w, u, j, dt):
    if j == 0 or j == 3:
        parts = [w[3 * dt + dy, 0 if j == 0 else 2] for dy in range(3)]
    else:
        parts = [u[j - 1, 3 * dt + dy] for dy in range(3)]
    return jnp.concatenate(parts, 0)


def both(w, u, j, dt_a, dt_b):
    return jnp.concatenate([taps_of(w, u, j, dt_a), taps_of(w, u, j, dt_b)], 1)


def rows_of(v, f, j, rows):
    half, c = v.shape[-2:]
    return jnp.concatenate(
        [v[f, j, dy : dy + rows].reshape(rows * half, c) for dy in range(3)], 1
    )


def dot(a, b):
    return jnp.dot(a, b, preferred_element_type=F32)


def in_vmem(count):
    return [pl.BlockSpec(memory_space=VMEM)] * count


def limit(mib):
    return pltpu.CompilerParams(vmem_limit_bytes=mib << 20)


def places(width, dx, transposed):
    shape = (width, width)
    to = column_of(lax.broadcasted_iota(jnp.int32, shape, 0 if transposed else 1), width)
    at = lax.broadcasted_iota(jnp.int32, shape, 1 if transposed else 0)
    return jnp.where(at == to + (dx - 1), 1.0, 0.0).astype(BF)


def put(v, f, r, row):
    half = row.shape[0] // 2
    parts = filtered(row[:half], row[half:])
    for j in range(4):
        v[f, j, r] = parts[j]


def first_conv_body(
    tiles,
    own, prev1, prev2, up, dn, cache_one, cache_up, cache_dn,
    w_in, b_in, gain_one, w, u, b_one, gain_two,
    n2_ref, h0_ref,
    lats, g, w_big, hs, v, acc,
):
    tm = lax.axis_index("tm")
    tile = lax.axis_index("tile")
    width = own.shape[-1]
    half = width // 2
    c = w_in.shape[1]
    chan = w_in.shape[0] // 27
    rows = own.shape[0] // (2 * chan)
    lat_rows = rows + 6
    rows1 = rows + 4
    rows2 = rows + 2
    slot = 4 * chan

    lats[...] = jnp.zeros_like(lats)
    place = jnp.concatenate([places(width, dx, False) for dx in range(3)], 1)

    def lay(block, f0, r0, count):
        moved = dot(block, place).astype(BF)
        for i in range(block.shape[0] // chan):
            f, r = f0 + i // count, r0 + i % count
            for dx in range(3):
                lats[f, r * slot + dx * chan : r * slot + (dx + 1) * chan] = moved[
                    i * chan : (i + 1) * chan, dx * width : (dx + 1) * width
                ]

    lay(up[...], 0, 0, 3)
    lay(prev2[...], 0, 3, rows)
    lay(prev1[...], 2, 3, rows)
    lay(own[...], 4, 3, rows)
    lay(dn[...], 0, 3 + rows, 3)
    eye = jnp.where(
        lax.broadcasted_iota(jnp.int32, (width, width), 0)
        == lax.broadcasted_iota(jnp.int32, (width, width), 1),
        1.0,
        0.0,
    ).astype(BF)
    for f in range(6):
        g[f * width : (f + 1) * width] = lax.dot_general(
            eye, lats[f], (((1,), (1,)), ((), ())), preferred_element_type=F32
        ).astype(BF)

    w_big[...] = jnp.zeros_like(w_big)
    for dt in range(3):
        for dy in range(3):
            taps = w_in[(3 * dt + dy) * 3 * chan : (3 * dt + dy + 1) * 3 * chan]
            for k in range(2):
                start = (4 * dt + dy + k) * slot
                w_big[start : start + 3 * chan, k * c : (k + 1) * c] = taps
    bias = jnp.concatenate([b_in[...], b_in[...]], 1)
    for p in range(rows1 // 2):
        patches = jnp.concatenate(
            [
                g[dt * width : (dt + 4) * width, 2 * p * slot : (2 * p + 4) * slot]
                for dt in range(3)
            ],
            1,
        )
        hs[p] = (dot(patches, w_big[...]) + bias).astype(BF)

    def valid(r, margin):
        at_row = tile * rows + r - margin
        return jnp.logical_and(at_row >= 0, at_row < tiles * rows)

    def normed(i, _):
        p = i // 4
        f = i % 4

        @pl.when(jnp.logical_or(f >= 2, tm > 0))
        def _():
            for k in range(2):
                r = 2 * p + k
                h0 = hs[p, pl.ds(pl.multiple_of(f * width, width), width), k * c : (k + 1) * c].astype(F32)
                gain = jnp.where(valid(r, 2), gain_one[...], 0.0)
                n1 = silu(rms(h0, gain)).astype(BF).astype(F32)
                put(v, f, r, n1)

        return 0

    lax.fori_loop(0, 2 * rows1, normed, 0)
    for f in range(2):
        for r in range(rows):
            p, k = (r + 2) // 2, (r + 2) % 2
            h0_ref[f, r] = hs[p, (f + 2) * width : (f + 3) * width, k * c : (k + 1) * c]

    @pl.when(tm == 0)
    def _():
        place = places(width, 1, True)
        for f in range(2):
            for r in range(rows1):
                if r < 2:
                    row = cache_up[f, r]
                elif r < 2 + rows:
                    row = cache_one[f, r - 2]
                else:
                    row = cache_dn[f, r - 2 - rows]
                put(v, f, r, dot(place, row))

    for j in range(4):
        pair = dot(
            jnp.concatenate([rows_of(v, 1, j, rows2), rows_of(v, 2, j, rows2)], 1),
            jnp.concatenate([both(w, u, j, 1, 0), both(w, u, j, 2, 1)], 0),
        )
        acc[j, 0] = pair[:, :c] + dot(rows_of(v, 0, j, rows2), taps_of(w, u, j, 0))
        acc[j, 1] = pair[:, c:] + dot(rows_of(v, 3, j, rows2), taps_of(w, u, j, 2))

    def finish(i, _):
        t = i // rows2
        r = i % rows2
        m = [acc[j, t, pl.ds(pl.multiple_of(r * half, half), half)] for j in range(4)]
        even = m[0] + m[1] + m[2] + b_one[...]
        odd = m[1] - m[2] - m[3] + b_one[...]
        gain = jnp.where(valid(r, 1), gain_two[...], 0.0)
        n2_ref[t, r, 0:half] = silu(rms(even, gain)).astype(BF)
        n2_ref[t, r, half:width] = silu(rms(odd, gain)).astype(BF)
        return 0

    lax.fori_loop(0, 2 * rows2, finish, 0)


def own_frames_body(n2, w, u, h0, b_two, part_ref, v, acc):
    rows2, width, c = n2.shape[1:]
    half = width // 2
    rows = rows2 - 2

    def split(i, _):
        f = i // rows2
        r = i % rows2
        put(v, f, r, n2[f, r].astype(F32))
        return 0

    lax.fori_loop(0, 2 * rows2, split, 0)
    for j in range(4):
        pair = dot(rows_of(v, 0, j, rows), both(w, u, j, 2, 1))
        acc[j, 0] = pair[:, :c]
        acc[j, 1] = pair[:, c:] + dot(rows_of(v, 1, j, rows), taps_of(w, u, j, 2))

    def finish(i, _):
        t = i // rows
        r = i % rows
        m = [acc[j, t, pl.ds(pl.multiple_of(r * half, half), half)] for j in range(4)]
        even = m[0] + m[1] + m[2] + b_two[...]
        odd = m[1] - m[2] - m[3] + b_two[...]
        part_ref[t, r, 0:half] = even + h0[t, r, 0:half].astype(F32)
        part_ref[t, r, half:width] = odd + h0[t, r, half:width].astype(F32)
        return 0

    lax.fori_loop(0, 2 * rows, finish, 0)


def earlier_frames_body(
    earlier, cache_two, cache_up, cache_dn, w, u, part, out_ref, v, acc
):
    tm = lax.axis_index("tm")
    rows2, width, c = earlier.shape[1:]
    half = width // 2
    rows = rows2 - 2

    @pl.when(tm > 0)
    def _():
        def split(i, _):
            f = i // rows2
            r = i % rows2
            put(v, f, r, earlier[f, r].astype(F32))
            return 0

        lax.fori_loop(0, 2 * rows2, split, 0)

    @pl.when(tm == 0)
    def _():
        place = places(width, 1, True)
        for f in range(2):
            for r in range(rows2):
                if r < 1:
                    row = cache_up[f, 2]
                elif r < 1 + rows:
                    row = cache_two[f, r - 1]
                else:
                    row = cache_dn[f, 2]
                put(v, f, r, dot(place, row))

    for j in range(4):
        pair = dot(rows_of(v, 1, j, rows), both(w, u, j, 1, 0))
        acc[j, 0] = pair[:, :c] + dot(rows_of(v, 0, j, rows), taps_of(w, u, j, 0))
        acc[j, 1] = pair[:, c:]

    back = places(width, 1, False)

    def finish(i, _):
        t = i // rows
        r = i % rows
        m = [acc[j, t, pl.ds(pl.multiple_of(r * half, half), half)] for j in range(4)]
        even = part[t, r, 0:half] + m[0] + m[1] + m[2]
        odd = part[t, r, half:width] + m[1] - m[2] - m[3]
        out_ref[t, r] = dot(back, jnp.concatenate([even, odd], 0).astype(BF)).astype(BF)
        return 0

    lax.fori_loop(0, 2 * rows, finish, 0)


def on_device(
    latent, cache_lat, cache_one, cache_two, w_in, b_in, gain_one, w_one, b_one, gain_two, w_two, b_two
):
    tm = lax.axis_index("tm")
    tiles = lax.axis_size("tile")
    frames, rows, width, chan = latent.shape
    c = w_in.shape[-1]
    half = width // 2

    own = jnp.swapaxes(latent, 2, 3)
    cache = jnp.swapaxes(cache_lat, 2, 3)
    prev1 = shifted(own, "tm", 1)
    prev2 = shifted(own, "tm", 2)
    prev1 = jnp.where(tm == 0, cache, prev1)
    prev2 = jnp.where(tm == 1, cache, prev2)
    six = jnp.concatenate([prev2, prev1, own], 0)
    up = shifted(six[:, rows - 3 :], "tile", 1)
    dn = shifted(six[:, :3], "tile", -1)

    caches = jnp.concatenate([cache_one[:, rows - 2 :], cache_two[:, rows - 1 :]], 1)
    cache_up = first_frames_only(caches, 1)
    caches = jnp.concatenate([cache_one[:, :2], cache_two[:, :1]], 1)
    cache_dn = first_frames_only(caches, -1)
    w1 = w_one.reshape(9, 3, c, c)
    w2 = w_two.reshape(9, 3, c, c)
    u1 = summed_kernels(w1)
    u2 = summed_kernels(w2)

    def row(x):
        return x.reshape(1, c)

    def flat(x):
        return x.reshape(-1, width)

    n2, h0 = pl.pallas_call(
        functools.partial(first_conv_body, tiles),
        out_shape=[
            jax.ShapeDtypeStruct((2, rows + 2, width, c), BF),
            jax.ShapeDtypeStruct((2, rows, width, c), BF),
        ],
        in_specs=in_vmem(15),
        out_specs=in_vmem(2),
        scratch_shapes=[
            VMEM((6, (rows + 6) * 4 * chan, width), BF),
            VMEM((6 * width, (rows + 6) * 4 * chan), BF),
            VMEM((48 * chan, 2 * c), BF),
            VMEM(((rows + 4) // 2, 4 * width, 2 * c), BF),
            VMEM((4, 4, rows + 4, half, c), BF),
            VMEM((4, 2, (rows + 2) * half, c), F32),
        ],
        compiler_params=limit(28),
        name="first_conv",
        cost_estimate=pl.CostEstimate(flops=14_000_000_000, bytes_accessed=14_000_000, transcendentals=0),
    )(
        flat(own), flat(prev1), flat(prev2), flat(up), flat(dn), cache_one, cache_up, cache_dn,
        w_in.reshape(-1, c), row(b_in), row(gain_one), w1, u1, row(b_one), row(gain_two),
    )
    earlier = shifted(n2, "tm", 1)
    part = pl.pallas_call(
        own_frames_body,
        out_shape=jax.ShapeDtypeStruct((2, rows, width, c), F32),
        in_specs=in_vmem(5),
        out_specs=in_vmem(1)[0],
        scratch_shapes=[
            VMEM((2, 4, rows + 2, half, c), BF),
            VMEM((4, 2, rows * half, c), F32),
        ],
        compiler_params=limit(16),
        name="own_frames",
        cost_estimate=pl.CostEstimate(flops=4_000_000_000, bytes_accessed=14_000_000, transcendentals=0),
    )(n2, w2, u2, h0, row(b_two))
    return pl.pallas_call(
        earlier_frames_body,
        out_shape=jax.ShapeDtypeStruct((2, rows, width, c), BF),
        in_specs=in_vmem(7),
        out_specs=in_vmem(1)[0],
        scratch_shapes=[
            VMEM((2, 4, rows + 2, half, c), BF),
            VMEM((4, 2, rows * half, c), F32),
        ],
        compiler_params=limit(16),
        name="earlier_frames",
        cost_estimate=pl.CostEstimate(flops=4_000_000_000, bytes_accessed=14_000_000, transcendentals=0),
    )(earlier, cache_two, cache_up, cache_dn, w2, u2, part)


def solution(mesh):
    return jax.shard_map(
        on_device,
        mesh=mesh,
        in_specs=(
            P("tm", "tile", None, None),
            P(None, "tile", None, None),
            P(None, "tile", None, None),
            P(None, "tile", None, None),
            P(),
            P(),
            P(),
            P(),
            P(),
            P(),
            P(),
            P(),
        ),
        out_specs=P("tm", "tile", None, None),
        check_vma=False,
    )
```

time: 88.5 us -> 68.9 us (0.78)
  the two profiles are of different devices: /device:TPU:0 before, /device:TPU:20 now
where the time goes in v2:
time: 68.9 us; the launch traced here: 68.4 us
  Pallas kernels  34.6 us (50%)
  starting transfers between devices  14.8 us (21%)
  waiting for transfers between devices  9.84 us (14%)
  local copies, waits for them, and re-layouts  7.17 us (10%)
  other arithmetic  1.68 us (2%)
    pallas_call x1, Pallas kernels, on_device(): pl.pallas_call(functools.partial(first_conv_body, tiles), out_shape=[jax....  19.8 us
    ppermute x5, starting transfers between devices, shifted(): lax.ppermute(x, axis, [(i, i + by) for i in range(count) if 0 <= i + by <...  13.4 us
    ppermute x5, waiting for transfers between devices, shifted(): lax.ppermute(x, axis, [(i, i + by) for i in range(count) if 0 <= i + by <...  9.83 us
    pallas_call x1, Pallas kernels, on_device(): pl.pallas_call(earlier_frames_body, out_shape=jax.ShapeDtypeStruct((2, ro...  6.56 us
    unnamed x26, local copies, waits for them, and re-layouts  4.86 us
    pallas_call x1, Pallas kernels, on_device(): pl.pallas_call(own_frames_body, out_shape=jax.ShapeDtypeStruct((2, rows,...  4.57 us
    pallas_call x2, Pallas kernels, summed_kernels(): pl.pallas_call(summed_kernels_body, in_specs=in_vmem(1), out_specs=in_vme...  3.68 us
    slice x2, local copies, waits for them, and re-layouts, on_device(): caches = jnp.concatenate([cache_one[:, :2], cache_two[:, :1]], 1)  2.27 us
  transfers between devices with their start and end apart: 7, of which 1 were waited for; matrix products, arithmetic and copies ran while one was open for 6% of the time, Pallas kernels for 12%

profile of v2, /device:TPU:20, one launch (start us, length us, event | category | flops | bytes accessed | tf_op | source)
XLA Modules:
  0.0 68.4 jit_solution(3801071495294057159)
XLA Ops:
  0.0 2.1 %collective-permute-start = (bf16[2,4,16,128]{3,2,1,0:T(8,128)(2,1)}, bf16[2,4,16,128]{3,2,1,0:T(8,128)(2,1)S(1)}, u32[]{:S(2)}, u32[]{:S(2)}) collective-permute-start(bf16[2,4,16,128]{3,2,1,0:T(8,128)(2,1)} %bitcast.22), channel_id=1, source_target_pairs={{0,4},{4,8},{8,12},{12,16},{16,20},{20,24},{24,28},{1,5},{5,9},{9,... | collective-permute-start | bytes 98312 | tf_op jit(solution)/shard_map/ppermute | solution.py:17
  2.1 3.4 %collective-permute-start.1 = (bf16[2,4,16,128]{3,2,1,0:T(8,128)(2,1)}, bf16[2,4,16,128]{3,2,1,0:T(8,128)(2,1)S(1)}, u32[]{:S(2)}, u32[]{:S(2)}) collective-permute-start(bf16[2,4,16,128]{3,2,1,0:T(8,128)(2,1)} %bitcast.23), channel_id=1, source_target_pairs={{0,8},{4,12},{8,16},{12,20},{16,24},{20,28},{1,9},{5,13},{9,17},{1... | collective-permute-start | bytes 98312 | tf_op jit(solution)/shard_map/ppermute | solution.py:17
  5.5 1.2 %fusion = (bf16[2,2,128,384]{3,2,1,0:T(8,128)(2,1)S(1)}, bf16[2,2,128,384]{3,2,1,0:T(8,128)(2,1)S(1)}) fusion(bf16[2,4,128,384]{3,2,1,0:T(8,128)(2,1)} %cache_one.1), kind=kLoop, calls=%fused_computation.5 | loop fusion | bytes 1572864 | tf_op jit(solution)/shard_map/slice | solution.py:351
  6.7 1.1 %fusion.1 = (bf16[2,1,128,384]{3,2,1,0:T(8,128)(2,1)S(1)}, bf16[2,1,128,384]{3,2,1,0:T(8,128)(2,1)S(1)}) fusion(bf16[2,4,128,384]{3,2,1,0:T(8,128)(2,1)} %cache_two.1), kind=kLoop, calls=%fused_computation.6 | loop fusion | bytes 786432 | tf_op jit(solution)/shard_map/slice | solution.py:351
  7.8 0.1 pad_maximum_fusion
  7.8 0.7 %collective-permute-start.4 = (bf16[2,3,128,384]{3,2,1,0:T(8,128)(2,1)S(1)}, bf16[2,3,128,384]{3,2,1,0:T(8,128)(2,1)S(1)}, u32[]{:S(2)}, u32[]{:S(2)}) collective-permute-start(bf16[2,3,128,384]{3,2,1,0:T(8,128)(2,1)S(1)} %pad_maximum_fusion), channel_id=1, source_target_pairs={{0,1},{1,2},{2,3}} | collective-permute-start | bytes 1769480 | tf_op jit(solution)/shard_map/ppermute | solution.py:22
  8.6 0.1 pad_maximum_fusion.1
  8.6 0.7 %collective-permute-start.5 = (bf16[2,3,128,384]{3,2,1,0:T(8,128)(2,1)S(1)}, bf16[2,3,128,384]{3,2,1,0:T(8,128)(2,1)S(1)}, u32[]{:S(2)}, u32[]{:S(2)}) collective-permute-start(bf16[2,3,128,384]{3,2,1,0:T(8,128)(2,1)S(1)} %pad_maximum_fusion.1), channel_id=1, source_target_pairs={{1,0},{2,1},{3,2}} | collective-permute-start | bytes 1769480 | tf_op jit(solution)/shard_map/ppermute | solution.py:22
  9.3 0.0 collective-permute-done
  9.4 0.0 collective-permute-done.1
  9.4 0.8 %bitcast_select_fusion = (bf16[2,4,16,128]{3,2,1,0:T(8,128)(2,1)S(1)}, bf16[2,4,16,128]{3,2,1,0:T(8,128)(2,1)S(1)}) fusion(bf16[2,4,16,128]{3,2,1,0:T(8,128)(2,1)S(1)} %collective-permute-done.1, bf16[2,4,128,16]{2,3,1,0:T(8,128)(2,1)} %param.13, pred[]{:T(512)S(6)} %eq.7, bf16[2,4,16,128]{3,2,1,0:T(8,128)(2,1)S(1)} %collective-permute-done, pred[]{:T(512)S(6)} %eq.6), kind=kLoop, calls=%fused_computation.3 | loop fusion | flops 32768 | bytes 163842 | tf_op jit(solution)/shard_map/jit(_where)/select_n | solution.py:344
  10.1 0.8 %pad_maximum_fusion.2 = bf16[6,4,16,128]{3,2,1,0:T(8,128)(2,1)S(1)} fusion(bf16[2,4,16,128]{3,2,1,0:T(8,128)(2,1)} %bitcast.24, bf16[2,4,16,128]{3,2,1,0:T(8,128)(2,1)S(1)} %get-tuple-element.16, bf16[2,4,16,128]{3,2,1,0:T(8,128)(2,1)S(1)} %get-tuple-element.15), kind=kLoop, calls=%fused_computation.2 | loop fusion | flops 98304 | bytes 196608 | tf_op jit(solution)/shard_map/concatenate | solution.py:345
  10.9 3.5 %collective-permute-start.2 = (bf16[6,3,16,128]{3,2,1,0:T(8,128)(2,1)S(1)}, bf16[6,3,16,128]{3,2,1,0:T(8,128)(2,1)S(1)}, u32[]{:S(2)}, u32[]{:S(2)}) collective-permute-start(bf16[6,3,16,128]{3,2,1,0:T(8,128)(2,1)S(1)} %get-tuple-element.14), channel_id=1, source_target_pairs={{0,1},{1,2},{2,3},{4,5},{5,6},{6,7},{8,9},{9,10},{10,11},{12,13},{... | collective-permute-start | bytes 221192 | tf_op jit(solution)/shard_map/ppermute | solution.py:17
  14.4 2.4 %collective-permute-start.3 = (bf16[6,3,16,128]{3,2,1,0:T(8,128)(2,1)S(1)}, bf16[6,3,16,128]{3,2,1,0:T(8,128)(2,1)S(1)}, u32[]{:S(2)}, u32[]{:S(2)}) collective-permute-start(bf16[6,3,16,128]{3,2,1,0:T(8,128)(2,1)S(1)} %get-tuple-element.13), channel_id=1, source_target_pairs={{1,0},{2,1},{3,2},{5,4},{6,5},{7,6},{9,8},{10,9},{11,10},{13,12},{... | collective-permute-start | bytes 221192 | tf_op jit(solution)/shard_map/ppermute | solution.py:17
  16.9 0.0 copy-start
  16.9 3.3 %copy-done = bf16[3,3,3,384,384]{4,3,2,1,0:T(8,128)(2,1)S(1)} copy-done((bf16[3,3,3,384,384]{4,3,2,1,0:T(8,128)(2,1)S(1)}, bf16[3,3,3,384,384]{4,3,2,1,0:T(8,128)(2,1)}, u32[]{:S(2)}) %copy-start) | copy-done | bytes 7962648
  20.2 1.8 %summed_kernels.2.u = bf16[2,9,384,384]{3,2,1,0:T(8,128)(2,1)S(1)} custom-call(bf16[9,3,384,384]{3,2,1,0:T(8,128)(2,1)S(1)} %bitcast.18), custom_call_target="tpu_custom_call" | custom-call | flops 7962624 | bytes 13271040 | tf_op jit(solution)/shard_map/summed_kernels/pallas_call | solution.py:69
  22.0 0.0 collective-permute-done.2
  22.0 0.0 collective-permute-done.3
  22.0 0.0 collective-permute-done.4.cache_up
  22.0 0.0 collective-permute-done.5.cache_dn
  22.0 0.0 slice-start
  22.1 1.3 %copy-done.1 = bf16[3,3,3,384,384]{4,3,2,1,0:T(8,128)(2,1)S(1)} copy-done((bf16[3,3,3,384,384]{4,3,2,1,0:T(8,128)(2,1)S(1)}, bf16[3,3,3,384,384]{4,3,2,1,0:T(8,128)(2,1)}, u32[]{:S(2)}) %copy-start.1) | copy-done | bytes 7962648
  23.4 0.1 copy-done.3
  23.5 0.1 copy-done.5
  23.6 19.8 %first_conv.1 = (bf16[2,6,128,384]{3,2,1,0:T(8,128)(2,1)S(1)}, bf16[2,4,128,384]{3,2,1,0:T(8,128)(2,1)S(1)}) custom-call(bf16[128,128]{1,0:T(8,128)(2,1)S(1)} %bitcast.25, bf16[128,128]{1,0:T(8,128)(2,1)S(1)} %bitcast.21, bf16[128,128]{1,0:T(8,128)(2,1)S(1)} %bitcast.20, bf16[288,128]{1,0:T(8,128)(2,1)S(1)} %bitcast.27, bf16[288,128]{1,0:T(8,128)(2,1)S(1)} %bitcast.28, ...), custom_call_target="tpu_custom_call" | custom-call | flops 14000000000 | bytes 14000000 | tf_op jit(solution)/shard_map/first_conv/pallas_call | solution.py:364
  43.4 2.1 %collective-permute-start.6 = (bf16[2,6,128,384]{3,2,1,0:T(8,128)(2,1)S(1)}, bf16[2,6,128,384]{3,2,1,0:T(8,128)(2,1)S(1)}, u32[]{:S(2)}, u32[]{:S(2)}) collective-permute-start(bf16[2,6,128,384]{3,2,1,0:T(8,128)(2,1)S(1)} %get-tuple-element.7.n2), channel_id=1, source_target_pairs={{0,4},{4,8},{8,12},{12,16},{16,20},{20,24},{24,28},{1,5},{5,9},{9,... | collective-permute-start | bytes 3538952 | tf_op jit(solution)/shard_map/ppermute | solution.py:17
  45.6 1.8 %summed_kernels.3.u = bf16[2,9,384,384]{3,2,1,0:T(8,128)(2,1)S(1)} custom-call(bf16[9,3,384,384]{3,2,1,0:T(8,128)(2,1)S(1)} %bitcast.15), custom_call_target="tpu_custom_call" | custom-call | flops 7962624 | bytes 13271040 | tf_op jit(solution)/shard_map/summed_kernels/pallas_call | solution.py:69
  47.4 0.0 copy-start.2
  47.5 4.6 %own_frames.1.part = f32[2,4,128,384]{3,2,1,0:T(8,128)S(1)} custom-call(bf16[2,6,128,384]{3,2,1,0:T(8,128)(2,1)S(1)} %get-tuple-element.7.n2, bf16[9,3,384,384]{3,2,1,0:T(8,128)(2,1)S(1)} %bitcast.16, bf16[2,9,384,384]{3,2,1,0:T(8,128)(2,1)S(1)} %summed_kernels.3.u, bf16[2,4,128,384]{3,2,1,0:T(8,128)(2,1)S(1)} %get-tuple-element.8.h0, ...), custom_call_target="tpu_custom_call" | custom-call | flops 4000000000 | bytes 14000000 | tf_op jit(solution)/shard_map/own_frames/pallas_call | solution.py:388
  52.0 9.8 %collective-permute-done.6.earlier = bf16[2,6,128,384]{3,2,1,0:T(8,128)(2,1)S(1)} collective-permute-done((bf16[2,6,128,384]{3,2,1,0:T(8,128)(2,1)S(1)}, bf16[2,6,128,384]{3,2,1,0:T(8,128)(2,1)S(1)}, u32[]{:S(2)}, u32[]{:S(2)}) %collective-permute-start.6) | collective-permute-done | bytes 1179680 | tf_op jit(solution)/shard_map/ppermute | solution.py:17
  61.9 6.6 %earlier_frames.1 = bf16[2,4,128,384]{3,2,1,0:T(8,128)(2,1)} custom-call(bf16[2,6,128,384]{3,2,1,0:T(8,128)(2,1)S(1)} %collective-permute-done.6.earlier, bf16[2,4,128,384]{3,2,1,0:T(8,128)(2,1)S(1)} %copy-done.2, bf16[2,3,128,384]{3,2,1,0:T(8,128)(2,1)S(1)} %collective-permute-done.4.cache_up, bf16[2,3,128,384]{3,2,1,0:T(8,128)(2,1)S(1)} %collective-permute-done.5.cache_dn, ...), custom_call_target="tpu_custom_call" | custom-call | flops 4000000000 | bytes 14000000 | tf_op jit(solution)/shard_map/earlier_frames/pallas_call | solution.py:401
  (26 shorter events, 0.1 us)
Async XLA Ops:
  0.0 16.8 %copy-start.6 = (f32[384]{0:T(512)S(1)}, f32[384]{0:T(512)}, u32[]{:S(2)}) copy-start(f32[384]{0:T(512)} %param.17) | copy-start | bytes 4612
  0.0 16.8 %copy-start.7 = (f32[384]{0:T(512)S(1)}, f32[384]{0:T(512)}, u32[]{:S(2)}) copy-start(f32[384]{0:T(512)} %param.18) | copy-start | bytes 4612
  0.0 16.8 %copy-start.8 = (f32[384]{0:T(512)S(1)}, f32[384]{0:T(512)}, u32[]{:S(2)}) copy-start(f32[384]{0:T(512)} %param.20) | copy-start | bytes 4612
  0.0 16.8 %copy-start.9 = (f32[384]{0:T(512)S(1)}, f32[384]{0:T(512)}, u32[]{:S(2)}) copy-start(f32[384]{0:T(512)} %param.21) | copy-start | bytes 4612
  0.0 9.3 %collective-permute-start = (bf16[2,4,16,128]{3,2,1,0:T(8,128)(2,1)}, bf16[2,4,16,128]{3,2,1,0:T(8,128)(2,1)S(1)}, u32[]{:S(2)}, u32[]{:S(2)}) collective-permute-start(bf16[2,4,16,128]{3,2,1,0:T(8,128)(2,1)} %bitcast.22), channel_id=1, source_target_pairs={{0,4},{4,8},{8,12},{12,16},{16,20},{20,24},{24,28},{1,5},{5,9},{9,... | collective-permute-start | bytes 98312 | tf_op jit(solution)/shard_map/ppermute | solution.py:17
  2.1 7.3 %collective-permute-start.1 = (bf16[2,4,16,128]{3,2,1,0:T(8,128)(2,1)}, bf16[2,4,16,128]{3,2,1,0:T(8,128)(2,1)S(1)}, u32[]{:S(2)}, u32[]{:S(2)}) collective-permute-start(bf16[2,4,16,128]{3,2,1,0:T(8,128)(2,1)} %bitcast.23), channel_id=1, source_target_pairs={{0,8},{4,12},{8,16},{12,20},{16,24},{20,28},{1,9},{5,13},{9,17},{1... | collective-permute-start | bytes 98312 | tf_op jit(solution)/shard_map/ppermute | solution.py:17
  7.8 14.2 %collective-permute-start.4 = (bf16[2,3,128,384]{3,2,1,0:T(8,128)(2,1)S(1)}, bf16[2,3,128,384]{3,2,1,0:T(8,128)(2,1)S(1)}, u32[]{:S(2)}, u32[]{:S(2)}) collective-permute-start(bf16[2,3,128,384]{3,2,1,0:T(8,128)(2,1)S(1)} %pad_maximum_fusion), channel_id=1, source_target_pairs={{0,1},{1,2},{2,3}} | collective-permute-start | bytes 1769480 | tf_op jit(solution)/shard_map/ppermute | solution.py:22
  8.6 13.4 %collective-permute-start.5 = (bf16[2,3,128,384]{3,2,1,0:T(8,128)(2,1)S(1)}, bf16[2,3,128,384]{3,2,1,0:T(8,128)(2,1)S(1)}, u32[]{:S(2)}, u32[]{:S(2)}) collective-permute-start(bf16[2,3,128,384]{3,2,1,0:T(8,128)(2,1)S(1)} %pad_maximum_fusion.1), channel_id=1, source_target_pairs={{1,0},{2,1},{3,2}} | collective-permute-start | bytes 1769480 | tf_op jit(solution)/shard_map/ppermute | solution.py:22
  10.9 11.1 %collective-permute-start.2 = (bf16[6,3,16,128]{3,2,1,0:T(8,128)(2,1)S(1)}, bf16[6,3,16,128]{3,2,1,0:T(8,128)(2,1)S(1)}, u32[]{:S(2)}, u32[]{:S(2)}) collective-permute-start(bf16[6,3,16,128]{3,2,1,0:T(8,128)(2,1)S(1)} %get-tuple-element.14), channel_id=1, source_target_pairs={{0,1},{1,2},{2,3},{4,5},{5,6},{6,7},{8,9},{9,10},{10,11},{12,13},{... | collective-permute-start | bytes 221192 | tf_op jit(solution)/shard_map/ppermute | solution.py:17
  14.4 7.6 %collective-permute-start.3 = (bf16[6,3,16,128]{3,2,1,0:T(8,128)(2,1)S(1)}, bf16[6,3,16,128]{3,2,1,0:T(8,128)(2,1)S(1)}, u32[]{:S(2)}, u32[]{:S(2)}) collective-permute-start(bf16[6,3,16,128]{3,2,1,0:T(8,128)(2,1)S(1)} %get-tuple-element.13), channel_id=1, source_target_pairs={{1,0},{2,1},{3,2},{5,4},{6,5},{7,6},{9,8},{10,9},{11,10},{13,12},{... | collective-permute-start | bytes 221192 | tf_op jit(solution)/shard_map/ppermute | solution.py:17
  16.9 3.3 %copy-start = (bf16[3,3,3,384,384]{4,3,2,1,0:T(8,128)(2,1)S(1)}, bf16[3,3,3,384,384]{4,3,2,1,0:T(8,128)(2,1)}, u32[]{:S(2)}) copy-start(bf16[3,3,3,384,384]{4,3,2,1,0:T(8,128)(2,1)} %param.19) | copy-start | bytes 23887876
  20.1 3.3 %copy-start.1 = (bf16[3,3,3,384,384]{4,3,2,1,0:T(8,128)(2,1)S(1)}, bf16[3,3,3,384,384]{4,3,2,1,0:T(8,128)(2,1)}, u32[]{:S(2)}) copy-start(bf16[3,3,3,384,384]{4,3,2,1,0:T(8,128)(2,1)} %param.19) | copy-start | bytes 23887876
  20.1 3.4 %copy-start.3 = (bf16[2,4,128,384]{3,2,1,0:T(8,128)(2,1)S(1)}, bf16[2,4,128,384]{3,2,1,0:T(8,128)(2,1)}, u32[]{:S(2)}) copy-start(bf16[2,4,128,384]{3,2,1,0:T(8,128)(2,1)} %cache_one.1) | copy-start | bytes 2359300
  20.1 3.4 %copy-start.4 = (bf16[2,4,128,16]{2,3,1,0:T(8,128)(2,1)S(1)}, bf16[2,4,128,16]{2,3,1,0:T(8,128)(2,1)}, u32[]{:S(2)}) copy-start(bf16[2,4,128,16]{2,3,1,0:T(8,128)(2,1)} %param.12) | copy-start | bytes 98308
  20.1 3.5 %copy-start.5 = (bf16[3,3,3,16,384]{4,3,2,1,0:T(8,128)(2,1)S(1)}, bf16[3,3,3,16,384]{4,3,2,1,0:T(8,128)(2,1)}, u32[]{:S(2)}) copy-start(bf16[3,3,3,16,384]{4,3,2,1,0:T(8,128)(2,1)} %param.16) | copy-start | bytes 995332
  22.0 23.5 %slice-start = ((s8[7962624]{0:T(1024)(128)(4,1)}), s8[4194304]{0:T(1024)(128)(4,1)S(1)}, s32[]{:S(2)}) async-start(s8[7962624]{0:T(1024)(128)(4,1)} %bitcast.13), calls=%async_computation | async-start | bytes 8388608
  23.6 21.9 %copy-start.10 = (f32[384]{0:T(512)S(1)}, f32[384]{0:T(512)}, u32[]{:S(2)}) copy-start(f32[384]{0:T(512)} %param.23) | copy-start | bytes 4612
  23.6 22.0 %slice-start.1 = ((s8[7962624]{0:T(1024)(128)(4,1)}), s8[3768320]{0:T(1024)(128)(4,1)S(1)}, s32[]{:S(2)}) async-start(s8[7962624]{0:T(1024)(128)(4,1)} %bitcast.13), calls=%async_computation.1 | async-start | bytes 7536640
  43.4 18.4 %collective-permute-start.6 = (bf16[2,6,128,384]{3,2,1,0:T(8,128)(2,1)S(1)}, bf16[2,6,128,384]{3,2,1,0:T(8,128)(2,1)S(1)}, u32[]{:S(2)}, u32[]{:S(2)}) collective-permute-start(bf16[2,6,128,384]{3,2,1,0:T(8,128)(2,1)S(1)} %get-tuple-element.7.n2), channel_id=1, source_target_pairs={{0,4},{4,8},{8,12},{12,16},{16,20},{20,24},{24,28},{1,5},{5,9},{9,... | collective-permute-start | bytes 3538952 | tf_op jit(solution)/shard_map/ppermute | solution.py:17
  47.4 14.4 %copy-start.2 = (bf16[2,4,128,384]{3,2,1,0:T(8,128)(2,1)S(1)}, bf16[2,4,128,384]{3,2,1,0:T(8,128)(2,1)}, u32[]{:S(2)}) copy-start(bf16[2,4,128,384]{3,2,1,0:T(8,128)(2,1)} %cache_two.1) | copy-start | bytes 2359300

commit v3 on v2

v3 whole, which is shorter than its diff:
```python
import functools

import jax
import jax.numpy as jnp
from jax import lax
from jax.experimental import pallas as pl
from jax.experimental.pallas import tpu as pltpu
from jax.sharding import PartitionSpec as P

BF = jnp.bfloat16
F32 = jnp.float32
VMEM = pltpu.VMEM


def shifted(x, axis, by):
    count = lax.axis_size(axis)
    return lax.ppermute(x, axis, [(i, i + by) for i in range(count) if 0 <= i + by < count])


def first_frames_only(x, by):
    rows = lax.axis_size("tile")
    return lax.ppermute(
        x, ("tm", "tile"), [(i, i + by) for i in range(rows) if 0 <= i + by < rows]
    )


def column_of(place, width):
    half = width // 2
    return jnp.where(place < half, 2 * place, 2 * (place - half) + 1)


def silu_of_twice(h):
    return h + h * jnp.tanh(h)


def rms(v, gain):
    return v * lax.rsqrt(jnp.mean(v * v, -1, keepdims=True) + 1e-6) * gain


def filtered(even, odd):
    half = even.shape[0]
    place = lax.broadcasted_iota(jnp.int32, even.shape, 0)
    odd_before = jnp.where(place == 0, 0.0, pltpu.roll(odd, 1, 0))
    even_after = jnp.where(place == half - 1, 0.0, pltpu.roll(even, half - 1, 0))
    return (
        (odd_before - odd).astype(BF),
        (even + odd).astype(BF),
        (odd - even).astype(BF),
        (even - even_after).astype(BF),
    )


def dot(a, b):
    return jnp.dot(a, b, preferred_element_type=F32)


def in_vmem(count):
    return [pl.BlockSpec(memory_space=VMEM)] * count


def limit(mib):
    return pltpu.CompilerParams(vmem_limit_bytes=mib << 20)


def places(width, dx, transposed):
    shape = (width, width)
    to = column_of(lax.broadcasted_iota(jnp.int32, shape, 0 if transposed else 1), width)
    at = lax.broadcasted_iota(jnp.int32, shape, 1 if transposed else 0)
    return jnp.where(at == to + (dx - 1), 1.0, 0.0).astype(BF)


def put(v, f, r, row):
    half = row.shape[0] // 2
    parts = filtered(row[:half], row[half:])
    for j in range(4):
        v[f][j, r] = parts[j]


def plain_and_sums(w, u):
    return lambda j, i: w[i, 0] if j == 0 else w[i, 2] if j == 3 else u[j - 1, i]


def taps_of(w, j, dt):
    return jnp.concatenate([w(j, 3 * dt + dy) for dy in range(3)], 0)


def both(w, j, dt_a, dt_b):
    return jnp.concatenate([taps_of(w, j, dt_a), taps_of(w, j, dt_b)], 1)


def rows_of(v, f, j, at, rows):
    half, c = v[f].shape[-2:]
    return jnp.concatenate(
        [v[f][j, at + dy : at + dy + rows].reshape(rows * half, c) for dy in range(3)], 1
    )


def sum_taps(w, u, i):
    s = 0.5 * (w[i, 0].astype(F32) + w[i, 2].astype(F32))
    h = 0.5 * w[i, 1].astype(F32)
    u[0, i] = (s + h).astype(BF)
    u[1, i] = (s - h).astype(BF)


def summed_kernels_body(w, u):
    def tap(i, _):
        sum_taps(w, u, i)
        return 0

    lax.fori_loop(0, w.shape[0], tap, 0)


def summed_kernels(w):
    taps, _, c, o = w.shape
    return pl.pallas_call(
        summed_kernels_body,
        in_specs=in_vmem(1),
        out_specs=in_vmem(1)[0],
        out_shape=jax.ShapeDtypeStruct((2, taps, c, o), BF),
        compiler_params=limit(16),
        name="summed_kernels",
        cost_estimate=pl.CostEstimate(flops=6 * taps * c * o, bytes_accessed=10 * taps * c * o, transcendentals=0),
    )(w)


def border_rows_body(chan, own, prev1, prev2, cache, one, two, to_dn, to_up):
    tm = lax.axis_index("tm")
    one[...] = jnp.where(tm == 0, cache[...], prev1[...])
    two[...] = jnp.where(tm == 1, cache[...], prev2[...])
    frame = own.shape[0] // 2
    for f, src in enumerate((two, two, one, one, own, own)):
        at = (f % 2) * frame
        to_dn[f * 3 * chan : (f + 1) * 3 * chan] = src[at + frame - 3 * chan : at + frame]
        to_up[f * 3 * chan : (f + 1) * 3 * chan] = src[at : at + 3 * chan]


def border_rows(chan, own, prev1, prev2, cache):
    same = jax.ShapeDtypeStruct(own.shape, BF)
    edge = jax.ShapeDtypeStruct((18 * chan, own.shape[1]), BF)
    return pl.pallas_call(
        functools.partial(border_rows_body, chan),
        in_specs=in_vmem(4),
        out_specs=in_vmem(4),
        out_shape=[same, same, edge, edge],
        compiler_params=limit(4),
        name="border_rows",
        cost_estimate=pl.CostEstimate(flops=6_000_000_000, bytes_accessed=400_000, transcendentals=0),
    )(own, prev1, prev2, cache)


def conv_pair(v, w, acc, j, at, rows):
    c = v[0].shape[-1]
    pair = dot(
        jnp.concatenate([rows_of(v, 1, j, at, rows), rows_of(v, 2, j, at, rows)], 1),
        jnp.concatenate([both(w, j, 1, 0), both(w, j, 2, 1)], 0),
    )
    acc[j, 0] = pair[:, :c]
    acc[j, 1] = pair[:, c:]


def finish_norm(tiles, acc, b_one, gain_two, n2_ref, t, r, at):
    half = n2_ref.shape[2] // 2
    rows = pl.ds(r * half, half)
    m = [acc[j, t, rows] for j in range(4)]
    rows_here = lax.axis_index("tile")
    at_row = rows_here * (tiles[1] // tiles[0]) + at + r - 1
    keep = jnp.logical_and(at_row >= 0, at_row < tiles[1])
    gain = jnp.where(keep, 0.5 * gain_two[...], 0.0)
    even = m[0] + m[1] + m[2] + b_one[...]
    odd = m[1] - m[2] - m[3] + b_one[...]
    n2_ref[t, r, 0:half] = silu_of_twice(rms(even, gain)).astype(BF)
    n2_ref[t, r, half:] = silu_of_twice(rms(odd, gain)).astype(BF)


def conv_normed(tiles, v, w, acc, b_one, gain_two, n2_ref, at, beside):
    rows = n2_ref.shape[1]
    for n, j in enumerate((0, 3, 1, 2)):
        beside[n]()
        conv_pair(v, w, acc, j, at, rows)
    for j in range(4):
        acc[j, 0] += dot(rows_of(v, 0, j, at, rows), taps_of(w, j, 0))
    for j in range(4):
        if j < rows:
            finish_norm(tiles, acc, b_one, gain_two, n2_ref, 0, j, at)
        acc[j, 1] += dot(rows_of(v, 3, j, at, rows), taps_of(w, j, 2))
    for r in range(rows):
        finish_norm(tiles, acc, b_one, gain_two, n2_ref, 1, r, at)


def first_conv_body(
    tiles,
    own, prev1, prev2, up, dn, cache_one, cache_up, cache_dn,
    w_in, b_in, gain_one, w, u, b_one, gain_two,
    n2_ref, v0, v1, v2, v3, h0_ref,
    lats, g, w_big, hs, cached, acc,
):
    v = (v0, v1, v2, v3)
    tm = lax.axis_index("tm")
    tile = lax.axis_index("tile")
    width = own.shape[-1]
    c = w_in.shape[1]
    chan = w_in.shape[0] // 27
    rows = own.shape[0] // (2 * chan)
    rows1 = rows + 4
    slot = 4 * chan

    @pl.when(tm == 0)
    def _():
        place = places(width, 1, True)
        for f in range(2):
            for r in range(rows1):
                if r < 2:
                    row = cache_up[f, r]
                elif r < 2 + rows:
                    row = cache_one[f, r - 2]
                else:
                    row = cache_dn[f, r - 2 - rows]
                cached[f, r] = dot(place, row).astype(BF)

    lats[...] = jnp.zeros_like(lats)
    place = jnp.concatenate([places(width, dx, False) for dx in range(3)], 1)

    def lay(block, f0, r0, count):
        moved = dot(block, place).astype(BF)
        for i in range(block.shape[0] // chan):
            f, r = f0 + i // count, r0 + i % count
            for dx in range(3):
                lats[f, r * slot + dx * chan : r * slot + (dx + 1) * chan] = moved[
                    i * chan : (i + 1) * chan, dx * width : (dx + 1) * width
                ]

    lay(up[...], 0, 0, 3)
    lay(prev2[...], 0, 3, rows)
    lay(prev1[...], 2, 3, rows)
    lay(own[...], 4, 3, rows)
    lay(dn[...], 0, 3 + rows, 3)
    eye = jnp.where(
        lax.broadcasted_iota(jnp.int32, (width, width), 0)
        == lax.broadcasted_iota(jnp.int32, (width, width), 1),
        1.0,
        0.0,
    ).astype(BF)
    for f in range(6):
        g[f * width : (f + 1) * width] = lax.dot_general(
            eye, lats[f], (((1,), (1,)), ((), ())), preferred_element_type=F32
        ).astype(BF)

    w_big[...] = jnp.zeros_like(w_big)
    for dt in range(3):
        for dy in range(3):
            taps = w_in[(3 * dt + dy) * 3 * chan : (3 * dt + dy + 1) * 3 * chan]
            for k in range(2):
                start = (4 * dt + dy + k) * slot
                w_big[start : start + 3 * chan, k * c : (k + 1) * c] = taps
    bias = jnp.concatenate([b_in[...], b_in[...]], 1)

    def project(p):
        patches = jnp.concatenate(
            [
                g[dt * width : (dt + 4) * width, 2 * p * slot : (2 * p + 4) * slot]
                for dt in range(3)
            ],
            1,
        )
        hs[p] = (dot(patches, w_big[...]) + bias).astype(BF)

    def normed(f, r):
        p, k = r // 2, r % 2
        h0 = hs[p, f * width : (f + 1) * width, k * c : (k + 1) * c]
        if f >= 2 and 2 <= r < 2 + rows:
            h0_ref[f - 2, r - 2] = h0
        at_row = tile * rows + r - 2
        keep = jnp.logical_and(at_row >= 0, at_row < tiles[1])
        gain = jnp.where(keep, 0.5 * gain_one[...], 0.0)
        n1 = silu_of_twice(rms(h0.astype(F32), gain)).astype(BF).astype(F32)
        if f < 2:
            n1 = jnp.where(tm == 0, cached[f, r].astype(F32), n1)
        put(v, f, r, n1)

    part = n2_ref.shape[1]
    needed = part + 2
    pairs = rows1 // 2
    ahead = 2
    for p in range(ahead):
        project(p)
    for p in range(pairs):
        if p + ahead < pairs:
            project(p + ahead)
        for r in (2 * p, 2 * p + 1):
            if r < needed:
                for f in range(4):
                    normed(f, r)

    def rest(n):
        def work():
            for r in range(needed, rows1):
                normed(n, r)

        return work

    conv_normed(tiles, v, plain_and_sums(w, u), acc, b_one, gain_two, n2_ref, 0, [rest(n) for n in range(4)])


def second_part_body(tiles, v0, v1, v2, v3, w, u, b_one, gain_two, n2_ref, acc):
    v = (v0, v1, v2, v3)
    at = n2_ref.shape[1]
    idle = [lambda: None] * 4
    conv_normed(tiles, v, plain_and_sums(w, u), acc, b_one, gain_two, n2_ref, at, idle)


def cached_rows(cache_two, cache_up, cache_dn, first, count, cached):
    rows = cache_two.shape[1]

    @pl.when(lax.axis_index("tm") == 0)
    def _():
        place = places(cache_two.shape[2], 1, True)
        for f in range(2):
            for i in range(count):
                r = first + i
                if r < 1:
                    row = cache_up[f, 2]
                elif r < 1 + rows:
                    row = cache_two[f, r - 1]
                else:
                    row = cache_dn[f, 2]
                cached[f, i] = dot(place, row).astype(BF)


def split_earlier(v, f, earlier, cached):
    at_start = lax.axis_index("tm") == 0
    for r in range(earlier.shape[1]):
        row = jnp.where(at_start, cached[f, r].astype(F32), earlier[f, r].astype(F32))
        put(v, f, r, row)


def halves(first, second):
    return [(first, r) for r in range(first.shape[1])] + [(second, r) for r in range(second.shape[1])]


def own_frames_body(
    n2a, n2b, earlier, cache_two, cache_up, w, h0, b_two,
    part_ref, u, ve0, ve1,
    cached, v, acc,
):
    width, c = n2a.shape[2:]
    half = width // 2
    rows = part_ref.shape[1]
    source = halves(n2a, n2b)
    v = (v.at[0], v.at[1])
    cached_rows(cache_two, cache_up, None, 0, n2a.shape[1], cached)

    def split(f):
        for r, (ref, at) in enumerate(source):
            put(v, f, r, ref[f, at].astype(F32))

    def finish(t, r):
        m = [acc[j, t, r * half : (r + 1) * half] for j in range(4)]
        even = m[0] + m[1] + m[2] + b_two[...]
        odd = m[1] - m[2] - m[3] + b_two[...]
        part_ref[t, r, 0:half] = even + h0[t, r, 0:half].astype(F32)
        part_ref[t, r, half:] = odd + h0[t, r, half:].astype(F32)

    split(0)
    split(1)
    for i in range(w.shape[0]):
        sum_taps(w, u, i)
    kernel = plain_and_sums(w, u)
    for j in (0, 3, 1, 2):
        pair = dot(rows_of(v, 0, j, 0, rows), both(kernel, j, 2, 1))
        acc[j, 0] = pair[:, :c]
        acc[j, 1] = pair[:, c:]
        if j == 0:
            split_earlier((ve0, ve1), 0, earlier, cached)
        if j == 3:
            split_earlier((ve0, ve1), 1, earlier, cached)
    for j in range(4):
        if j < rows:
            finish(0, j)
        acc[j, 1] += dot(rows_of(v, 1, j, 0, rows), taps_of(kernel, j, 2))
    for r in range(rows):
        finish(1, r)


def rows_joined(first, last, f, j, rows):
    half, c = last[f].shape[-2:]
    split = first[f].shape[1]
    out = []
    for dy in range(3):
        a = first[f][j, dy:split].reshape((split - dy) * half, c)
        b = last[f][j, 0 : rows + dy - split].reshape((rows + dy - split) * half, c)
        out.append(jnp.concatenate([a, b], 0))
    return jnp.concatenate(out, 1)


def earlier_frames_body(
    ve0, ve1, earlier, cache_two, cache_dn, w, u, part, out_ref, cached, late, acc
):
    width, c = earlier.shape[2:]
    half = width // 2
    rows = out_ref.shape[1]
    kernel = plain_and_sums(w, u)
    first = (ve0, ve1)
    late = (late.at[0], late.at[1])
    cached_rows(cache_two, None, cache_dn, ve0.shape[1], earlier.shape[1], cached)
    back = places(width, 1, False)

    def finish(t, r):
        m = [acc[j, t, r * half : (r + 1) * half] for j in range(4)]
        even = part[t, r, 0:half] + m[0] + m[1] + m[2]
        odd = part[t, r, half:] + m[1] - m[2] - m[3]
        out_ref[t, r] = dot(back, jnp.concatenate([even, odd], 0).astype(BF)).astype(BF)

    split_earlier(late, 1, earlier, cached)
    for j in range(4):
        pair = dot(rows_joined(first, late, 1, j, rows), both(kernel, j, 1, 0))
        acc[j, 0] = pair[:, :c]
        acc[j, 1] = pair[:, c:]
        if j == 0:
            split_earlier(late, 0, earlier, cached)
    for j in range(4):
        if j < rows:
            finish(1, j)
        acc[j, 0] += dot(rows_joined(first, late, 0, j, rows), taps_of(kernel, j, 0))
    for r in range(rows):
        finish(0, r)


def on_device(
    latent, cache_lat, cache_one, cache_two, w_in, b_in, gain_one, w_one, b_one, gain_two, w_two, b_two
):
    frames, rows, width, chan = latent.shape
    c = w_in.shape[-1]
    half = width // 2
    part_rows = (rows + 2) // 2
    tiles = (lax.axis_size("tile"), rows * lax.axis_size("tile"))

    def flat(x):
        return x.reshape(-1, width)

    def row(x):
        return x.reshape(1, c)

    def cost(gflop):
        return pl.CostEstimate(flops=int(gflop * 1e9), bytes_accessed=int(gflop * 1e6), transcendentals=0)

    own = flat(jnp.swapaxes(latent, 2, 3))
    prev1 = shifted(own, "tm", 1)
    prev2 = shifted(own, "tm", 2)
    prev1, prev2, to_dn, to_up = border_rows(
        chan, own, prev1, prev2, flat(jnp.swapaxes(cache_lat, 2, 3))
    )
    up = shifted(to_dn, "tile", 1)
    dn = shifted(to_up, "tile", -1)
    caches = jnp.concatenate([cache_one[:, rows - 2 :], cache_two[:, rows - 1 :]], 1)
    cache_up = first_frames_only(caches, 1)
    caches = jnp.concatenate([cache_one[:, :2], cache_two[:, :1]], 1)
    cache_dn = first_frames_only(caches, -1)

    normed_part = jax.ShapeDtypeStruct((2, part_rows, width, c), BF)
    filtered_shape = (4, rows + 4, half, c)
    w1 = w_one.reshape(9, 3, c, c)
    w2 = w_two.reshape(9, 3, c, c)
    u1 = summed_kernels(w1)
    n2a, *v1, h0 = pl.pallas_call(
        functools.partial(first_conv_body, tiles),
        out_shape=[
            normed_part,
            *[jax.ShapeDtypeStruct(filtered_shape, BF)] * 4,
            jax.ShapeDtypeStruct((2, rows, width, c), BF),
        ],
        in_specs=in_vmem(15),
        out_specs=in_vmem(6),
        scratch_shapes=[
            VMEM((6, (rows + 6) * 4 * chan, width), BF),
            VMEM((6 * width, (rows + 6) * 4 * chan), BF),
            VMEM((48 * chan, 2 * c), BF),
            VMEM(((rows + 4) // 2, 4 * width, 2 * c), BF),
            VMEM((2, rows + 4, width, c), BF),
            VMEM((4, 2, part_rows * half, c), F32),
        ],
        compiler_params=limit(21),
        name="first_conv",
        cost_estimate=cost(8),
    )(
        own, prev1, prev2, up, dn, cache_one, cache_up, cache_dn,
        w_in.reshape(-1, c), row(b_in), row(gain_one), w1, u1, row(b_one), row(gain_two),
    )
    earlier_a = shifted(n2a, "tm", 1)
    n2b = pl.pallas_call(
        functools.partial(second_part_body, tiles),
        out_shape=normed_part,
        in_specs=in_vmem(8),
        out_specs=in_vmem(1)[0],
        scratch_shapes=[VMEM((4, 2, part_rows * half, c), F32)],
        compiler_params=limit(20),
        name="second_part",
        cost_estimate=cost(0.2),
    )(*v1, w1, u1, row(b_one), row(gain_two))
    earlier_b = shifted(n2b, "tm", 1)
    filtered_part = jax.ShapeDtypeStruct((4, part_rows, half, c), BF)
    part, u2, *ve = pl.pallas_call(
        own_frames_body,
        out_shape=[
            jax.ShapeDtypeStruct((2, rows, width, c), F32),
            jax.ShapeDtypeStruct((2, 9, c, c), BF),
            filtered_part,
            filtered_part,
        ],
        in_specs=in_vmem(8),
        out_specs=in_vmem(4),
        scratch_shapes=[
            VMEM((2, part_rows, width, c), BF),
            VMEM((2, 4, rows + 2, half, c), BF),
            VMEM((4, 2, rows * half, c), F32),
        ],
        compiler_params=limit(20),
        name="own_frames",
        cost_estimate=cost(4),
    )(n2a, n2b, earlier_a, cache_two, cache_up, w2, h0, row(b_two))
    return pl.pallas_call(
        earlier_frames_body,
        out_shape=jax.ShapeDtypeStruct((2, rows, width, c), BF),
        in_specs=in_vmem(8),
        out_specs=in_vmem(1)[0],
        scratch_shapes=[
            VMEM((2, part_rows, width, c), BF),
            VMEM((2, 4, part_rows, half, c), BF),
            VMEM((4, 2, rows * half, c), F32),
        ],
        compiler_params=limit(20),
        name="earlier_frames",
        cost_estimate=cost(4),
    )(*ve, earlier_b, cache_two, cache_dn, w2, u2, part)


def solution(mesh):
    return jax.shard_map(
        on_device,
        mesh=mesh,
        in_specs=(
            P("tm", "tile", None, None),
            P(None, "tile", None, None),
            P(None, "tile", None, None),
            P(None, "tile", None, None),
            P(),
            P(),
            P(),
            P(),
            P(),
            P(),
            P(),
            P(),
        ),
        out_specs=P("tm", "tile", None, None),
        check_vma=False,
    )
```

time: 68.9 us -> 58 us (0.84)
  the two profiles are of different devices: /device:TPU:20 before, /device:TPU:0 now
where the time goes in v3:
time: 58 us; the launch traced here: 57.7 us
  Pallas kernels  30.4 us (52%)
  starting transfers between devices  20.5 us (35%)
  waiting for transfers between devices  3.8 us (7%)
  local copies, waits for them, and re-layouts  2.38 us (4%)
    ppermute x6, starting transfers between devices, shifted(): lax.ppermute(x, axis, [(i, i + by) for i in range(count) if 0 <= i + by <...  15.7 us
    pallas_call x1, Pallas kernels, on_device(): pl.pallas_call(functools.partial(first_conv_body, tiles), out_shape=[norm...  11.6 us
    pallas_call x1, Pallas kernels, on_device(): pl.pallas_call(own_frames_body, out_shape=[jax.ShapeDtypeStruct((2, rows,...  6.25 us
    pallas_call x1, Pallas kernels, on_device(): pl.pallas_call(earlier_frames_body, out_shape=jax.ShapeDtypeStruct((2, ro...  5.52 us
    pallas_call x1, Pallas kernels, on_device(): pl.pallas_call(functools.partial(second_part_body, tiles), out_shape=norm...  5.2 us
    ppermute x2, starting transfers between devices, first_frames_only(): lax.ppermute(x, ('tm', 'tile'), [(i, i + by) for i in range(rows) if 0 <=...  4.81 us
    ppermute x6, waiting for transfers between devices, shifted(): lax.ppermute(x, axis, [(i, i + by) for i in range(count) if 0 <= i + by <...  3.79 us
    slice x2, local copies, waits for them, and re-layouts, on_device(): caches = jnp.concatenate([cache_one[:, :2], cache_two[:, :1]], 1)  2.27 us
  transfers between devices with their start and end apart: 8, of which 1 were waited for; matrix products, arithmetic and copies ran while one was open for 4% of the time, Pallas kernels for 23%

profile of v3, /device:TPU:0, one launch (start us, length us, event | category | flops | bytes accessed | tf_op | source)
XLA Modules:
  0.0 57.7 jit_solution(16580869411730032866)
XLA Ops:
  0.0 2.3 %collective-permute-start = (bf16[128,128]{1,0:T(8,128)(2,1)}, bf16[128,128]{1,0:T(8,128)(2,1)S(1)}, u32[]{:S(2)}, u32[]{:S(2)}) collective-permute-start(bf16[128,128]{1,0:T(8,128)(2,1)} %bitcast.20), channel_id=1, source_target_pairs={{0,4},{4,8},{8,12},{12,16},{16,20},{20,24},{24,28},{1,5},{5,9},{9,... | collective-permute-start | bytes 98312 | tf_op jit(solution)/shard_map/ppermute | solution.py:17
  2.4 4.4 %collective-permute-start.1 = (bf16[128,128]{1,0:T(8,128)(2,1)}, bf16[128,128]{1,0:T(8,128)(2,1)S(1)}, u32[]{:S(2)}, u32[]{:S(2)}) collective-permute-start(bf16[128,128]{1,0:T(8,128)(2,1)} %bitcast.21), channel_id=1, source_target_pairs={{0,8},{4,12},{8,16},{12,20},{16,24},{20,28},{1,9},{5,13},{9,17},{1... | collective-permute-start | bytes 98312 | tf_op jit(solution)/shard_map/ppermute | solution.py:17
  6.8 1.1 %fusion.1 = (bf16[2,1,128,384]{3,2,1,0:T(8,128)(2,1)S(1)}, bf16[2,1,128,384]{3,2,1,0:T(8,128)(2,1)S(1)}) fusion(bf16[2,4,128,384]{3,2,1,0:T(8,128)(2,1)} %cache_two.3), kind=kLoop, calls=%fused_computation.3 | loop fusion | bytes 786432 | tf_op jit(solution)/shard_map/slice | solution.py:456
  7.8 1.2 %fusion = (bf16[2,2,128,384]{3,2,1,0:T(8,128)(2,1)S(1)}, bf16[2,2,128,384]{3,2,1,0:T(8,128)(2,1)S(1)}) fusion(bf16[2,4,128,384]{3,2,1,0:T(8,128)(2,1)} %cache_one.1), kind=kLoop, calls=%fused_computation.2 | loop fusion | bytes 1572864 | tf_op jit(solution)/shard_map/slice | solution.py:456
  9.1 0.0 copy-start.3
  9.1 0.0 copy-start.4
  9.1 0.1 pad_maximum_fusion
  9.2 3.5 %collective-permute-start.4 = (bf16[2,3,128,384]{3,2,1,0:T(8,128)(2,1)S(1)}, bf16[2,3,128,384]{3,2,1,0:T(8,128)(2,1)S(1)}, u32[]{:S(2)}, u32[]{:S(2)}) collective-permute-start(bf16[2,3,128,384]{3,2,1,0:T(8,128)(2,1)S(1)} %pad_maximum_fusion), channel_id=1, source_target_pairs={{0,1},{1,2},{2,3}} | collective-permute-start | bytes 1769480 | tf_op jit(solution)/shard_map/ppermute | solution.py:22
  12.7 0.1 pad_maximum_fusion.1
  12.8 1.3 %collective-permute-start.5 = (bf16[2,3,128,384]{3,2,1,0:T(8,128)(2,1)S(1)}, bf16[2,3,128,384]{3,2,1,0:T(8,128)(2,1)S(1)}, u32[]{:S(2)}, u32[]{:S(2)}) collective-permute-start(bf16[2,3,128,384]{3,2,1,0:T(8,128)(2,1)S(1)} %pad_maximum_fusion.1), channel_id=1, source_target_pairs={{1,0},{2,1},{3,2}} | collective-permute-start | bytes 1769480 | tf_op jit(solution)/shard_map/ppermute | solution.py:22
  14.1 0.0 collective-permute-done.1.prev2
  14.1 0.0 slice-start
  14.1 0.0 copy-start.5
  14.1 0.0 copy-start.6
  14.1 0.0 copy-start.7
  14.2 0.0 copy-start.8
  14.2 4.8 %collective-permute-start.2 = (bf16[288,128]{1,0:T(8,128)(2,1)S(1)}, bf16[288,128]{1,0:T(8,128)(2,1)S(1)}, u32[]{:S(2)}, u32[]{:S(2)}) collective-permute-start(bf16[288,128]{1,0:T(8,128)(2,1)S(1)} %get-tuple-element.21), channel_id=1, source_target_pairs={{0,1},{1,2},{2,3},{4,5},{5,6},{6,7},{8,9},{9,10},{10,11},{12,13},{... | collective-permute-start | bytes 221192 | tf_op jit(solution)/shard_map/ppermute | solution.py:17
  19.0 1.3 %collective-permute-start.3 = (bf16[288,128]{1,0:T(8,128)(2,1)S(1)}, bf16[288,128]{1,0:T(8,128)(2,1)S(1)}, u32[]{:S(2)}, u32[]{:S(2)}) collective-permute-start(bf16[288,128]{1,0:T(8,128)(2,1)S(1)} %get-tuple-element.22), channel_id=1, source_target_pairs={{1,0},{2,1},{3,2},{5,4},{6,5},{7,6},{9,8},{10,9},{11,10},{13,12},{... | collective-permute-start | bytes 221192 | tf_op jit(solution)/shard_map/ppermute | solution.py:17
  20.5 0.0 copy-start.1
  20.5 0.0 copy-start.2
  20.5 0.0 slice-start.2
  20.5 1.8 %summed_kernels.1.u = bf16[2,9,384,384]{3,2,1,0:T(8,128)(2,1)S(1)} custom-call(bf16[9,3,384,384]{3,2,1,0:T(8,128)(2,1)S(1)} %bitcast.11), custom_call_target="tpu_custom_call" | custom-call | flops 7962624 | bytes 13271040 | tf_op jit(solution)/shard_map/summed_kernels/pallas_call | solution.py:115
  22.3 3.8 %collective-permute-done.3.dn = bf16[288,128]{1,0:T(8,128)(2,1)S(1)} collective-permute-done((bf16[288,128]{1,0:T(8,128)(2,1)S(1)}, bf16[288,128]{1,0:T(8,128)(2,1)S(1)}, u32[]{:S(2)}, u32[]{:S(2)}) %collective-permute-start.3) | collective-permute-done | bytes 73760 | tf_op jit(solution)/shard_map/ppermute | solution.py:17
  26.1 0.0 slice-start.3
  26.2 11.6 %first_conv.1 = (bf16[2,3,128,384]{3,2,1,0:T(8,128)(2,1)S(1)}, bf16[4,8,64,384]{3,2,1,0:T(8,128)(2,1)S(1)}, bf16[4,8,64,384]{3,2,1,0:T(8,128)(2,1)S(1)}, bf16[4,...) custom-call(bf16[128,128]{1,0:T(8,128)(2,1)S(1)} %bitcast.23, ...), custom_call_target="tpu_custom_call" | custom-call | flops 8000000000 | bytes 8000000 | tf_op jit(solution)/shard_map/first_conv/pallas_call | solution.py:464
  37.8 1.5 %collective-permute-start.6 = (bf16[2,3,128,384]{3,2,1,0:T(8,128)(2,1)S(1)}, bf16[2,3,128,384]{3,2,1,0:T(8,128)(2,1)S(1)}, u32[]{:S(2)}, u32[]{:S(2)}) collective-permute-start(bf16[2,3,128,384]{3,2,1,0:T(8,128)(2,1)S(1)} %get-tuple-element.23.n2a), channel_id=1, source_target_pairs={{0,4},{4,8},{8,12},{12,16},{16,20},{20,24},{24,28},{1,5},{5,9},{9,... | collective-permute-start | bytes 1769480 | tf_op jit(solution)/shard_map/ppermute | solution.py:17
  39.3 0.0 copy-start.9
  39.3 0.0 copy-start
  39.3 5.2 %second_part.1.n2b = bf16[2,3,128,384]{3,2,1,0:T(8,128)(2,1)S(1)} custom-call(bf16[4,8,64,384]{3,2,1,0:T(8,128)(2,1)S(1)} %get-tuple-element.24.v0, bf16[4,8,64,384]{3,2,1,0:T(8,128)(2,1)S(1)} %get-tuple-element.25.v1, bf16[4,8,64,384]{3,2,1,0:T(8,128)(2,1)S(1)} %get-tuple-element.26.v2, bf16[4,8,64,384]{3,2,1,0:T(8,128)(2,1)S(1)} %get-tuple-element.27.v3, ...), custom_call_target="tpu_custom_call" | custom-call | flops 200000000 | bytes 200000 | tf_op jit(solution)/shard_map/second_part/pallas_call | solution.py:489
  44.5 1.3 %collective-permute-start.7 = (bf16[2,3,128,384]{3,2,1,0:T(8,128)(2,1)S(1)}, bf16[2,3,128,384]{3,2,1,0:T(8,128)(2,1)S(1)}, u32[]{:S(2)}, u32[]{:S(2)}) collective-permute-start(bf16[2,3,128,384]{3,2,1,0:T(8,128)(2,1)S(1)} %second_part.1.n2b), channel_id=1, source_target_pairs={{0,4},{4,8},{8,12},{12,16},{16,20},{20,24},{24,28},{1,5},{5,9},{9,... | collective-permute-start | bytes 1769480 | tf_op jit(solution)/shard_map/ppermute | solution.py:17
  45.9 6.2 %own_frames.1 = (f32[2,4,128,384]{3,2,1,0:T(8,128)S(1)}, bf16[2,9,384,384]{3,2,1,0:T(8,128)(2,1)S(1)}, bf16[4,3,64,384]{3,2,1,0:T(8,128)(2,1)S(1)}, bf16[4,3,64,384]{3,2,1,0:T(8,128)(2,1)S(1)}) custom-call(bf16[2,3,128,384]{3,2,1,0:T(8,128)(2,1)S(1)} %get-tuple-element.23.n2a, bf16[2,3,128,384]{3,2,1,0:T(8,128)(2,1)S(1)} %second_part.1.n2b, ...), custom_call_target="tpu_custom_call" | custom-call | flops 4000000000 | bytes 4000000 | tf_op jit(solution)/shard_map/own_frames/pallas_call | solution.py:501
  52.2 5.5 %earlier_frames.1 = bf16[2,4,128,384]{3,2,1,0:T(8,128)(2,1)} custom-call(bf16[4,3,64,384]{3,2,1,0:T(8,128)(2,1)S(1)} %get-tuple-element.29.ve0, bf16[4,3,64,384]{3,2,1,0:T(8,128)(2,1)S(1)} %get-tuple-element.30.ve1, bf16[2,3,128,384]{3,2,1,0:T(8,128)(2,1)S(1)} %collective-permute-done.7.earlier, bf16[2,4,128,384]{3,2,1,0:T(8,128)(2,1)S(1)} %copy-done, ...), custom_call_target="tpu_custom_call" | custom-call | flops 4000000000 | bytes 4000000 | tf_op jit(solution)/shard_map/earlier_frames/pallas_call | solution.py:520
  (29 shorter events, 0.1 us)
Async XLA Ops:
  0.0 14.1 %collective-permute-start = (bf16[128,128]{1,0:T(8,128)(2,1)}, bf16[128,128]{1,0:T(8,128)(2,1)S(1)}, u32[]{:S(2)}, u32[]{:S(2)}) collective-permute-start(bf16[128,128]{1,0:T(8,128)(2,1)} %bitcast.20), channel_id=1, source_target_pairs={{0,4},{4,8},{8,12},{12,16},{16,20},{20,24},{24,28},{1,5},{5,9},{9,... | collective-permute-start | bytes 98312 | tf_op jit(solution)/shard_map/ppermute | solution.py:17
  2.4 11.7 %collective-permute-start.1 = (bf16[128,128]{1,0:T(8,128)(2,1)}, bf16[128,128]{1,0:T(8,128)(2,1)S(1)}, u32[]{:S(2)}, u32[]{:S(2)}) collective-permute-start(bf16[128,128]{1,0:T(8,128)(2,1)} %bitcast.21), channel_id=1, source_target_pairs={{0,8},{4,12},{8,16},{12,20},{16,24},{20,28},{1,9},{5,13},{9,17},{1... | collective-permute-start | bytes 98312 | tf_op jit(solution)/shard_map/ppermute | solution.py:17
  9.1 5.0 %copy-start.3 = (bf16[2,4,128,16]{2,3,1,0:T(8,128)(2,1)S(1)}, bf16[2,4,128,16]{2,3,1,0:T(8,128)(2,1)}, u32[]{:S(2)}) copy-start(bf16[2,4,128,16]{2,3,1,0:T(8,128)(2,1)} %param.13) | copy-start | bytes 98308
  9.1 5.0 %copy-start.4 = (bf16[2,4,128,16]{2,3,1,0:T(8,128)(2,1)S(1)}, bf16[2,4,128,16]{2,3,1,0:T(8,128)(2,1)}, u32[]{:S(2)}) copy-start(bf16[2,4,128,16]{2,3,1,0:T(8,128)(2,1)} %param.12) | copy-start | bytes 98308
  9.2 17.0 %collective-permute-start.4 = (bf16[2,3,128,384]{3,2,1,0:T(8,128)(2,1)S(1)}, bf16[2,3,128,384]{3,2,1,0:T(8,128)(2,1)S(1)}, u32[]{:S(2)}, u32[]{:S(2)}) collective-permute-start(bf16[2,3,128,384]{3,2,1,0:T(8,128)(2,1)S(1)} %pad_maximum_fusion), channel_id=1, source_target_pairs={{0,1},{1,2},{2,3}} | collective-permute-start | bytes 1769480 | tf_op jit(solution)/shard_map/ppermute | solution.py:22
  12.8 13.4 %collective-permute-start.5 = (bf16[2,3,128,384]{3,2,1,0:T(8,128)(2,1)S(1)}, bf16[2,3,128,384]{3,2,1,0:T(8,128)(2,1)S(1)}, u32[]{:S(2)}, u32[]{:S(2)}) collective-permute-start(bf16[2,3,128,384]{3,2,1,0:T(8,128)(2,1)S(1)} %pad_maximum_fusion.1), channel_id=1, source_target_pairs={{1,0},{2,1},{3,2}} | collective-permute-start | bytes 1769480 | tf_op jit(solution)/shard_map/ppermute | solution.py:22
  14.1 6.3 %slice-start = ((s8[7962624]{0:T(1024)(128)(4,1)}), s8[4194304]{0:T(1024)(128)(4,1)S(1)}, s32[]{:S(2)}) async-start(s8[7962624]{0:T(1024)(128)(4,1)} %bitcast.9), calls=%async_computation | async-start | bytes 8388608
  14.1 6.2 %copy-start.5 = (f32[384]{0:T(512)S(1)}, f32[384]{0:T(512)}, u32[]{:S(2)}) copy-start(f32[384]{0:T(512)} %param.17) | copy-start | bytes 4612
  14.1 6.2 %copy-start.6 = (f32[384]{0:T(512)S(1)}, f32[384]{0:T(512)}, u32[]{:S(2)}) copy-start(f32[384]{0:T(512)} %param.18) | copy-start | bytes 4612
  14.1 6.2 %copy-start.7 = (f32[384]{0:T(512)S(1)}, f32[384]{0:T(512)}, u32[]{:S(2)}) copy-start(f32[384]{0:T(512)} %param.20) | copy-start | bytes 4612
  14.2 6.3 %copy-start.8 = (f32[384]{0:T(512)S(1)}, f32[384]{0:T(512)}, u32[]{:S(2)}) copy-start(f32[384]{0:T(512)} %param.21) | copy-start | bytes 4612
  14.2 6.3 %slice-start.1 = ((s8[7962624]{0:T(1024)(128)(4,1)}), s8[3768320]{0:T(1024)(128)(4,1)S(1)}, s32[]{:S(2)}) async-start(s8[7962624]{0:T(1024)(128)(4,1)} %bitcast.9), calls=%async_computation.1 | async-start | bytes 7536640
  14.2 8.1 %collective-permute-start.2 = (bf16[288,128]{1,0:T(8,128)(2,1)S(1)}, bf16[288,128]{1,0:T(8,128)(2,1)S(1)}, u32[]{:S(2)}, u32[]{:S(2)}) collective-permute-start(bf16[288,128]{1,0:T(8,128)(2,1)S(1)} %get-tuple-element.21), channel_id=1, source_target_pairs={{0,1},{1,2},{2,3},{4,5},{5,6},{6,7},{8,9},{9,10},{10,11},{12,13},{... | collective-permute-start | bytes 221192 | tf_op jit(solution)/shard_map/ppermute | solution.py:17
  19.0 7.1 %collective-permute-start.3 = (bf16[288,128]{1,0:T(8,128)(2,1)S(1)}, bf16[288,128]{1,0:T(8,128)(2,1)S(1)}, u32[]{:S(2)}, u32[]{:S(2)}) collective-permute-start(bf16[288,128]{1,0:T(8,128)(2,1)S(1)} %get-tuple-element.22), channel_id=1, source_target_pairs={{1,0},{2,1},{3,2},{5,4},{6,5},{7,6},{9,8},{10,9},{11,10},{13,12},{... | collective-permute-start | bytes 221192 | tf_op jit(solution)/shard_map/ppermute | solution.py:17
  20.5 5.7 %copy-start.1 = (bf16[2,4,128,384]{3,2,1,0:T(8,128)(2,1)S(1)}, bf16[2,4,128,384]{3,2,1,0:T(8,128)(2,1)}, u32[]{:S(2)}) copy-start(bf16[2,4,128,384]{3,2,1,0:T(8,128)(2,1)} %cache_one.1) | copy-start | bytes 2359300
  20.5 5.7 %copy-start.2 = (bf16[3,3,3,16,384]{4,3,2,1,0:T(8,128)(2,1)S(1)}, bf16[3,3,3,16,384]{4,3,2,1,0:T(8,128)(2,1)}, u32[]{:S(2)}) copy-start(bf16[3,3,3,16,384]{4,3,2,1,0:T(8,128)(2,1)} %param.16) | copy-start | bytes 995332
  20.5 25.4 %slice-start.2 = ((s8[7962624]{0:T(1024)(128)(4,1)}), s8[4194304]{0:T(1024)(128)(4,1)S(1)}, s32[]{:S(2)}) async-start(s8[7962624]{0:T(1024)(128)(4,1)} %bitcast.14), calls=%async_computation.2 | async-start | bytes 8388608
  26.1 19.7 %slice-start.3 = ((s8[7962624]{0:T(1024)(128)(4,1)}), s8[3768320]{0:T(1024)(128)(4,1)S(1)}, s32[]{:S(2)}) async-start(s8[7962624]{0:T(1024)(128)(4,1)} %bitcast.14), calls=%async_computation.3 | async-start | bytes 7536640
  37.8 8.1 %collective-permute-start.6 = (bf16[2,3,128,384]{3,2,1,0:T(8,128)(2,1)S(1)}, bf16[2,3,128,384]{3,2,1,0:T(8,128)(2,1)S(1)}, u32[]{:S(2)}, u32[]{:S(2)}) collective-permute-start(bf16[2,3,128,384]{3,2,1,0:T(8,128)(2,1)S(1)} %get-tuple-element.23.n2a), channel_id=1, source_target_pairs={{0,4},{4,8},{8,12},{12,16},{16,20},{20,24},{24,28},{1,5},{5,9},{9,... | collective-permute-start | bytes 1769480 | tf_op jit(solution)/shard_map/ppermute | solution.py:17
  39.3 6.6 %copy-start.9 = (f32[384]{0:T(512)S(1)}, f32[384]{0:T(512)}, u32[]{:S(2)}) copy-start(f32[384]{0:T(512)} %param.23) | copy-start | bytes 4612
  39.3 6.6 %copy-start = (bf16[2,4,128,384]{3,2,1,0:T(8,128)(2,1)S(1)}, bf16[2,4,128,384]{3,2,1,0:T(8,128)(2,1)}, u32[]{:S(2)}) copy-start(bf16[2,4,128,384]{3,2,1,0:T(8,128)(2,1)} %cache_two.3) | copy-start | bytes 2359300
  44.5 7.7 %collective-permute-start.7 = (bf16[2,3,128,384]{3,2,1,0:T(8,128)(2,1)S(1)}, bf16[2,3,128,384]{3,2,1,0:T(8,128)(2,1)S(1)}, u32[]{:S(2)}, u32[]{:S(2)}) collective-permute-start(bf16[2,3,128,384]{3,2,1,0:T(8,128)(2,1)S(1)} %second_part.1.n2b), channel_id=1, source_target_pairs={{0,4},{4,8},{8,12},{12,16},{16,20},{20,24},{24,28},{1,5},{5,9},{9,... | collective-permute-start | bytes 1769480 | tf_op jit(solution)/shard_map/ppermute | solution.py:17

commit v4 on v3

v4 whole, which is shorter than its diff:
```python
import functools

import jax
import jax.numpy as jnp
from jax import lax
from jax.experimental import pallas as pl
from jax.experimental.pallas import tpu as pltpu
from jax.sharding import PartitionSpec as P

BF = jnp.bfloat16
F32 = jnp.float32
VMEM = pltpu.VMEM


def shifted(x, axis, by):
    count = lax.axis_size(axis)
    return lax.ppermute(x, axis, [(i, i + by) for i in range(count) if 0 <= i + by < count])


def first_frames_only(x, by):
    rows = lax.axis_size("tile")
    return lax.ppermute(
        x, ("tm", "tile"), [(i, i + by) for i in range(rows) if 0 <= i + by < rows]
    )


def column_of(place, width):
    half = width // 2
    return jnp.where(place < half, 2 * place, 2 * (place - half) + 1)


def silu_of_twice(h):
    return h + h * jnp.tanh(h)


def rms(v, gain):
    return v * lax.rsqrt(jnp.mean(v * v, -1, keepdims=True) + 1e-6) * gain


def filtered(even, odd):
    half, c = even.shape
    place = lax.broadcasted_iota(jnp.int32, (8, c), 0)
    odd_before = pltpu.roll(odd, 1, 0)
    odd_before = jnp.concatenate([jnp.where(place == 0, 0.0, odd_before[:8]), odd_before[8:]], 0)
    even_after = pltpu.roll(even, half - 1, 0)
    even_after = jnp.concatenate(
        [even_after[: half - 8], jnp.where(place == 7, 0.0, even_after[half - 8 :])], 0
    )
    odd_before, odd = odd_before.astype(BF), odd.astype(BF)
    even, even_after = even.astype(BF), even_after.astype(BF)
    return odd_before - odd, even + odd, odd - even, even - even_after


def dot(a, b):
    return jnp.dot(a, b, preferred_element_type=F32)


def in_vmem(count):
    return [pl.BlockSpec(memory_space=VMEM)] * count


def limit(mib):
    return pltpu.CompilerParams(vmem_limit_bytes=mib << 20)


def places(width, dx, transposed):
    shape = (width, width)
    to = column_of(lax.broadcasted_iota(jnp.int32, shape, 0 if transposed else 1), width)
    at = lax.broadcasted_iota(jnp.int32, shape, 1 if transposed else 0)
    return jnp.where(at == to + (dx - 1), 1.0, 0.0).astype(BF)


def put(v, f, r, row):
    half = row.shape[0] // 2
    parts = filtered(row[:half], row[half:])
    for j in range(4):
        v[f][j, r] = parts[j]


def plain_and_sums(w, u):
    def tap(j, i, columns):
        if j == 0 or j == 3:
            return w[i, 0 if j == 0 else 2, :, columns]
        return u[j - 1, i, :, columns]

    return tap


def taps_of(w, j, dt, columns=slice(None)):
    return jnp.concatenate([w(j, 3 * dt + dy, columns) for dy in range(3)], 0)


def weave(products, vector):
    done = 0
    for n, product in enumerate(products):
        product()
        upto = len(vector) * (n + 1) // len(products)
        for work in vector[done:upto]:
            work()
        done = upto


def pair_pieces(acc, w, j, dts, patches, add=False):
    c = acc.shape[-1]
    n = 2 * c // 3

    def piece(k):
        def product():
            lo, hi = k * n, (k + 1) * n
            kernels = []
            for dt_a, dt_b in dts:
                parts = []
                if lo < c:
                    parts.append(taps_of(w, j, dt_a, slice(lo, min(hi, c))))
                if hi > c:
                    parts.append(taps_of(w, j, dt_b, slice(max(lo, c) - c, hi - c)))
                kernels.append(jnp.concatenate(parts, 1))
            out = dot(patches(), jnp.concatenate(kernels, 0))
            if lo < c:
                acc[j, 0, :, lo : min(hi, c)] = out[:, : min(hi, c) - lo]
            if hi > c:
                here = slice(max(lo, c) - c, hi - c)
                if add:
                    acc[j, 1, :, here] += out[:, max(c - lo, 0) :]
                else:
                    acc[j, 1, :, here] = out[:, max(c - lo, 0) :]

        return product

    return [piece(k) for k in range(3)]


def single(acc, w, j, t, dt, patches, add=True):
    def product():
        out = dot(patches(), taps_of(w, j, dt))
        acc[j, t] = acc[j, t] + out if add else out

    return product


def do(function, *args):
    return lambda: function(*args)


def rows_of(v, f, j, at, rows):
    half, c = v[f].shape[-2:]
    return jnp.concatenate(
        [v[f][j, at + dy : at + dy + rows].reshape(rows * half, c) for dy in range(3)], 1
    )


def rows_joined(first, last, f, j, at, rows):
    half, c = last[f].shape[-2:]
    split = first[f].shape[1]
    out = []
    for dy in range(3):
        start, end = at + dy, at + dy + rows
        if start < split:
            a = first[f][j, start:split].reshape((split - start) * half, c)
            b = last[f][j, 0 : end - split].reshape((end - split) * half, c)
            out.append(jnp.concatenate([a, b], 0))
        else:
            out.append(last[f][j, start - split : end - split].reshape(rows * half, c))
    return jnp.concatenate(out, 1)


def sum_taps(w, u, i):
    s = 0.5 * (w[i, 0].astype(F32) + w[i, 2].astype(F32))
    h = 0.5 * w[i, 1].astype(F32)
    u[0, i] = (s + h).astype(BF)
    u[1, i] = (s - h).astype(BF)


def summed_kernels_body(w, u):
    def tap(i, _):
        sum_taps(w, u, i)
        return 0

    lax.fori_loop(0, w.shape[0], tap, 0)


def summed_kernels(w):
    taps, _, c, o = w.shape
    return pl.pallas_call(
        summed_kernels_body,
        in_specs=in_vmem(1),
        out_specs=in_vmem(1)[0],
        out_shape=jax.ShapeDtypeStruct((2, taps, c, o), BF),
        compiler_params=limit(16),
        name="summed_kernels",
        cost_estimate=pl.CostEstimate(flops=6 * taps * c * o, bytes_accessed=10 * taps * c * o, transcendentals=0),
    )(w)


def border_rows_body(chan, both, prev1, prev2, one, two, to_dn, to_up):
    size = prev1.shape[0]
    own, cache = both.at[0:size], both.at[size : 2 * size]
    tm = lax.axis_index("tm")
    one[...] = jnp.where(tm == 0, cache[...], prev1[...])
    two[...] = jnp.where(tm == 1, cache[...], prev2[...])
    frame = own.shape[0] // 2
    for f, src in enumerate((two, two, one, one, own, own)):
        at = (f % 2) * frame
        to_dn[f * 3 * chan : (f + 1) * 3 * chan] = src[at + frame - 3 * chan : at + frame]
        to_up[f * 3 * chan : (f + 1) * 3 * chan] = src[at : at + 3 * chan]


def border_rows(chan, both, prev1, prev2):
    same = jax.ShapeDtypeStruct(prev1.shape, BF)
    edge = jax.ShapeDtypeStruct((18 * chan, prev1.shape[1]), BF)
    return pl.pallas_call(
        functools.partial(border_rows_body, chan),
        in_specs=in_vmem(3),
        out_specs=in_vmem(4),
        out_shape=[same, same, edge, edge],
        compiler_params=limit(4),
        name="border_rows",
        cost_estimate=pl.CostEstimate(flops=6_000_000_000, bytes_accessed=400_000, transcendentals=0),
    )(both, prev1, prev2)


def finish_norm(tiles, acc, b_one, gain_two, n2_ref, t, r, at):
    half = n2_ref.shape[2] // 2
    rows = pl.ds(r * half, half)
    m = [acc[j, t, rows] for j in range(4)]
    rows_here = lax.axis_index("tile")
    at_row = rows_here * (tiles[1] // tiles[0]) + at + r - 1
    keep = jnp.logical_and(at_row >= 0, at_row < tiles[1])
    gain = jnp.where(keep, 0.5 * gain_two[...], 0.0)
    even = m[0] + m[1] + m[2] + b_one[...]
    odd = m[1] - m[2] - m[3] + b_one[...]
    n2_ref[t, r, 0:half] = silu_of_twice(rms(even, gain)).astype(BF)
    n2_ref[t, r, half:] = silu_of_twice(rms(odd, gain)).astype(BF)


def conv_normed(tiles, patches, w, acc, b_one, gain_two, n2_ref, at, beside_last, beside_pairs):
    rows = n2_ref.shape[1]

    def middle(j):
        return lambda: jnp.concatenate([patches(1, j), patches(2, j)], 1)

    def finish(t):
        return [
            do(finish_norm, tiles, acc, b_one, gain_two, n2_ref, t, r, at) for r in range(rows)
        ]

    weave(
        [single(acc, w, j, 1, 2, do(patches, 3, j), False) for j in range(4)],
        beside_last,
    )
    pairs = []
    for j in range(4):
        pairs += pair_pieces(acc, w, j, ((1, 0), (2, 1)), middle(j), True)
    weave(pairs, beside_pairs)
    weave([single(acc, w, j, 0, 0, do(patches, 0, j)) for j in range(4)], finish(1))
    weave([lambda: None], finish(0))


def normed_row(tiles, gain_one, hs, f, r):
    tile = lax.axis_index("tile")
    width, c = hs.shape[1] // 4, hs.shape[2] // 2
    rows = tiles[1] // tiles[0]
    p, k = r // 2, r % 2
    h0 = hs[p, f * width : (f + 1) * width, k * c : (k + 1) * c]
    at_row = tile * rows + r - 2
    keep = jnp.logical_and(at_row >= 0, at_row < tiles[1])
    gain = jnp.where(keep, 0.5 * gain_one[...], 0.0)
    return h0, silu_of_twice(rms(h0.astype(F32), gain))


def projection_body(
    tiles,
    both, prev1, prev2, up, dn, w_in, b_in, gain_one,
    hs, v2, v3, h0_ref,
    lats, g, w_big,
):
    own = both.at[0 : prev1.shape[0]]
    v = (None, None, v2, v3)
    width = own.shape[-1]
    c = w_in.shape[1]
    chan = w_in.shape[0] // 27
    rows = own.shape[0] // (2 * chan)
    rows1 = rows + 4
    slot = 4 * chan

    lats[...] = jnp.zeros_like(lats)
    place = jnp.concatenate([places(width, dx, False) for dx in range(3)], 1)

    def lay(block, f0, r0, count):
        moved = dot(block, place).astype(BF)
        for i in range(block.shape[0] // chan):
            f, r = f0 + i // count, r0 + i % count
            for dx in range(3):
                lats[f, r * slot + dx * chan : r * slot + (dx + 1) * chan] = moved[
                    i * chan : (i + 1) * chan, dx * width : (dx + 1) * width
                ]

    lay(up[...], 0, 0, 3)
    lay(prev2[...], 0, 3, rows)
    lay(prev1[...], 2, 3, rows)
    lay(own[...], 4, 3, rows)
    lay(dn[...], 0, 3 + rows, 3)
    eye = jnp.where(
        lax.broadcasted_iota(jnp.int32, (width, width), 0)
        == lax.broadcasted_iota(jnp.int32, (width, width), 1),
        1.0,
        0.0,
    ).astype(BF)
    for f in range(6):
        g[f * width : (f + 1) * width] = lax.dot_general(
            eye, lats[f], (((1,), (1,)), ((), ())), preferred_element_type=F32
        ).astype(BF)

    w_big[...] = jnp.zeros_like(w_big)
    for dt in range(3):
        for dy in range(3):
            taps = w_in[(3 * dt + dy) * 3 * chan : (3 * dt + dy + 1) * 3 * chan]
            for k in range(2):
                start = (4 * dt + dy + k) * slot
                w_big[start : start + 3 * chan, k * c : (k + 1) * c] = taps
    bias = jnp.concatenate([b_in[...], b_in[...]], 1)

    columns = 2 * c // 3

    def project(p):
        def piece(k):
            def product():
                patches = jnp.concatenate(
                    [
                        g[dt * width : (dt + 4) * width, 2 * p * slot : (2 * p + 4) * slot]
                        for dt in range(3)
                    ],
                    1,
                )
                here = slice(k * columns, (k + 1) * columns)
                hs[p, :, here] = (dot(patches, w_big[:, here]) + bias[:, here]).astype(BF)

            return product

        return [piece(k) for k in range(3)]

    def normed(f, r):
        h0, n1 = normed_row(tiles, gain_one, hs, f, r)
        if 2 <= r < 2 + rows:
            h0_ref[f - 2, r - 2] = h0
        put(v, f, r, n1)

    def units(p):
        return [do(normed, f, 2 * p + k) for k in range(2) for f in (2, 3)]

    pairs = rows1 // 2
    weave(project(0), [])
    for p in range(pairs):
        weave(project(p + 1) if p + 1 < pairs else [lambda: None], units(p))


def first_cache(cache_one, cache_up, cache_dn, first, count, cached):
    rows = cache_one.shape[1]

    @pl.when(lax.axis_index("tm") == 0)
    def _():
        place = places(cache_one.shape[2], 1, True)
        for f in range(2):
            for i in range(count):
                r = first + i
                if r < 2:
                    row = cache_up[f, r]
                elif r < 2 + rows:
                    row = cache_one[f, r - 2]
                else:
                    row = cache_dn[f, r - 2 - rows]
                cached[f, i] = dot(place, row).astype(BF)


def earlier_units(tiles, gain_one, hs, v, cached, f, first, count):
    at_start = lax.axis_index("tm") == 0

    def normed(i):
        _, n1 = normed_row(tiles, gain_one, hs, f, first + i)
        put(v, f, i, jnp.where(at_start, cached[f, i].astype(F32), n1))

    return [do(normed, i) for i in range(count)]


def first_part_body(
    tiles, hs, v2, v3, cache_one, cache_up, gain_one, w, u, b_one, gain_two,
    n2_ref, v0, v1,
    cached, acc,
):
    v = (v0, v1, v2, v3)
    rows = n2_ref.shape[1]
    needed = rows + 2
    first_cache(cache_one, cache_up, None, 0, needed, cached)

    def units(f):
        return earlier_units(tiles, gain_one, hs, v, cached, f, 0, needed)

    conv_normed(
        tiles, lambda f, j: rows_of(v, f, j, 0, rows), plain_and_sums(w, u), acc, b_one,
        gain_two, n2_ref, 0, units(1), units(0),
    )


def second_part_body(
    tiles, hs, v0, v1, v2, v3, cache_one, cache_dn, gain_one, w, u, b_one, gain_two,
    n2_ref, cached, late, acc,
):
    rows = n2_ref.shape[1]
    there = v0.shape[1]
    early, late, own = (v0, v1), (late.at[0], late.at[1]), (None, None, v2, v3)
    first_cache(cache_one, None, cache_dn, there, rows, cached)

    def patches(f, j):
        if f < 2:
            return rows_joined(early, late, f, j, rows, rows)
        return rows_of(own, f, j, rows, rows)

    def units(f):
        return earlier_units(tiles, gain_one, hs, late, cached, f, there, rows)

    conv_normed(
        tiles, patches, plain_and_sums(w, u), acc, b_one, gain_two, n2_ref, rows,
        units(1), units(0),
    )


def cached_rows(cache_two, cache_up, cache_dn, first, count, cached):
    rows = cache_two.shape[1]

    @pl.when(lax.axis_index("tm") == 0)
    def _():
        place = places(cache_two.shape[2], 1, True)
        for f in range(2):
            for i in range(count):
                r = first + i
                if r < 1:
                    row = cache_up[f, 2]
                elif r < 1 + rows:
                    row = cache_two[f, r - 1]
                else:
                    row = cache_dn[f, 2]
                cached[f, i] = dot(place, row).astype(BF)


def split_earlier(v, f, earlier, cached):
    at_start = lax.axis_index("tm") == 0

    def split(r):
        row = jnp.where(at_start, cached[f, r].astype(F32), earlier[f, r].astype(F32))
        put(v, f, r, row)

    return [do(split, r) for r in range(earlier.shape[1])]


def halves(first, second):
    return [(first, r) for r in range(first.shape[1])] + [(second, r) for r in range(second.shape[1])]


def own_frames_body(
    n2a, n2b, earlier, cache_two, cache_up, w, u, h0, b_two,
    part_ref, ve0, ve1,
    cached, v, acc,
):
    width, c = n2a.shape[2:]
    half = width // 2
    rows = part_ref.shape[1]
    source = halves(n2a, n2b)
    v = (v.at[0], v.at[1])
    cached_rows(cache_two, cache_up, None, 0, n2a.shape[1], cached)

    def split(f):
        return [
            do(lambda r, ref, at: put(v, f, r, ref[f, at].astype(F32)), r, ref, at)
            for r, (ref, at) in enumerate(source)
        ]

    def finish(t, r):
        m = [acc[j, t, r * half : (r + 1) * half] for j in range(4)]
        even = m[0] + m[1] + m[2] + b_two[...]
        odd = m[1] - m[2] - m[3] + b_two[...]
        part_ref[t, r, 0:half] = even + h0[t, r, 0:half].astype(F32)
        part_ref[t, r, half:] = odd + h0[t, r, half:].astype(F32)

    kernel = plain_and_sums(w, u)

    def pair(j):
        return pair_pieces(acc, kernel, j, ((2, 1),), do(rows_of, v, 0, j, 0, rows))

    def other(j):
        return single(acc, kernel, j, 1, 2, do(rows_of, v, 1, j, 0, rows))

    ve = (ve0, ve1)
    weave([lambda: None], split(0))
    weave(pair(0) + pair(1), split(1))
    weave(
        pair(2) + pair(3),
        split_earlier(ve, 0, earlier, cached) + split_earlier(ve, 1, earlier, cached),
    )
    weave([other(j) for j in range(4)], [do(finish, 0, r) for r in range(rows)])
    weave([lambda: None], [do(finish, 1, r) for r in range(rows)])


def earlier_frames_body(
    ve0, ve1, earlier, cache_two, cache_dn, w, u, part, out_ref, cached, late, acc
):
    width, c = earlier.shape[2:]
    half = width // 2
    rows = out_ref.shape[1]
    kernel = plain_and_sums(w, u)
    first = (ve0, ve1)
    late = (late.at[0], late.at[1])
    cached_rows(cache_two, None, cache_dn, ve0.shape[1], earlier.shape[1], cached)
    back = places(width, 1, False)

    def finish(t, r):
        m = [acc[j, t, r * half : (r + 1) * half] for j in range(4)]
        even = part[t, r, 0:half] + m[0] + m[1] + m[2]
        odd = part[t, r, half:] + m[1] - m[2] - m[3]
        out_ref[t, r] = dot(back, jnp.concatenate([even, odd], 0).astype(BF)).astype(BF)

    weave([lambda: None], split_earlier(late, 1, earlier, cached))
    pairs = []
    for j in range(4):
        pairs += pair_pieces(acc, kernel, j, ((1, 0),), do(rows_joined, first, late, 1, j, 0, rows))
    weave(pairs, split_earlier(late, 0, earlier, cached))
    weave(
        [single(acc, kernel, j, 0, 0, do(rows_joined, first, late, 0, j, 0, rows)) for j in range(4)],
        [do(finish, 1, r) for r in range(rows)],
    )
    weave([lambda: None], [do(finish, 0, r) for r in range(rows)])


def on_device(
    latent, cache_lat, cache_one, cache_two, w_in, b_in, gain_one, w_one, b_one, gain_two, w_two, b_two
):
    frames, rows, width, chan = latent.shape
    c = w_in.shape[-1]
    half = width // 2
    part_rows = (rows + 2) // 2
    tiles = (lax.axis_size("tile"), rows * lax.axis_size("tile"))

    def flat(x):
        return x.reshape(-1, width)

    def row(x):
        return x.reshape(1, c)

    def cost(gflop):
        return pl.CostEstimate(flops=int(gflop * 1e9), bytes_accessed=int(gflop * 1e6), transcendentals=0)

    own = flat(jnp.swapaxes(latent, 2, 3))
    prev1 = shifted(own, "tm", 1)
    prev2 = shifted(own, "tm", 2)
    own_and_cache = jnp.concatenate([own, flat(jnp.swapaxes(cache_lat, 2, 3))], 0)
    prev1, prev2, to_dn, to_up = border_rows(chan, own_and_cache, prev1, prev2)
    up = shifted(to_dn, "tile", 1)
    dn = shifted(to_up, "tile", -1)
    caches = jnp.concatenate([cache_one[:, rows - 2 :], cache_two[:, rows - 1 :]], 1)
    cache_up = first_frames_only(caches, 1)
    caches = jnp.concatenate([cache_one[:, :2], cache_two[:, :1]], 1)
    cache_dn = first_frames_only(caches, -1)

    normed_part = jax.ShapeDtypeStruct((2, part_rows, width, c), BF)
    w1 = w_one.reshape(9, 3, c, c)
    w2 = w_two.reshape(9, 3, c, c)
    u1 = summed_kernels(w1)
    u2 = summed_kernels(w2)
    filtered = jax.ShapeDtypeStruct((4, rows + 4, half, c), BF)
    hs, *v_own, h0 = pl.pallas_call(
        functools.partial(projection_body, tiles),
        out_shape=[
            jax.ShapeDtypeStruct(((rows + 4) // 2, 4 * width, 2 * c), BF),
            filtered,
            filtered,
            jax.ShapeDtypeStruct((2, rows, width, c), BF),
        ],
        in_specs=in_vmem(8),
        out_specs=in_vmem(4),
        scratch_shapes=[
            VMEM((6, (rows + 6) * 4 * chan, width), BF),
            VMEM((6 * width, (rows + 6) * 4 * chan), BF),
            VMEM((48 * chan, 2 * c), BF),
        ],
        compiler_params=limit(16),
        name="projection",
        cost_estimate=cost(6),
    )(own_and_cache, prev1, prev2, up, dn, w_in.reshape(-1, c), row(b_in), row(gain_one))
    n2a, *v_earlier = pl.pallas_call(
        functools.partial(first_part_body, tiles),
        out_shape=[normed_part, *[jax.ShapeDtypeStruct((4, part_rows + 2, half, c), BF)] * 2],
        in_specs=in_vmem(10),
        out_specs=in_vmem(3),
        scratch_shapes=[
            VMEM((2, part_rows + 2, width, c), BF),
            VMEM((4, 2, part_rows * half, c), F32),
        ],
        compiler_params=limit(20),
        name="first_part",
        cost_estimate=cost(8),
    )(
        hs, *v_own, cache_one, cache_up, row(gain_one),
        w1, u1, row(b_one), row(gain_two),
    )
    earlier_a = shifted(n2a, "tm", 1)
    n2b = pl.pallas_call(
        functools.partial(second_part_body, tiles),
        out_shape=normed_part,
        in_specs=in_vmem(12),
        out_specs=in_vmem(1)[0],
        scratch_shapes=[
            VMEM((2, part_rows, width, c), BF),
            VMEM((2, 4, part_rows, half, c), BF),
            VMEM((4, 2, part_rows * half, c), F32),
        ],
        compiler_params=limit(20),
        name="second_part",
        cost_estimate=cost(0.2),
    )(
        hs, *v_earlier, *v_own, cache_one, cache_dn, row(gain_one),
        w1, u1, row(b_one), row(gain_two),
    )
    earlier_b = shifted(n2b, "tm", 1)
    filtered_part = jax.ShapeDtypeStruct((4, part_rows, half, c), BF)
    part, *ve = pl.pallas_call(
        own_frames_body,
        out_shape=[
            jax.ShapeDtypeStruct((2, rows, width, c), F32),
            filtered_part,
            filtered_part,
        ],
        in_specs=in_vmem(9),
        out_specs=in_vmem(3),
        scratch_shapes=[
            VMEM((2, part_rows, width, c), BF),
            VMEM((2, 4, rows + 2, half, c), BF),
            VMEM((4, 2, rows * half, c), F32),
        ],
        compiler_params=limit(20),
        name="own_frames",
        cost_estimate=cost(4),
    )(n2a, n2b, earlier_a, cache_two, cache_up, w2, u2, h0, row(b_two))
    return pl.pallas_call(
        earlier_frames_body,
        out_shape=jax.ShapeDtypeStruct((2, rows, width, c), BF),
        in_specs=in_vmem(8),
        out_specs=in_vmem(1)[0],
        scratch_shapes=[
            VMEM((2, part_rows, width, c), BF),
            VMEM((2, 4, part_rows, half, c), BF),
            VMEM((4, 2, rows * half, c), F32),
        ],
        compiler_params=limit(20),
        name="earlier_frames",
        cost_estimate=cost(4),
    )(*ve, earlier_b, cache_two, cache_dn, w2, u2, part)


def solution(mesh):
    return jax.shard_map(
        on_device,
        mesh=mesh,
        in_specs=(
            P("tm", "tile", None, None),
            P(None, "tile", None, None),
            P(None, "tile", None, None),
            P(None, "tile", None, None),
            P(),
            P(),
            P(),
            P(),
            P(),
            P(),
            P(),
            P(),
        ),
        out_specs=P("tm", "tile", None, None),
        check_vma=False,
    )
```

time: 58 us -> 54.9 us (0.947)
  waiting for transfers between devices: 3.8 us -> 1.61 us
  starting transfers between devices: 20.5 us -> 19.3 us
  other arithmetic: 0.14 us -> 1.07 us
    ppermute x6, waiting for transfers between devices: 3.79 us -> 1.61 us  [shifted(): lax.ppermute(x, axis, [(i, i + by) for i in range(count) if 0 <= i + by <...]
    pallas_call x1, Pallas kernels: 6.25 us -> 4.23 us  [on_device(): pl.pallas_call(own_frames_body, out_shape=[jax.ShapeDtypeStruct((2, rows,...]
    pallas_call x1 -> x2, Pallas kernels: 1.83 us -> 3.66 us  [summed_kernels(): pl.pallas_call(summed_kernels_body, in_specs=in_vmem(1), out_specs=in_vme...]
    ppermute x6, starting transfers between devices: 15.7 us -> 14.4 us  [shifted(): lax.ppermute(x, axis, [(i, i + by) for i in range(count) if 0 <= i + by <...]
    pallas_call x1 -> x2, Pallas kernels: 11.6 us -> 10.5 us  [the longest x1 6.34 us: on_device(): pl.pallas_call(functools.partial(first_part_body, tiles), out_shape=[norm...]
    concatenate x0 -> x1, other arithmetic: none -> 0.93 us  [on_device(): jnp.concatenate([own, flat(jnp.swapaxes(cache_lat, 2, 3))], 0)]
    pallas_call x1, Pallas kernels: 5.2 us -> 6.12 us  [on_device(): pl.pallas_call(functools.partial(second_part_body, tiles), out_shape=norm...]
  transfers between devices with their start and end apart: 8 -> 8, of which waited for: 1 -> 1; matrix products, arithmetic and copies ran while one was open for 4% -> 6% of each run, Pallas kernels for 23% -> 45%
where the time goes in v4:
time: 54.9 us; the launch traced here: 54.7 us
  Pallas kernels  29.9 us (54%)
  starting transfers between devices  19.3 us (35%)
  local copies, waits for them, and re-layouts  2.36 us (4%)
  waiting for transfers between devices  1.61 us (3%)
  other arithmetic  1.07 us (2%)
    ppermute x6, starting transfers between devices, shifted(): lax.ppermute(x, axis, [(i, i + by) for i in range(count) if 0 <= i + by <...  14.4 us
    pallas_call x1, Pallas kernels, on_device(): pl.pallas_call(functools.partial(first_part_body, tiles), out_shape=[norm...  6.34 us
    pallas_call x1, Pallas kernels, on_device(): pl.pallas_call(functools.partial(second_part_body, tiles), out_shape=norm...  6.12 us
    pallas_call x1, Pallas kernels, on_device(): pl.pallas_call(earlier_frames_body, out_shape=jax.ShapeDtypeStruct((2, ro...  5.4 us
    ppermute x2, starting transfers between devices, first_frames_only(): lax.ppermute(x, ('tm', 'tile'), [(i, i + by) for i in range(rows) if 0 <=...  4.81 us
    pallas_call x1, Pallas kernels, on_device(): pl.pallas_call(own_frames_body, out_shape=[jax.ShapeDtypeStruct((2, rows,...  4.23 us
    pallas_call x1, Pallas kernels, on_device(): pl.pallas_call(functools.partial(projection_body, tiles), out_shape=[jax....  4.15 us
    pallas_call x2, Pallas kernels, summed_kernels(): pl.pallas_call(summed_kernels_body, in_specs=in_vmem(1), out_specs=in_vme...  3.66 us
  transfers between devices with their start and end apart: 8, of which 1 were waited for; matrix products, arithmetic and copies ran while one was open for 6% of the time, Pallas kernels for 45%

profile of v4, /device:TPU:0, one launch (start us, length us, event | category | flops | bytes accessed | tf_op | source)
XLA Modules:
  0.0 54.7 jit_solution(12012313730085431160)
XLA Ops:
  0.0 2.3 %collective-permute-start = (bf16[128,128]{1,0:T(8,128)(2,1)}, bf16[128,128]{1,0:T(8,128)(2,1)S(1)}, u32[]{:S(2)}, u32[]{:S(2)}) collective-permute-start(bf16[128,128]{1,0:T(8,128)(2,1)} %bitcast.21), channel_id=1, source_target_pairs={{0,4},{4,8},{8,12},{12,16},{16,20},{20,24},{24,28},{1,5},{5,9},{9,... | collective-permute-start | bytes 98312 | tf_op jit(solution)/shard_map/ppermute | solution.py:17
  2.4 4.4 %collective-permute-start.1 = (bf16[128,128]{1,0:T(8,128)(2,1)}, bf16[128,128]{1,0:T(8,128)(2,1)S(1)}, u32[]{:S(2)}, u32[]{:S(2)}) collective-permute-start(bf16[128,128]{1,0:T(8,128)(2,1)} %bitcast.22), channel_id=1, source_target_pairs={{0,8},{4,12},{8,16},{12,20},{16,24},{20,28},{1,9},{5,13},{9,17},{1... | collective-permute-start | bytes 98312 | tf_op jit(solution)/shard_map/ppermute | solution.py:17
  6.8 1.1 %fusion.1 = (bf16[2,1,128,384]{3,2,1,0:T(8,128)(2,1)S(1)}, bf16[2,1,128,384]{3,2,1,0:T(8,128)(2,1)S(1)}) fusion(bf16[2,4,128,384]{3,2,1,0:T(8,128)(2,1)} %cache_two.3), kind=kLoop, calls=%fused_computation.4 | loop fusion | bytes 786432 | tf_op jit(solution)/shard_map/slice | solution.py:560
  7.8 1.2 %fusion = (bf16[2,2,128,384]{3,2,1,0:T(8,128)(2,1)S(1)}, bf16[2,2,128,384]{3,2,1,0:T(8,128)(2,1)S(1)}) fusion(bf16[2,4,128,384]{3,2,1,0:T(8,128)(2,1)} %cache_one.3), kind=kLoop, calls=%fused_computation.3 | loop fusion | bytes 1572864 | tf_op jit(solution)/shard_map/slice | solution.py:560
  9.1 0.1 pad_maximum_fusion
  9.1 3.5 %collective-permute-start.4 = (bf16[2,3,128,384]{3,2,1,0:T(8,128)(2,1)S(1)}, bf16[2,3,128,384]{3,2,1,0:T(8,128)(2,1)S(1)}, u32[]{:S(2)}, u32[]{:S(2)}) collective-permute-start(bf16[2,3,128,384]{3,2,1,0:T(8,128)(2,1)S(1)} %pad_maximum_fusion), channel_id=1, source_target_pairs={{0,1},{1,2},{2,3}} | collective-permute-start | bytes 1769480 | tf_op jit(solution)/shard_map/ppermute | solution.py:22
  12.7 0.0 slice-start.2
  12.7 0.9 %pad_maximum_fusion.2.both = bf16[256,128]{1,0:T(8,128)(2,1)S(1)} fusion(bf16[128,128]{1,0:T(8,128)(2,1)} %bitcast.20, bf16[128,128]{1,0:T(8,128)(2,1)} %bitcast.23), kind=kLoop, calls=%fused_computation.2 | loop fusion | flops 131072 | bytes 131072 | tf_op jit(solution)/shard_map/concatenate | solution.py:554
  13.6 0.0 copy-start.5
  13.6 0.0 copy-start.6
  13.6 0.0 slice-start.3
  13.7 0.0 collective-permute-done.1.prev2
  13.7 3.7 %collective-permute-start.2 = (bf16[288,128]{1,0:T(8,128)(2,1)S(1)}, bf16[288,128]{1,0:T(8,128)(2,1)S(1)}, u32[]{:S(2)}, u32[]{:S(2)}) collective-permute-start(bf16[288,128]{1,0:T(8,128)(2,1)S(1)} %get-tuple-element.21), channel_id=1, source_target_pairs={{0,1},{1,2},{2,3},{4,5},{5,6},{6,7},{8,9},{9,10},{10,11},{12,13},{... | collective-permute-start | bytes 221192 | tf_op jit(solution)/shard_map/ppermute | solution.py:17
  17.4 1.3 %collective-permute-start.3 = (bf16[288,128]{1,0:T(8,128)(2,1)S(1)}, bf16[288,128]{1,0:T(8,128)(2,1)S(1)}, u32[]{:S(2)}, u32[]{:S(2)}) collective-permute-start(bf16[288,128]{1,0:T(8,128)(2,1)S(1)} %get-tuple-element.22), channel_id=1, source_target_pairs={{1,0},{2,1},{3,2},{5,4},{6,5},{7,6},{9,8},{10,9},{11,10},{13,12},{... | collective-permute-start | bytes 221192 | tf_op jit(solution)/shard_map/ppermute | solution.py:17
  18.7 0.1 pad_maximum_fusion.1
  18.8 1.3 %collective-permute-start.5 = (bf16[2,3,128,384]{3,2,1,0:T(8,128)(2,1)S(1)}, bf16[2,3,128,384]{3,2,1,0:T(8,128)(2,1)S(1)}, u32[]{:S(2)}, u32[]{:S(2)}) collective-permute-start(bf16[2,3,128,384]{3,2,1,0:T(8,128)(2,1)S(1)} %pad_maximum_fusion.1), channel_id=1, source_target_pairs={{1,0},{2,1},{3,2}} | collective-permute-start | bytes 1769480 | tf_op jit(solution)/shard_map/ppermute | solution.py:22
  20.2 0.0 copy-start.2
  20.2 1.8 %summed_kernels.2.u = bf16[2,9,384,384]{3,2,1,0:T(8,128)(2,1)S(1)} custom-call(bf16[9,3,384,384]{3,2,1,0:T(8,128)(2,1)S(1)} %bitcast.16), custom_call_target="tpu_custom_call" | custom-call | flops 7962624 | bytes 13271040 | tf_op jit(solution)/shard_map/summed_kernels/pallas_call | solution.py:184
  22.1 1.6 %collective-permute-done.3.dn = bf16[288,128]{1,0:T(8,128)(2,1)S(1)} collective-permute-done((bf16[288,128]{1,0:T(8,128)(2,1)S(1)}, bf16[288,128]{1,0:T(8,128)(2,1)S(1)}, u32[]{:S(2)}, u32[]{:S(2)}) %collective-permute-start.3) | collective-permute-done | bytes 73760 | tf_op jit(solution)/shard_map/ppermute | solution.py:17
  23.7 4.2 %projection.1 = (bf16[4,512,768]{2,1,0:T(8,128)(2,1)S(1)}, bf16[4,8,64,384]{3,2,1,0:T(8,128)(2,1)S(1)}, bf16[4,8,64,384]{3,2,1,0:T(8,128)(2,1)S(1)}, bf16[2,4,128,384]{3,2,1,0:T(8,128)(2,1)S(1)}) custom-call(bf16[256,128]{1,0:T(8,128)(2,1)S(1)} %pad_maximum_fusion.2.both, bf16[128,128]{1,0:T(8,128)(2,1)S(1)} %get-tuple-element.19.prev1, ...), custom_call_target="tpu_custom_call" | custom-call | flops 6000000000 | bytes 6000000 | tf_op jit(solution)/shard_map/projection/pallas_call | solution.py:569
  27.9 6.3 %first_part.1 = (bf16[2,3,128,384]{3,2,1,0:T(8,128)(2,1)S(1)}, bf16[4,5,64,384]{3,2,1,0:T(8,128)(2,1)S(1)}, bf16[4,5,64,384]{3,2,1,0:T(8,128)(2,1)S(1)}) custom-call(bf16[4,512,768]{2,1,0:T(8,128)(2,1)S(1)} %get-tuple-element.23.hs, bf16[4,8,64,384]{3,2,1,0:T(8,128)(2,1)S(1)} %get-tuple-element.24.v2, bf16[4,8,64,384]{3,2,1,0:T(8,128)(2,1)S(1)} %get-tuple-element.25.v3, ...), custom_call_target="tpu_custom_call" | custom-call | flops 8000000000 | bytes 8000000 | tf_op jit(solution)/shard_map/first_part/pallas_call | solution.py:588
  34.2 1.3 %collective-permute-start.6 = (bf16[2,3,128,384]{3,2,1,0:T(8,128)(2,1)S(1)}, bf16[2,3,128,384]{3,2,1,0:T(8,128)(2,1)S(1)}, u32[]{:S(2)}, u32[]{:S(2)}) collective-permute-start(bf16[2,3,128,384]{3,2,1,0:T(8,128)(2,1)S(1)} %get-tuple-element.26.n2a), channel_id=1, source_target_pairs={{0,4},{4,8},{8,12},{12,16},{16,20},{20,24},{24,28},{1,5},{5,9},{9,... | collective-permute-start | bytes 1769480 | tf_op jit(solution)/shard_map/ppermute | solution.py:17
  35.6 0.0 slice-start
  35.6 0.0 copy-start.7
  35.6 0.0 slice-start.1
  35.6 6.1 %second_part.1.n2b = bf16[2,3,128,384]{3,2,1,0:T(8,128)(2,1)S(1)} custom-call(bf16[4,512,768]{2,1,0:T(8,128)(2,1)S(1)} %get-tuple-element.23.hs, bf16[4,5,64,384]{3,2,1,0:T(8,128)(2,1)S(1)} %get-tuple-element.27.v0, bf16[4,5,64,384]{3,2,1,0:T(8,128)(2,1)S(1)} %get-tuple-element.28.v1, bf16[4,8,64,384]{3,2,1,0:T(8,128)(2,1)S(1)} %get-tuple-element.24.v2, ...), custom_call_target="tpu_custom_call" | custom-call | flops 200000000 | bytes 200000 | tf_op jit(solution)/shard_map/second_part/pallas_call | solution.py:605
  41.7 1.4 %collective-permute-start.7 = (bf16[2,3,128,384]{3,2,1,0:T(8,128)(2,1)S(1)}, bf16[2,3,128,384]{3,2,1,0:T(8,128)(2,1)S(1)}, u32[]{:S(2)}, u32[]{:S(2)}) collective-permute-start(bf16[2,3,128,384]{3,2,1,0:T(8,128)(2,1)S(1)} %second_part.1.n2b), channel_id=1, source_target_pairs={{0,4},{4,8},{8,12},{12,16},{16,20},{20,24},{24,28},{1,5},{5,9},{9,... | collective-permute-start | bytes 1769480 | tf_op jit(solution)/shard_map/ppermute | solution.py:17
  43.1 0.0 copy-start
  43.2 1.8 %summed_kernels.3.u = bf16[2,9,384,384]{3,2,1,0:T(8,128)(2,1)S(1)} custom-call(bf16[9,3,384,384]{3,2,1,0:T(8,128)(2,1)S(1)} %bitcast.11), custom_call_target="tpu_custom_call" | custom-call | flops 7962624 | bytes 13271040 | tf_op jit(solution)/shard_map/summed_kernels/pallas_call | solution.py:184
  45.0 4.2 %own_frames.1 = (f32[2,4,128,384]{3,2,1,0:T(8,128)S(1)}, bf16[4,3,64,384]{3,2,1,0:T(8,128)(2,1)S(1)}, bf16[4,3,64,384]{3,2,1,0:T(8,128)(2,1)S(1)}) custom-call(bf16[2,3,128,384]{3,2,1,0:T(8,128)(2,1)S(1)} %get-tuple-element.26.n2a, bf16[2,3,128,384]{3,2,1,0:T(8,128)(2,1)S(1)} %second_part.1.n2b, bf16[2,3,128,384]{3,2,1,0:T(8,128)(2,1)S(1)} %collective-permute-done.6.earlier, ...), custom_call_target="tpu_custom_call" | custom-call | flops 4000000000 | bytes 4000000 | tf_op jit(solution)/shard_map/own_frames/pallas_call | solution.py:624
  49.2 0.0 collective-permute-done.7.earlier
  49.3 5.4 %earlier_frames.1 = bf16[2,4,128,384]{3,2,1,0:T(8,128)(2,1)} custom-call(bf16[4,3,64,384]{3,2,1,0:T(8,128)(2,1)S(1)} %get-tuple-element.30.ve0, bf16[4,3,64,384]{3,2,1,0:T(8,128)(2,1)S(1)} %get-tuple-element.31.ve1, bf16[2,3,128,384]{3,2,1,0:T(8,128)(2,1)S(1)} %collective-permute-done.7.earlier, bf16[2,4,128,384]{3,2,1,0:T(8,128)(2,1)S(1)} %copy-done, ...), custom_call_target="tpu_custom_call" | custom-call | flops 4000000000 | bytes 4000000 | tf_op jit(solution)/shard_map/earlier_frames/pallas_call | solution.py:642
  (28 shorter events, 0.1 us)
Async XLA Ops:
  0.0 13.6 %collective-permute-start = (bf16[128,128]{1,0:T(8,128)(2,1)}, bf16[128,128]{1,0:T(8,128)(2,1)S(1)}, u32[]{:S(2)}, u32[]{:S(2)}) collective-permute-start(bf16[128,128]{1,0:T(8,128)(2,1)} %bitcast.21), channel_id=1, source_target_pairs={{0,4},{4,8},{8,12},{12,16},{16,20},{20,24},{24,28},{1,5},{5,9},{9,... | collective-permute-start | bytes 98312 | tf_op jit(solution)/shard_map/ppermute | solution.py:17
  2.4 11.3 %collective-permute-start.1 = (bf16[128,128]{1,0:T(8,128)(2,1)}, bf16[128,128]{1,0:T(8,128)(2,1)S(1)}, u32[]{:S(2)}, u32[]{:S(2)}) collective-permute-start(bf16[128,128]{1,0:T(8,128)(2,1)} %bitcast.22), channel_id=1, source_target_pairs={{0,8},{4,12},{8,16},{12,20},{16,24},{20,28},{1,9},{5,13},{9,17},{1... | collective-permute-start | bytes 98312 | tf_op jit(solution)/shard_map/ppermute | solution.py:17
  9.1 18.7 %collective-permute-start.4 = (bf16[2,3,128,384]{3,2,1,0:T(8,128)(2,1)S(1)}, bf16[2,3,128,384]{3,2,1,0:T(8,128)(2,1)S(1)}, u32[]{:S(2)}, u32[]{:S(2)}) collective-permute-start(bf16[2,3,128,384]{3,2,1,0:T(8,128)(2,1)S(1)} %pad_maximum_fusion), channel_id=1, source_target_pairs={{0,1},{1,2},{2,3}} | collective-permute-start | bytes 1769480 | tf_op jit(solution)/shard_map/ppermute | solution.py:22
  12.7 7.5 %slice-start.2 = ((s8[7962624]{0:T(1024)(128)(4,1)}), s8[4194304]{0:T(1024)(128)(4,1)S(1)}, s32[]{:S(2)}) async-start(s8[7962624]{0:T(1024)(128)(4,1)} %bitcast.14), calls=%async_computation.2 | async-start | bytes 8388608
  13.6 6.5 %copy-start.3 = (f32[384]{0:T(512)S(1)}, f32[384]{0:T(512)}, u32[]{:S(2)}) copy-start(f32[384]{0:T(512)} %param.17) | copy-start | bytes 4612
  13.6 6.5 %copy-start.4 = (f32[384]{0:T(512)S(1)}, f32[384]{0:T(512)}, u32[]{:S(2)}) copy-start(f32[384]{0:T(512)} %param.18) | copy-start | bytes 4612
  13.6 6.5 %copy-start.5 = (f32[384]{0:T(512)S(1)}, f32[384]{0:T(512)}, u32[]{:S(2)}) copy-start(f32[384]{0:T(512)} %param.20) | copy-start | bytes 4612
  13.6 6.6 %copy-start.6 = (f32[384]{0:T(512)S(1)}, f32[384]{0:T(512)}, u32[]{:S(2)}) copy-start(f32[384]{0:T(512)} %param.21) | copy-start | bytes 4612
  13.6 6.6 %slice-start.3 = ((s8[7962624]{0:T(1024)(128)(4,1)}), s8[3768320]{0:T(1024)(128)(4,1)S(1)}, s32[]{:S(2)}) async-start(s8[7962624]{0:T(1024)(128)(4,1)} %bitcast.14), calls=%async_computation.3 | async-start | bytes 7536640
  13.7 8.4 %collective-permute-start.2 = (bf16[288,128]{1,0:T(8,128)(2,1)S(1)}, bf16[288,128]{1,0:T(8,128)(2,1)S(1)}, u32[]{:S(2)}, u32[]{:S(2)}) collective-permute-start(bf16[288,128]{1,0:T(8,128)(2,1)S(1)} %get-tuple-element.21), channel_id=1, source_target_pairs={{0,1},{1,2},{2,3},{4,5},{5,6},{6,7},{8,9},{9,10},{10,11},{12,13},{... | collective-permute-start | bytes 221192 | tf_op jit(solution)/shard_map/ppermute | solution.py:17
  17.4 6.2 %collective-permute-start.3 = (bf16[288,128]{1,0:T(8,128)(2,1)S(1)}, bf16[288,128]{1,0:T(8,128)(2,1)S(1)}, u32[]{:S(2)}, u32[]{:S(2)}) collective-permute-start(bf16[288,128]{1,0:T(8,128)(2,1)S(1)} %get-tuple-element.22), channel_id=1, source_target_pairs={{1,0},{2,1},{3,2},{5,4},{6,5},{7,6},{9,8},{10,9},{11,10},{13,12},{... | collective-permute-start | bytes 221192 | tf_op jit(solution)/shard_map/ppermute | solution.py:17
  18.8 16.7 %collective-permute-start.5 = (bf16[2,3,128,384]{3,2,1,0:T(8,128)(2,1)S(1)}, bf16[2,3,128,384]{3,2,1,0:T(8,128)(2,1)S(1)}, u32[]{:S(2)}, u32[]{:S(2)}) collective-permute-start(bf16[2,3,128,384]{3,2,1,0:T(8,128)(2,1)S(1)} %pad_maximum_fusion.1), channel_id=1, source_target_pairs={{1,0},{2,1},{3,2}} | collective-permute-start | bytes 1769480 | tf_op jit(solution)/shard_map/ppermute | solution.py:22
  20.2 3.5 %copy-start.2 = (bf16[3,3,3,16,384]{4,3,2,1,0:T(8,128)(2,1)S(1)}, bf16[3,3,3,16,384]{4,3,2,1,0:T(8,128)(2,1)}, u32[]{:S(2)}) copy-start(bf16[3,3,3,16,384]{4,3,2,1,0:T(8,128)(2,1)} %param.16) | copy-start | bytes 995332
  23.7 4.2 %copy-start.1 = (bf16[2,4,128,384]{3,2,1,0:T(8,128)(2,1)S(1)}, bf16[2,4,128,384]{3,2,1,0:T(8,128)(2,1)}, u32[]{:S(2)}) copy-start(bf16[2,4,128,384]{3,2,1,0:T(8,128)(2,1)} %cache_one.3) | copy-start | bytes 2359300
  34.2 10.8 %collective-permute-start.6 = (bf16[2,3,128,384]{3,2,1,0:T(8,128)(2,1)S(1)}, bf16[2,3,128,384]{3,2,1,0:T(8,128)(2,1)S(1)}, u32[]{:S(2)}, u32[]{:S(2)}) collective-permute-start(bf16[2,3,128,384]{3,2,1,0:T(8,128)(2,1)S(1)} %get-tuple-element.26.n2a), channel_id=1, source_target_pairs={{0,4},{4,8},{8,12},{12,16},{16,20},{20,24},{24,28},{1,5},{5,9},{9,... | collective-permute-start | bytes 1769480 | tf_op jit(solution)/shard_map/ppermute | solution.py:17
  35.6 7.6 %slice-start = ((s8[7962624]{0:T(1024)(128)(4,1)}), s8[4194304]{0:T(1024)(128)(4,1)S(1)}, s32[]{:S(2)}) async-start(s8[7962624]{0:T(1024)(128)(4,1)} %bitcast.9), calls=%async_computation | async-start | bytes 8388608
  35.6 7.5 %copy-start.7 = (f32[384]{0:T(512)S(1)}, f32[384]{0:T(512)}, u32[]{:S(2)}) copy-start(f32[384]{0:T(512)} %param.23) | copy-start | bytes 4612
  35.6 7.5 %slice-start.1 = ((s8[7962624]{0:T(1024)(128)(4,1)}), s8[3768320]{0:T(1024)(128)(4,1)S(1)}, s32[]{:S(2)}) async-start(s8[7962624]{0:T(1024)(128)(4,1)} %bitcast.9), calls=%async_computation.1 | async-start | bytes 7536640
  41.7 7.5 %collective-permute-start.7 = (bf16[2,3,128,384]{3,2,1,0:T(8,128)(2,1)S(1)}, bf16[2,3,128,384]{3,2,1,0:T(8,128)(2,1)S(1)}, u32[]{:S(2)}, u32[]{:S(2)}) collective-permute-start(bf16[2,3,128,384]{3,2,1,0:T(8,128)(2,1)S(1)} %second_part.1.n2b), channel_id=1, source_target_pairs={{0,4},{4,8},{8,12},{12,16},{16,20},{20,24},{24,28},{1,5},{5,9},{9,... | collective-permute-start | bytes 1769480 | tf_op jit(solution)/shard_map/ppermute | solution.py:17
  43.1 1.9 %copy-start = (bf16[2,4,128,384]{3,2,1,0:T(8,128)(2,1)S(1)}, bf16[2,4,128,384]{3,2,1,0:T(8,128)(2,1)}, u32[]{:S(2)}) copy-start(bf16[2,4,128,384]{3,2,1,0:T(8,128)(2,1)} %cache_two.3) | copy-start | bytes 2359300

commit v5 on v4

--- a/solution.py
+++ b/solution.py
@@ -179,6 +179,48 @@
     lax.fori_loop(0, w.shape[0], tap, 0)
 
 
+def first_kernels_body(w, w_in, cache_one, cache_two, u, w_big, placed_one, placed_two):
+    summed_kernels_body(w, u)
+
+    @pl.when(lax.axis_index("tm") == 0)
+    def _():
+        place = places(cache_one.shape[2], 1, True)
+        for source, placed in ((cache_one, placed_one), (cache_two, placed_two)):
+            for f in range(source.shape[0]):
+                for r in range(source.shape[1]):
+                    placed[f, r] = dot(place, source[f, r]).astype(BF)
+
+    c = w_in.shape[1]
+    chan = w_in.shape[0] // 27
+    slot = 4 * chan
+    w_big[...] = jnp.zeros_like(w_big)
+    for dt in range(3):
+        for dy in range(3):
+            taps = w_in[(3 * dt + dy) * 3 * chan : (3 * dt + dy + 1) * 3 * chan]
+            for k in range(2):
+                start = (4 * dt + dy + k) * slot
+                w_big[start : start + 3 * chan, k * c : (k + 1) * c] = taps
+
+
+def first_kernels(w, w_in, cache_one, cache_two):
+    taps, _, c, o = w.shape
+    chan = w_in.shape[0] // 27
+    return pl.pallas_call(
+        first_kernels_body,
+        in_specs=in_vmem(4),
+        out_specs=in_vmem(4),
+        out_shape=[
+            jax.ShapeDtypeStruct((2, taps, c, o), BF),
+            jax.ShapeDtypeStruct((48 * chan, 2 * c), BF),
+            jax.ShapeDtypeStruct(cache_one.shape, BF),
+            jax.ShapeDtypeStruct(cache_two.shape, BF),
+        ],
+        compiler_params=limit(16),
+        name="first_kernels",
+        cost_estimate=pl.CostEstimate(flops=6 * taps * c * o, bytes_accessed=10 * taps * c * o, transcendentals=0),
+    )(w, w_in, cache_one, cache_two)
+
+
 def summed_kernels(w):
     taps, _, c, o = w.shape
     return pl.pallas_call(
@@ -270,20 +312,22 @@
 
 def projection_body(
     tiles,
-    both, prev1, prev2, up, dn, w_in, b_in, gain_one,
+    both, prev1, prev2, up, dn, w_big, b_in, gain_one,
     hs, v2, v3, h0_ref,
-    lats, g, w_big,
+    lats, g,
 ):
     own = both.at[0 : prev1.shape[0]]
     v = (None, None, v2, v3)
     width = own.shape[-1]
-    c = w_in.shape[1]
-    chan = w_in.shape[0] // 27
+    c = w_big.shape[1] // 2
+    chan = w_big.shape[0] // 48
     rows = own.shape[0] // (2 * chan)
     rows1 = rows + 4
     slot = 4 * chan
 
-    lats[...] = jnp.zeros_like(lats)
+    empty = jnp.zeros((6, chan, width), BF)
+    for r in range(rows + 6):
+        lats[:, (r + 1) * slot - chan : (r + 1) * slot] = empty
     place = jnp.concatenate([places(width, dx, False) for dx in range(3)], 1)
 
     def lay(block, f0, r0, count):
@@ -311,13 +355,6 @@
             eye, lats[f], (((1,), (1,)), ((), ())), preferred_element_type=F32
         ).astype(BF)
 
-    w_big[...] = jnp.zeros_like(w_big)
-    for dt in range(3):
-        for dy in range(3):
-            taps = w_in[(3 * dt + dy) * 3 * chan : (3 * dt + dy + 1) * 3 * chan]
-            for k in range(2):
-                start = (4 * dt + dy + k) * slot
-                w_big[start : start + 3 * chan, k * c : (k + 1) * c] = taps
     bias = jnp.concatenate([b_in[...], b_in[...]], 1)
 
     columns = 2 * c // 3
@@ -354,46 +391,40 @@
         weave(project(p + 1) if p + 1 < pairs else [lambda: None], units(p))
 
 
-def first_cache(cache_one, cache_up, cache_dn, first, count, cached):
-    rows = cache_one.shape[1]
-
+def place_border(border, first, count, cached):
     @pl.when(lax.axis_index("tm") == 0)
     def _():
-        place = places(cache_one.shape[2], 1, True)
+        place = places(border.shape[2], 1, True)
         for f in range(2):
             for i in range(count):
-                r = first + i
-                if r < 2:
-                    row = cache_up[f, r]
-                elif r < 2 + rows:
-                    row = cache_one[f, r - 2]
-                else:
-                    row = cache_dn[f, r - 2 - rows]
-                cached[f, i] = dot(place, row).astype(BF)
-
-
-def earlier_units(tiles, gain_one, hs, v, cached, f, first, count):
+                cached[f, i] = dot(place, border[f, first + i]).astype(BF)
+
+
+def earlier_units(tiles, gain_one, hs, v, source, f, first, count):
     at_start = lax.axis_index("tm") == 0
 
     def normed(i):
         _, n1 = normed_row(tiles, gain_one, hs, f, first + i)
-        put(v, f, i, jnp.where(at_start, cached[f, i].astype(F32), n1))
+        put(v, f, i, jnp.where(at_start, source(f, first + i).astype(F32), n1))
 
     return [do(normed, i) for i in range(count)]
 
 
 def first_part_body(
-    tiles, hs, v2, v3, cache_one, cache_up, gain_one, w, u, b_one, gain_two,
+    tiles, hs, v2, v3, placed, cache_up, gain_one, w, u, b_one, gain_two,
     n2_ref, v0, v1,
     cached, acc,
 ):
     v = (v0, v1, v2, v3)
     rows = n2_ref.shape[1]
     needed = rows + 2
-    first_cache(cache_one, cache_up, None, 0, needed, cached)
+    place_border(cache_up, 0, 2, cached)
+
+    def source(f, r):
+        return cached[f, r] if r < 2 else placed[f, r - 2]
 
     def units(f):
-        return earlier_units(tiles, gain_one, hs, v, cached, f, 0, needed)
+        return earlier_units(tiles, gain_one, hs, v, source, f, 0, needed)
 
     conv_normed(
         tiles, lambda f, j: rows_of(v, f, j, 0, rows), plain_and_sums(w, u), acc, b_one,
@@ -402,13 +433,17 @@
 
 
 def second_part_body(
-    tiles, hs, v0, v1, v2, v3, cache_one, cache_dn, gain_one, w, u, b_one, gain_two,
+    tiles, hs, v0, v1, v2, v3, placed, cache_dn, gain_one, w, u, b_one, gain_two,
     n2_ref, cached, late, acc,
 ):
     rows = n2_ref.shape[1]
     there = v0.shape[1]
     early, late, own = (v0, v1), (late.at[0], late.at[1]), (None, None, v2, v3)
-    first_cache(cache_one, None, cache_dn, there, rows, cached)
+    here = placed.shape[1] + 2
+    place_border(cache_dn, 0, 2, cached)
+
+    def source(f, r):
+        return placed[f, r - 2] if r < here else cached[f, r - here]
 
     def patches(f, j):
         if f < 2:
@@ -416,7 +451,7 @@
         return rows_of(own, f, j, rows, rows)
 
     def units(f):
-        return earlier_units(tiles, gain_one, hs, late, cached, f, there, rows)
+        return earlier_units(tiles, gain_one, hs, late, source, f, there, rows)
 
     conv_normed(
         tiles, patches, plain_and_sums(w, u), acc, b_one, gain_two, n2_ref, rows,
@@ -424,29 +459,11 @@
     )
 
 
-def cached_rows(cache_two, cache_up, cache_dn, first, count, cached):
-    rows = cache_two.shape[1]
-
-    @pl.when(lax.axis_index("tm") == 0)
-    def _():
-        place = places(cache_two.shape[2], 1, True)
-        for f in range(2):
-            for i in range(count):
-                r = first + i
-                if r < 1:
-                    row = cache_up[f, 2]
-                elif r < 1 + rows:
-                    row = cache_two[f, r - 1]
-                else:
-                    row = cache_dn[f, 2]
-                cached[f, i] = dot(place, row).astype(BF)
-
-
-def split_earlier(v, f, earlier, cached):
+def split_earlier(v, f, earlier, source, first):
     at_start = lax.axis_index("tm") == 0
 
     def split(r):
-        row = jnp.where(at_start, cached[f, r].astype(F32), earlier[f, r].astype(F32))
+        row = jnp.where(at_start, source(f, first + r).astype(F32), earlier[f, r].astype(F32))
         put(v, f, r, row)
 
     return [do(split, r) for r in range(earlier.shape[1])]
@@ -457,7 +474,7 @@
 
 
 def own_frames_body(
-    n2a, n2b, earlier, cache_two, cache_up, w, u, h0, b_two,
+    n2a, n2b, earlier, placed, cache_up, w, u, h0, b_two,
     part_ref, ve0, ve1,
     cached, v, acc,
 ):
@@ -466,7 +483,10 @@
     rows = part_ref.shape[1]
     source = halves(n2a, n2b)
     v = (v.at[0], v.at[1])
-    cached_rows(cache_two, cache_up, None, 0, n2a.shape[1], cached)
+    place_border(cache_up, 2, 1, cached)
+
+    def cache_row(f, r):
+        return cached[f, 0] if r < 1 else placed[f, r - 1]
 
     def split(f):
         return [
@@ -494,14 +514,14 @@
     weave(pair(0) + pair(1), split(1))
     weave(
         pair(2) + pair(3),
-        split_earlier(ve, 0, earlier, cached) + split_earlier(ve, 1, earlier, cached),
+        split_earlier(ve, 0, earlier, cache_row, 0) + split_earlier(ve, 1, earlier, cache_row, 0),
     )
     weave([other(j) for j in range(4)], [do(finish, 0, r) for r in range(rows)])
     weave([lambda: None], [do(finish, 1, r) for r in range(rows)])
 
 
 def earlier_frames_body(
-    ve0, ve1, earlier, cache_two, cache_dn, w, u, part, out_ref, cached, late, acc
+    ve0, ve1, earlier, placed, cache_dn, w, u, part, out_ref, cached, late, acc
 ):
     width, c = earlier.shape[2:]
     half = width // 2
@@ -509,7 +529,12 @@
     kernel = plain_and_sums(w, u)
     first = (ve0, ve1)
     late = (late.at[0], late.at[1])
-    cached_rows(cache_two, None, cache_dn, ve0.shape[1], earlier.shape[1], cached)
+    place_border(cache_dn, 2, 1, cached)
+    there = ve0.shape[1]
+
+    def cache_row(f, r):
+        return placed[f, r - 1] if r < 1 + rows else cached[f, 0]
+
     back = places(width, 1, False)
 
     def finish(t, r):
@@ -518,11 +543,11 @@
         odd = part[t, r, half:] + m[1] - m[2] - m[3]
         out_ref[t, r] = dot(back, jnp.concatenate([even, odd], 0).astype(BF)).astype(BF)
 
-    weave([lambda: None], split_earlier(late, 1, earlier, cached))
+    weave([lambda: None], split_earlier(late, 1, earlier, cache_row, there))
     pairs = []
     for j in range(4):
         pairs += pair_pieces(acc, kernel, j, ((1, 0),), do(rows_joined, first, late, 1, j, 0, rows))
-    weave(pairs, split_earlier(late, 0, earlier, cached))
+    weave(pairs, split_earlier(late, 0, earlier, cache_row, there))
     weave(
         [single(acc, kernel, j, 0, 0, do(rows_joined, first, late, 0, j, 0, rows)) for j in range(4)],
         [do(finish, 1, r) for r in range(rows)],
@@ -563,7 +588,9 @@
     normed_part = jax.ShapeDtypeStruct((2, part_rows, width, c), BF)
     w1 = w_one.reshape(9, 3, c, c)
     w2 = w_two.reshape(9, 3, c, c)
-    u1 = summed_kernels(w1)
+    u1, w_big, placed_one, placed_two = first_kernels(
+        w1, w_in.reshape(-1, c), cache_one, cache_two
+    )
     u2 = summed_kernels(w2)
     filtered = jax.ShapeDtypeStruct((4, rows + 4, half, c), BF)
     hs, *v_own, h0 = pl.pallas_call(
@@ -579,26 +606,25 @@
         scratch_shapes=[
             VMEM((6, (rows + 6) * 4 * chan, width), BF),
             VMEM((6 * width, (rows + 6) * 4 * chan), BF),
-            VMEM((48 * chan, 2 * c), BF),
         ],
         compiler_params=limit(16),
         name="projection",
         cost_estimate=cost(6),
-    )(own_and_cache, prev1, prev2, up, dn, w_in.reshape(-1, c), row(b_in), row(gain_one))
+    )(own_and_cache, prev1, prev2, up, dn, w_big, row(b_in), row(gain_one))
     n2a, *v_earlier = pl.pallas_call(
         functools.partial(first_part_body, tiles),
         out_shape=[normed_part, *[jax.ShapeDtypeStruct((4, part_rows + 2, half, c), BF)] * 2],
         in_specs=in_vmem(10),
         out_specs=in_vmem(3),
         scratch_shapes=[
-            VMEM((2, part_rows + 2, width, c), BF),
+            VMEM((2, 2, width, c), BF),
             VMEM((4, 2, part_rows * half, c), F32),
         ],
         compiler_params=limit(20),
         name="first_part",
         cost_estimate=cost(8),
     )(
-        hs, *v_own, cache_one, cache_up, row(gain_one),
+        hs, *v_own, placed_one, cache_up, row(gain_one),
         w1, u1, row(b_one), row(gain_two),
     )
     earlier_a = shifted(n2a, "tm", 1)
@@ -608,7 +634,7 @@
         in_specs=in_vmem(12),
         out_specs=in_vmem(1)[0],
         scratch_shapes=[
-            VMEM((2, part_rows, width, c), BF),
+            VMEM((2, 2, width, c), BF),
             VMEM((2, 4, part_rows, half, c), BF),
             VMEM((4, 2, part_rows * half, c), F32),
         ],
@@ -616,7 +642,7 @@
         name="second_part",
         cost_estimate=cost(0.2),
     )(
-        hs, *v_earlier, *v_own, cache_one, cache_dn, row(gain_one),
+        hs, *v_earlier, *v_own, placed_one, cache_dn, row(gain_one),
         w1, u1, row(b_one), row(gain_two),
     )
     earlier_b = shifted(n2b, "tm", 1)
@@ -631,28 +657,28 @@
         in_specs=in_vmem(9),
         out_specs=in_vmem(3),
         scratch_shapes=[
-            VMEM((2, part_rows, width, c), BF),
+            VMEM((2, 2, width, c), BF),
             VMEM((2, 4, rows + 2, half, c), BF),
             VMEM((4, 2, rows * half, c), F32),
         ],
         compiler_params=limit(20),
         name="own_frames",
         cost_estimate=cost(4),
-    )(n2a, n2b, earlier_a, cache_two, cache_up, w2, u2, h0, row(b_two))
+    )(n2a, n2b, earlier_a, placed_two, cache_up, w2, u2, h0, row(b_two))
     return pl.pallas_call(
         earlier_frames_body,
         out_shape=jax.ShapeDtypeStruct((2, rows, width, c), BF),
         in_specs=in_vmem(8),
         out_specs=in_vmem(1)[0],
         scratch_shapes=[
-            VMEM((2, part_rows, width, c), BF),
+            VMEM((2, 2, width, c), BF),
             VMEM((2, 4, part_rows, half, c), BF),
             VMEM((4, 2, rows * half, c), F32),
         ],
         compiler_params=limit(20),
         name="earlier_frames",
         cost_estimate=cost(4),
-    )(*ve, earlier_b, cache_two, cache_dn, w2, u2, part)
+    )(*ve, earlier_b, placed_two, cache_dn, w2, u2, part)
 
 
 def solution(mesh):

time: 54.9 us -> 53.8 us (0.980)
  other arithmetic: 1.07 us -> 0.15 us
  waiting for transfers between devices: 1.61 us -> 0.91 us
    pallas_call x0 -> x1, Pallas kernels: none -> 2.52 us  [first_kernels(): pl.pallas_call(first_kernels_body, in_specs=in_vmem(4), out_specs=in_vmem...]
    pallas_call x2 -> x1, Pallas kernels: 3.66 us -> 1.83 us  [summed_kernels(): pl.pallas_call(summed_kernels_body, in_specs=in_vmem(1), out_specs=in_vme...]
    concatenate x1, other arithmetic: 0.93 us -> 0.01 us  [on_device(): jnp.concatenate([own, flat(jnp.swapaxes(cache_lat, 2, 3))], 0)]
    ppermute x6, waiting for transfers between devices: 1.61 us -> 0.9 us  [shifted(): lax.ppermute(x, axis, [(i, i + by) for i in range(count) if 0 <= i + by <...]
  transfers between devices with their start and end apart: 8 -> 8, of which waited for: 1 -> 1; matrix products, arithmetic and copies ran while one was open for 6% -> 5% of each run, Pallas kernels for 45% -> 46%
where the time goes in v5:
time: 53.8 us; the launch traced here: 53.2 us
  Pallas kernels  29.7 us (55%)
  starting transfers between devices  19.6 us (36%)
  local copies, waits for them, and re-layouts  2.38 us (4%)
  waiting for transfers between devices  0.91 us (2%)
    ppermute x6, starting transfers between devices, shifted(): lax.ppermute(x, axis, [(i, i + by) for i in range(count) if 0 <= i + by <...  14.8 us
    pallas_call x1, Pallas kernels, on_device(): pl.pallas_call(functools.partial(first_part_body, tiles), out_shape=[norm...  6.06 us
    pallas_call x1, Pallas kernels, on_device(): pl.pallas_call(functools.partial(second_part_body, tiles), out_shape=norm...  6 us
    pallas_call x1, Pallas kernels, on_device(): pl.pallas_call(earlier_frames_body, out_shape=jax.ShapeDtypeStruct((2, ro...  5.23 us
    ppermute x2, starting transfers between devices, first_frames_only(): lax.ppermute(x, ('tm', 'tile'), [(i, i + by) for i in range(rows) if 0 <=...  4.81 us
    pallas_call x1, Pallas kernels, on_device(): pl.pallas_call(own_frames_body, out_shape=[jax.ShapeDtypeStruct((2, rows,...  4.12 us
    pallas_call x1, Pallas kernels, on_device(): pl.pallas_call(functools.partial(projection_body, tiles), out_shape=[jax....  3.93 us
    pallas_call x1, Pallas kernels, first_kernels(): pl.pallas_call(first_kernels_body, in_specs=in_vmem(4), out_specs=in_vmem...  2.52 us
  transfers between devices with their start and end apart: 8, of which 1 were waited for; matrix products, arithmetic and copies ran while one was open for 5% of the time, Pallas kernels for 46%

profile of v5, /device:TPU:0, one launch (start us, length us, event | category | flops | bytes accessed | tf_op | source)
XLA Modules:
  0.0 53.2 jit_solution(15680744414287763173)
XLA Ops:
  0.0 2.5 %collective-permute-start = (bf16[128,128]{1,0:T(8,128)(2,1)}, bf16[128,128]{1,0:T(8,128)(2,1)S(1)}, u32[]{:S(2)}, u32[]{:S(2)}) collective-permute-start(bf16[128,128]{1,0:T(8,128)(2,1)} %bitcast.21), channel_id=1, source_target_pairs={{0,4},{4,8},{8,12},{12,16},{16,20},{20,24},{24,28},{1,5},{5,9},{9,... | collective-permute-start | bytes 98312 | tf_op jit(solution)/shard_map/ppermute | solution.py:17
  2.5 4.4 %collective-permute-start.1 = (bf16[128,128]{1,0:T(8,128)(2,1)}, bf16[128,128]{1,0:T(8,128)(2,1)S(1)}, u32[]{:S(2)}, u32[]{:S(2)}) collective-permute-start(bf16[128,128]{1,0:T(8,128)(2,1)} %bitcast.22), channel_id=1, source_target_pairs={{0,8},{4,12},{8,16},{12,20},{16,24},{20,28},{1,9},{5,13},{9,17},{1... | collective-permute-start | bytes 98312 | tf_op jit(solution)/shard_map/ppermute | solution.py:17
  6.9 1.1 %fusion.1 = (bf16[2,1,128,384]{3,2,1,0:T(8,128)(2,1)S(1)}, bf16[2,1,128,384]{3,2,1,0:T(8,128)(2,1)S(1)}) fusion(bf16[2,4,128,384]{3,2,1,0:T(8,128)(2,1)} %cache_two.1), kind=kLoop, calls=%fused_computation.4 | loop fusion | bytes 786432 | tf_op jit(solution)/shard_map/slice | solution.py:585
  8.0 1.2 %fusion = (bf16[2,2,128,384]{3,2,1,0:T(8,128)(2,1)S(1)}, bf16[2,2,128,384]{3,2,1,0:T(8,128)(2,1)S(1)}) fusion(bf16[2,4,128,384]{3,2,1,0:T(8,128)(2,1)} %cache_one.1), kind=kLoop, calls=%fused_computation.3 | loop fusion | bytes 1572864 | tf_op jit(solution)/shard_map/slice | solution.py:585
  9.2 0.1 pad_maximum_fusion
  9.3 3.5 %collective-permute-start.4 = (bf16[2,3,128,384]{3,2,1,0:T(8,128)(2,1)S(1)}, bf16[2,3,128,384]{3,2,1,0:T(8,128)(2,1)S(1)}, u32[]{:S(2)}, u32[]{:S(2)}) collective-permute-start(bf16[2,3,128,384]{3,2,1,0:T(8,128)(2,1)S(1)} %pad_maximum_fusion), channel_id=1, source_target_pairs={{0,1},{1,2},{2,3}} | collective-permute-start | bytes 1769480 | tf_op jit(solution)/shard_map/ppermute | solution.py:22
  12.8 0.0 slice-start.2
  12.8 0.0 copy-start.5
  12.9 0.0 copy-start.6
  12.9 0.0 copy-start.7
  12.9 0.0 copy-start.8
  12.9 0.0 slice-start.3
  12.9 0.0 copy-start
  12.9 0.0 copy-start.1
  12.9 0.0 copy-start.2
  13.0 3.7 %collective-permute-start.2 = (bf16[288,128]{1,0:T(8,128)(2,1)S(1)}, bf16[288,128]{1,0:T(8,128)(2,1)S(1)}, u32[]{:S(2)}, u32[]{:S(2)}) collective-permute-start(bf16[288,128]{1,0:T(8,128)(2,1)S(1)} %get-tuple-element.25), channel_id=1, source_target_pairs={{0,1},{1,2},{2,3},{4,5},{5,6},{6,7},{8,9},{9,10},{10,11},{12,13},{... | collective-permute-start | bytes 221192 | tf_op jit(solution)/shard_map/ppermute | solution.py:17
  16.7 1.3 %collective-permute-start.3 = (bf16[288,128]{1,0:T(8,128)(2,1)S(1)}, bf16[288,128]{1,0:T(8,128)(2,1)S(1)}, u32[]{:S(2)}, u32[]{:S(2)}) collective-permute-start(bf16[288,128]{1,0:T(8,128)(2,1)S(1)} %get-tuple-element.26), channel_id=1, source_target_pairs={{1,0},{2,1},{3,2},{5,4},{6,5},{7,6},{9,8},{10,9},{11,10},{13,12},{... | collective-permute-start | bytes 221192 | tf_op jit(solution)/shard_map/ppermute | solution.py:17
  18.0 0.1 pad_maximum_fusion.1
  18.1 1.3 %collective-permute-start.5 = (bf16[2,3,128,384]{3,2,1,0:T(8,128)(2,1)S(1)}, bf16[2,3,128,384]{3,2,1,0:T(8,128)(2,1)S(1)}, u32[]{:S(2)}, u32[]{:S(2)}) collective-permute-start(bf16[2,3,128,384]{3,2,1,0:T(8,128)(2,1)S(1)} %pad_maximum_fusion.1), channel_id=1, source_target_pairs={{1,0},{2,1},{3,2}} | collective-permute-start | bytes 1769480 | tf_op jit(solution)/shard_map/ppermute | solution.py:22
  19.5 2.5 %first_kernels.1 = (bf16[2,9,384,384]{3,2,1,0:T(8,128)(2,1)S(1)}, bf16[768,768]{1,0:T(8,128)(2,1)S(1)}, bf16[2,4,128,384]{3,2,1,0:T(8,128)(2,1)S(1)}, bf16[2,4,128,384]{3,2,1,0:T(8,128)(2,1)S(1)}) custom-call(bf16[9,3,384,384]{3,2,1,0:T(8,128)(2,1)S(1)} %bitcast.16, bf16[432,384]{1,0:T(8,128)(2,1)S(1)} %bitcast.19, bf16[2,4,128,384]{3,2,1,0:T(8,128)(2,1)S(1)} %copy-done, ...), custom_call_target="tpu_custom_call" | custom-call | flops 7962624 | bytes 13271040 | tf_op jit(solution)/shard_map/first_kernels/pallas_call | solution.py:208
  22.1 0.9 %collective-permute-done.3.dn = bf16[288,128]{1,0:T(8,128)(2,1)S(1)} collective-permute-done((bf16[288,128]{1,0:T(8,128)(2,1)S(1)}, bf16[288,128]{1,0:T(8,128)(2,1)S(1)}, u32[]{:S(2)}, u32[]{:S(2)}) %collective-permute-start.3) | collective-permute-done | bytes 73760 | tf_op jit(solution)/shard_map/ppermute | solution.py:17
  23.0 3.9 %projection.1 = (bf16[4,512,768]{2,1,0:T(8,128)(2,1)S(1)}, bf16[4,8,64,384]{3,2,1,0:T(8,128)(2,1)S(1)}, bf16[4,8,64,384]{3,2,1,0:T(8,128)(2,1)S(1)}, bf16[2,4,128,384]{3,2,1,0:T(8,128)(2,1)S(1)}) custom-call(bf16[256,128]{1,0:T(8,128)(2,1)S(1)} %pad_maximum_fusion.2.both, bf16[128,128]{1,0:T(8,128)(2,1)S(1)} %get-tuple-element.23.prev1, ...), custom_call_target="tpu_custom_call" | custom-call | flops 6000000000 | bytes 6000000 | tf_op jit(solution)/shard_map/projection/pallas_call | solution.py:596
  26.9 0.0 collective-permute-done.4.cache_up
  26.9 6.1 %first_part.1 = (bf16[2,3,128,384]{3,2,1,0:T(8,128)(2,1)S(1)}, bf16[4,5,64,384]{3,2,1,0:T(8,128)(2,1)S(1)}, bf16[4,5,64,384]{3,2,1,0:T(8,128)(2,1)S(1)}) custom-call(bf16[4,512,768]{2,1,0:T(8,128)(2,1)S(1)} %get-tuple-element.28.hs, bf16[4,8,64,384]{3,2,1,0:T(8,128)(2,1)S(1)} %get-tuple-element.29.v2, bf16[4,8,64,384]{3,2,1,0:T(8,128)(2,1)S(1)} %get-tuple-element.30.v3, ...), custom_call_target="tpu_custom_call" | custom-call | flops 8000000000 | bytes 8000000 | tf_op jit(solution)/shard_map/first_part/pallas_call | solution.py:614
  33.0 1.3 %collective-permute-start.6 = (bf16[2,3,128,384]{3,2,1,0:T(8,128)(2,1)S(1)}, bf16[2,3,128,384]{3,2,1,0:T(8,128)(2,1)S(1)}, u32[]{:S(2)}, u32[]{:S(2)}) collective-permute-start(bf16[2,3,128,384]{3,2,1,0:T(8,128)(2,1)S(1)} %get-tuple-element.33.n2a), channel_id=1, source_target_pairs={{0,4},{4,8},{8,12},{12,16},{16,20},{20,24},{24,28},{1,5},{5,9},{9,... | collective-permute-start | bytes 1769480 | tf_op jit(solution)/shard_map/ppermute | solution.py:17
  34.3 0.0 slice-start
  34.3 0.0 copy-start.9
  34.4 6.0 %second_part.1.n2b = bf16[2,3,128,384]{3,2,1,0:T(8,128)(2,1)S(1)} custom-call(bf16[4,512,768]{2,1,0:T(8,128)(2,1)S(1)} %get-tuple-element.28.hs, bf16[4,5,64,384]{3,2,1,0:T(8,128)(2,1)S(1)} %get-tuple-element.34.v0, bf16[4,5,64,384]{3,2,1,0:T(8,128)(2,1)S(1)} %get-tuple-element.35.v1, bf16[4,8,64,384]{3,2,1,0:T(8,128)(2,1)S(1)} %get-tuple-element.29.v2, ...), custom_call_target="tpu_custom_call" | custom-call | flops 200000000 | bytes 200000 | tf_op jit(solution)/shard_map/second_part/pallas_call | solution.py:631
  40.4 1.6 %collective-permute-start.7 = (bf16[2,3,128,384]{3,2,1,0:T(8,128)(2,1)S(1)}, bf16[2,3,128,384]{3,2,1,0:T(8,128)(2,1)S(1)}, u32[]{:S(2)}, u32[]{:S(2)}) collective-permute-start(bf16[2,3,128,384]{3,2,1,0:T(8,128)(2,1)S(1)} %second_part.1.n2b), channel_id=1, source_target_pairs={{0,4},{4,8},{8,12},{12,16},{16,20},{20,24},{24,28},{1,5},{5,9},{9,... | collective-permute-start | bytes 1769480 | tf_op jit(solution)/shard_map/ppermute | solution.py:17
  42.0 1.8 %summed_kernels.1.u = bf16[2,9,384,384]{3,2,1,0:T(8,128)(2,1)S(1)} custom-call(bf16[9,3,384,384]{3,2,1,0:T(8,128)(2,1)S(1)} %bitcast.11), custom_call_target="tpu_custom_call" | custom-call | flops 7962624 | bytes 13271040 | tf_op jit(solution)/shard_map/summed_kernels/pallas_call | solution.py:226
  43.9 4.1 %own_frames.1 = (f32[2,4,128,384]{3,2,1,0:T(8,128)S(1)}, bf16[4,3,64,384]{3,2,1,0:T(8,128)(2,1)S(1)}, bf16[4,3,64,384]{3,2,1,0:T(8,128)(2,1)S(1)}) custom-call(bf16[2,3,128,384]{3,2,1,0:T(8,128)(2,1)S(1)} %get-tuple-element.33.n2a, bf16[2,3,128,384]{3,2,1,0:T(8,128)(2,1)S(1)} %second_part.1.n2b, bf16[2,3,128,384]{3,2,1,0:T(8,128)(2,1)S(1)} %collective-permute-done.6.earlier, ...), custom_call_target="tpu_custom_call" | custom-call | flops 4000000000 | bytes 4000000 | tf_op jit(solution)/shard_map/own_frames/pallas_call | solution.py:650
  48.0 5.2 %earlier_frames.1 = bf16[2,4,128,384]{3,2,1,0:T(8,128)(2,1)} custom-call(bf16[4,3,64,384]{3,2,1,0:T(8,128)(2,1)S(1)} %get-tuple-element.38.ve0, bf16[4,3,64,384]{3,2,1,0:T(8,128)(2,1)S(1)} %get-tuple-element.39.ve1, bf16[2,3,128,384]{3,2,1,0:T(8,128)(2,1)S(1)} %collective-permute-done.7.earlier, bf16[2,4,128,384]{3,2,1,0:T(8,128)(2,1)S(1)} %get-tuple-element.36.placed, ...), custom_call_target="tpu_custom_call" | custom-call | flops 4000000000 | bytes 4000000 | tf_op jit(solution)/shard_map/earlier_frames/pallas_call | solution.py:668
  (32 shorter events, 0.1 us)
Async XLA Ops:
  0.0 12.8 %copy-start.4 = (bf16[2,4,128,16]{2,3,1,0:T(8,128)(2,1)S(1)}, bf16[2,4,128,16]{2,3,1,0:T(8,128)(2,1)}, u32[]{:S(2)}) copy-start(bf16[2,4,128,16]{2,3,1,0:T(8,128)(2,1)} %param.12) | copy-start | bytes 98308
  0.0 12.8 %copy-start.3 = (bf16[2,4,128,16]{2,3,1,0:T(8,128)(2,1)S(1)}, bf16[2,4,128,16]{2,3,1,0:T(8,128)(2,1)}, u32[]{:S(2)}) copy-start(bf16[2,4,128,16]{2,3,1,0:T(8,128)(2,1)} %param.13) | copy-start | bytes 98308
  0.0 12.9 %collective-permute-start = (bf16[128,128]{1,0:T(8,128)(2,1)}, bf16[128,128]{1,0:T(8,128)(2,1)S(1)}, u32[]{:S(2)}, u32[]{:S(2)}) collective-permute-start(bf16[128,128]{1,0:T(8,128)(2,1)} %bitcast.21), channel_id=1, source_target_pairs={{0,4},{4,8},{8,12},{12,16},{16,20},{20,24},{24,28},{1,5},{5,9},{9,... | collective-permute-start | bytes 98312 | tf_op jit(solution)/shard_map/ppermute | solution.py:17
  2.5 10.5 %collective-permute-start.1 = (bf16[128,128]{1,0:T(8,128)(2,1)}, bf16[128,128]{1,0:T(8,128)(2,1)S(1)}, u32[]{:S(2)}, u32[]{:S(2)}) collective-permute-start(bf16[128,128]{1,0:T(8,128)(2,1)} %bitcast.22), channel_id=1, source_target_pairs={{0,8},{4,12},{8,16},{12,20},{16,24},{20,28},{1,9},{5,13},{9,17},{1... | collective-permute-start | bytes 98312 | tf_op jit(solution)/shard_map/ppermute | solution.py:17
  9.3 17.6 %collective-permute-start.4 = (bf16[2,3,128,384]{3,2,1,0:T(8,128)(2,1)S(1)}, bf16[2,3,128,384]{3,2,1,0:T(8,128)(2,1)S(1)}, u32[]{:S(2)}, u32[]{:S(2)}) collective-permute-start(bf16[2,3,128,384]{3,2,1,0:T(8,128)(2,1)S(1)} %pad_maximum_fusion), channel_id=1, source_target_pairs={{0,1},{1,2},{2,3}} | collective-permute-start | bytes 1769480 | tf_op jit(solution)/shard_map/ppermute | solution.py:22
  12.8 6.7 %slice-start.2 = ((s8[7962624]{0:T(1024)(128)(4,1)}), s8[4194304]{0:T(1024)(128)(4,1)S(1)}, s32[]{:S(2)}) async-start(s8[7962624]{0:T(1024)(128)(4,1)} %bitcast.14), calls=%async_computation.2 | async-start | bytes 8388608
  12.8 6.6 %copy-start.5 = (f32[384]{0:T(512)S(1)}, f32[384]{0:T(512)}, u32[]{:S(2)}) copy-start(f32[384]{0:T(512)} %param.17) | copy-start | bytes 4612
  12.9 6.6 %copy-start.6 = (f32[384]{0:T(512)S(1)}, f32[384]{0:T(512)}, u32[]{:S(2)}) copy-start(f32[384]{0:T(512)} %param.18) | copy-start | bytes 4612
  12.9 6.6 %copy-start.7 = (f32[384]{0:T(512)S(1)}, f32[384]{0:T(512)}, u32[]{:S(2)}) copy-start(f32[384]{0:T(512)} %param.20) | copy-start | bytes 4612
  12.9 6.6 %copy-start.8 = (f32[384]{0:T(512)S(1)}, f32[384]{0:T(512)}, u32[]{:S(2)}) copy-start(f32[384]{0:T(512)} %param.21) | copy-start | bytes 4612
  12.9 6.6 %slice-start.3 = ((s8[7962624]{0:T(1024)(128)(4,1)}), s8[3768320]{0:T(1024)(128)(4,1)S(1)}, s32[]{:S(2)}) async-start(s8[7962624]{0:T(1024)(128)(4,1)} %bitcast.14), calls=%async_computation.3 | async-start | bytes 7536640
  12.9 6.6 %copy-start = (bf16[2,4,128,384]{3,2,1,0:T(8,128)(2,1)S(1)}, bf16[2,4,128,384]{3,2,1,0:T(8,128)(2,1)}, u32[]{:S(2)}) copy-start(bf16[2,4,128,384]{3,2,1,0:T(8,128)(2,1)} %cache_one.1) | copy-start | bytes 2359300
  12.9 6.6 %copy-start.1 = (bf16[2,4,128,384]{3,2,1,0:T(8,128)(2,1)S(1)}, bf16[2,4,128,384]{3,2,1,0:T(8,128)(2,1)}, u32[]{:S(2)}) copy-start(bf16[2,4,128,384]{3,2,1,0:T(8,128)(2,1)} %cache_two.1) | copy-start | bytes 2359300
  12.9 6.6 %copy-start.2 = (bf16[3,3,3,16,384]{4,3,2,1,0:T(8,128)(2,1)S(1)}, bf16[3,3,3,16,384]{4,3,2,1,0:T(8,128)(2,1)}, u32[]{:S(2)}) copy-start(bf16[3,3,3,16,384]{4,3,2,1,0:T(8,128)(2,1)} %param.16) | copy-start | bytes 995332
  13.0 9.1 %collective-permute-start.2 = (bf16[288,128]{1,0:T(8,128)(2,1)S(1)}, bf16[288,128]{1,0:T(8,128)(2,1)S(1)}, u32[]{:S(2)}, u32[]{:S(2)}) collective-permute-start(bf16[288,128]{1,0:T(8,128)(2,1)S(1)} %get-tuple-element.25), channel_id=1, source_target_pairs={{0,1},{1,2},{2,3},{4,5},{5,6},{6,7},{8,9},{9,10},{10,11},{12,13},{... | collective-permute-start | bytes 221192 | tf_op jit(solution)/shard_map/ppermute | solution.py:17
  16.7 6.2 %collective-permute-start.3 = (bf16[288,128]{1,0:T(8,128)(2,1)S(1)}, bf16[288,128]{1,0:T(8,128)(2,1)S(1)}, u32[]{:S(2)}, u32[]{:S(2)}) collective-permute-start(bf16[288,128]{1,0:T(8,128)(2,1)S(1)} %get-tuple-element.26), channel_id=1, source_target_pairs={{1,0},{2,1},{3,2},{5,4},{6,5},{7,6},{9,8},{10,9},{11,10},{13,12},{... | collective-permute-start | bytes 221192 | tf_op jit(solution)/shard_map/ppermute | solution.py:17
  18.1 16.2 %collective-permute-start.5 = (bf16[2,3,128,384]{3,2,1,0:T(8,128)(2,1)S(1)}, bf16[2,3,128,384]{3,2,1,0:T(8,128)(2,1)S(1)}, u32[]{:S(2)}, u32[]{:S(2)}) collective-permute-start(bf16[2,3,128,384]{3,2,1,0:T(8,128)(2,1)S(1)} %pad_maximum_fusion.1), channel_id=1, source_target_pairs={{1,0},{2,1},{3,2}} | collective-permute-start | bytes 1769480 | tf_op jit(solution)/shard_map/ppermute | solution.py:22
  33.0 10.9 %collective-permute-start.6 = (bf16[2,3,128,384]{3,2,1,0:T(8,128)(2,1)S(1)}, bf16[2,3,128,384]{3,2,1,0:T(8,128)(2,1)S(1)}, u32[]{:S(2)}, u32[]{:S(2)}) collective-permute-start(bf16[2,3,128,384]{3,2,1,0:T(8,128)(2,1)S(1)} %get-tuple-element.33.n2a), channel_id=1, source_target_pairs={{0,4},{4,8},{8,12},{12,16},{16,20},{20,24},{24,28},{1,5},{5,9},{9,... | collective-permute-start | bytes 1769480 | tf_op jit(solution)/shard_map/ppermute | solution.py:17
  34.3 7.6 %slice-start = ((s8[7962624]{0:T(1024)(128)(4,1)}), s8[4194304]{0:T(1024)(128)(4,1)S(1)}, s32[]{:S(2)}) async-start(s8[7962624]{0:T(1024)(128)(4,1)} %bitcast.9), calls=%async_computation | async-start | bytes 8388608
  34.3 7.6 %copy-start.9 = (f32[384]{0:T(512)S(1)}, f32[384]{0:T(512)}, u32[]{:S(2)}) copy-start(f32[384]{0:T(512)} %param.23) | copy-start | bytes 4612
  34.4 7.6 %slice-start.1 = ((s8[7962624]{0:T(1024)(128)(4,1)}), s8[3768320]{0:T(1024)(128)(4,1)S(1)}, s32[]{:S(2)}) async-start(s8[7962624]{0:T(1024)(128)(4,1)} %bitcast.9), calls=%async_computation.1 | async-start | bytes 7536640
  40.4 7.6 %collective-permute-start.7 = (bf16[2,3,128,384]{3,2,1,0:T(8,128)(2,1)S(1)}, bf16[2,3,128,384]{3,2,1,0:T(8,128)(2,1)S(1)}, u32[]{:S(2)}, u32[]{:S(2)}) collective-permute-start(bf16[2,3,128,384]{3,2,1,0:T(8,128)(2,1)S(1)} %second_part.1.n2b), channel_id=1, source_target_pairs={{0,4},{4,8},{8,12},{12,16},{16,20},{20,24},{24,28},{1,5},{5,9},{9,... | collective-permute-start | bytes 1769480 | tf_op jit(solution)/shard_map/ppermute | solution.py:17

commit v6 on v5

--- a/solution.py
+++ b/solution.py
@@ -155,7 +155,9 @@
     out = []
     for dy in range(3):
         start, end = at + dy, at + dy + rows
-        if start < split:
+        if end <= split:
+            out.append(first[f][j, start:end].reshape(rows * half, c))
+        elif start < split:
             a = first[f][j, start:split].reshape((split - start) * half, c)
             b = last[f][j, 0 : end - split].reshape((end - split) * half, c)
             out.append(jnp.concatenate([a, b], 0))
@@ -521,7 +523,7 @@
 
 
 def earlier_frames_body(
-    ve0, ve1, earlier, placed, cache_dn, w, u, part, out_ref, cached, late, acc
+    ve0, ve1, earlier, placed, cache_dn, w, u, part, out_ref, cached, late, acc, columns
 ):
     width, c = earlier.shape[2:]
     half = width // 2
@@ -535,13 +537,17 @@
     def cache_row(f, r):
         return placed[f, r - 1] if r < 1 + rows else cached[f, 0]
 
-    back = places(width, 1, False)
 
     def finish(t, r):
         m = [acc[j, t, r * half : (r + 1) * half] for j in range(4)]
         even = part[t, r, 0:half] + m[0] + m[1] + m[2]
         odd = part[t, r, half:] + m[1] - m[2] - m[3]
-        out_ref[t, r] = dot(back, jnp.concatenate([even, odd], 0).astype(BF)).astype(BF)
+        for k in range(c // 128):
+            lanes = slice(k * 128, (k + 1) * 128)
+            row = columns.at[(t * rows + r) * (c // 128) + k]
+            row[pl.ds(0, half, stride=2)] = even[:, lanes]
+            row[pl.ds(1, half, stride=2)] = odd[:, lanes]
+            out_ref[t, r, :, lanes] = row[...].astype(BF)
 
     weave([lambda: None], split_earlier(late, 1, earlier, cache_row, there))
     pairs = []
@@ -674,6 +680,7 @@
             VMEM((2, 2, width, c), BF),
             VMEM((2, 4, part_rows, half, c), BF),
             VMEM((4, 2, rows * half, c), F32),
+            VMEM((2 * rows * (c // 128), width, 128), F32),
         ],
         compiler_params=limit(20),
         name="earlier_frames",

time: 53.8 us -> 53.6 us (level)
  no operation moved by 1% of the time
where the time goes in v6:
time: 53.6 us; the launch traced here: 53.1 us
  Pallas kernels  29.6 us (55%)
  starting transfers between devices  19.6 us (37%)
  local copies, waits for them, and re-layouts  2.38 us (4%)
  waiting for transfers between devices  0.91 us (2%)
    ppermute x6, starting transfers between devices, shifted(): lax.ppermute(x, axis, [(i, i + by) for i in range(count) if 0 <= i + by <...  14.8 us
    pallas_call x1, Pallas kernels, on_device(): pl.pallas_call(functools.partial(first_part_body, tiles), out_shape=[norm...  6.06 us
    pallas_call x1, Pallas kernels, on_device(): pl.pallas_call(functools.partial(second_part_body, tiles), out_shape=norm...  6 us
    pallas_call x1, Pallas kernels, on_device(): pl.pallas_call(earlier_frames_body, out_shape=jax.ShapeDtypeStruct((2, ro...  5.08 us
    ppermute x2, starting transfers between devices, first_frames_only(): lax.ppermute(x, ('tm', 'tile'), [(i, i + by) for i in range(rows) if 0 <=...  4.81 us
    pallas_call x1, Pallas kernels, on_device(): pl.pallas_call(own_frames_body, out_shape=[jax.ShapeDtypeStruct((2, rows,...  4.12 us
    pallas_call x1, Pallas kernels, on_device(): pl.pallas_call(functools.partial(projection_body, tiles), out_shape=[jax....  3.93 us
    pallas_call x1, Pallas kernels, first_kernels(): pl.pallas_call(first_kernels_body, in_specs=in_vmem(4), out_specs=in_vmem...  2.52 us
  transfers between devices with their start and end apart: 8, of which 1 were waited for; matrix products, arithmetic and copies ran while one was open for 5% of the time, Pallas kernels for 46%

profile of v6, /device:TPU:0, one launch (start us, length us, event | category | flops | bytes accessed | tf_op | source)
XLA Modules:
  0.0 53.1 jit_solution(16482682645109539322)
XLA Ops:
  0.0 2.5 %collective-permute-start = (bf16[128,128]{1,0:T(8,128)(2,1)}, bf16[128,128]{1,0:T(8,128)(2,1)S(1)}, u32[]{:S(2)}, u32[]{:S(2)}) collective-permute-start(bf16[128,128]{1,0:T(8,128)(2,1)} %bitcast.21), channel_id=1, source_target_pairs={{0,4},{4,8},{8,12},{12,16},{16,20},{20,24},{24,28},{1,5},{5,9},{9,... | collective-permute-start | bytes 98312 | tf_op jit(solution)/shard_map/ppermute | solution.py:17
  2.5 4.4 %collective-permute-start.1 = (bf16[128,128]{1,0:T(8,128)(2,1)}, bf16[128,128]{1,0:T(8,128)(2,1)S(1)}, u32[]{:S(2)}, u32[]{:S(2)}) collective-permute-start(bf16[128,128]{1,0:T(8,128)(2,1)} %bitcast.22), channel_id=1, source_target_pairs={{0,8},{4,12},{8,16},{12,20},{16,24},{20,28},{1,9},{5,13},{9,17},{1... | collective-permute-start | bytes 98312 | tf_op jit(solution)/shard_map/ppermute | solution.py:17
  6.9 1.1 %fusion.1 = (bf16[2,1,128,384]{3,2,1,0:T(8,128)(2,1)S(1)}, bf16[2,1,128,384]{3,2,1,0:T(8,128)(2,1)S(1)}) fusion(bf16[2,4,128,384]{3,2,1,0:T(8,128)(2,1)} %cache_two.1), kind=kLoop, calls=%fused_computation.4 | loop fusion | bytes 786432 | tf_op jit(solution)/shard_map/slice | solution.py:591
  8.0 1.2 %fusion = (bf16[2,2,128,384]{3,2,1,0:T(8,128)(2,1)S(1)}, bf16[2,2,128,384]{3,2,1,0:T(8,128)(2,1)S(1)}) fusion(bf16[2,4,128,384]{3,2,1,0:T(8,128)(2,1)} %cache_one.1), kind=kLoop, calls=%fused_computation.3 | loop fusion | bytes 1572864 | tf_op jit(solution)/shard_map/slice | solution.py:591
  9.2 0.1 pad_maximum_fusion
  9.3 3.5 %collective-permute-start.4 = (bf16[2,3,128,384]{3,2,1,0:T(8,128)(2,1)S(1)}, bf16[2,3,128,384]{3,2,1,0:T(8,128)(2,1)S(1)}, u32[]{:S(2)}, u32[]{:S(2)}) collective-permute-start(bf16[2,3,128,384]{3,2,1,0:T(8,128)(2,1)S(1)} %pad_maximum_fusion), channel_id=1, source_target_pairs={{0,1},{1,2},{2,3}} | collective-permute-start | bytes 1769480 | tf_op jit(solution)/shard_map/ppermute | solution.py:22
  12.8 0.0 slice-start.2
  12.8 0.0 copy-start.5
  12.9 0.0 copy-start.6
  12.9 0.0 copy-start.7
  12.9 0.0 copy-start.8
  12.9 0.0 slice-start.3
  12.9 0.0 copy-start
  12.9 0.0 copy-start.1
  12.9 0.0 copy-start.2
  12.9 0.0 collective-permute-done.prev1
  13.0 3.7 %collective-permute-start.2 = (bf16[288,128]{1,0:T(8,128)(2,1)S(1)}, bf16[288,128]{1,0:T(8,128)(2,1)S(1)}, u32[]{:S(2)}, u32[]{:S(2)}) collective-permute-start(bf16[288,128]{1,0:T(8,128)(2,1)S(1)} %get-tuple-element.25), channel_id=1, source_target_pairs={{0,1},{1,2},{2,3},{4,5},{5,6},{6,7},{8,9},{9,10},{10,11},{12,13},{... | collective-permute-start | bytes 221192 | tf_op jit(solution)/shard_map/ppermute | solution.py:17
  16.7 1.3 %collective-permute-start.3 = (bf16[288,128]{1,0:T(8,128)(2,1)S(1)}, bf16[288,128]{1,0:T(8,128)(2,1)S(1)}, u32[]{:S(2)}, u32[]{:S(2)}) collective-permute-start(bf16[288,128]{1,0:T(8,128)(2,1)S(1)} %get-tuple-element.26), channel_id=1, source_target_pairs={{1,0},{2,1},{3,2},{5,4},{6,5},{7,6},{9,8},{10,9},{11,10},{13,12},{... | collective-permute-start | bytes 221192 | tf_op jit(solution)/shard_map/ppermute | solution.py:17
  18.0 0.1 pad_maximum_fusion.1
  18.1 1.3 %collective-permute-start.5 = (bf16[2,3,128,384]{3,2,1,0:T(8,128)(2,1)S(1)}, bf16[2,3,128,384]{3,2,1,0:T(8,128)(2,1)S(1)}, u32[]{:S(2)}, u32[]{:S(2)}) collective-permute-start(bf16[2,3,128,384]{3,2,1,0:T(8,128)(2,1)S(1)} %pad_maximum_fusion.1), channel_id=1, source_target_pairs={{1,0},{2,1},{3,2}} | collective-permute-start | bytes 1769480 | tf_op jit(solution)/shard_map/ppermute | solution.py:22
  19.5 2.5 %first_kernels.1 = (bf16[2,9,384,384]{3,2,1,0:T(8,128)(2,1)S(1)}, bf16[768,768]{1,0:T(8,128)(2,1)S(1)}, bf16[2,4,128,384]{3,2,1,0:T(8,128)(2,1)S(1)}, bf16[2,4,128,384]{3,2,1,0:T(8,128)(2,1)S(1)}) custom-call(bf16[9,3,384,384]{3,2,1,0:T(8,128)(2,1)S(1)} %bitcast.16, bf16[432,384]{1,0:T(8,128)(2,1)S(1)} %bitcast.19, bf16[2,4,128,384]{3,2,1,0:T(8,128)(2,1)S(1)} %copy-done, ...), custom_call_target="tpu_custom_call" | custom-call | flops 7962624 | bytes 13271040 | tf_op jit(solution)/shard_map/first_kernels/pallas_call | solution.py:210
  22.1 0.9 %collective-permute-done.3.dn = bf16[288,128]{1,0:T(8,128)(2,1)S(1)} collective-permute-done((bf16[288,128]{1,0:T(8,128)(2,1)S(1)}, bf16[288,128]{1,0:T(8,128)(2,1)S(1)}, u32[]{:S(2)}, u32[]{:S(2)}) %collective-permute-start.3) | collective-permute-done | bytes 73760 | tf_op jit(solution)/shard_map/ppermute | solution.py:17
  23.0 3.9 %projection.1 = (bf16[4,512,768]{2,1,0:T(8,128)(2,1)S(1)}, bf16[4,8,64,384]{3,2,1,0:T(8,128)(2,1)S(1)}, bf16[4,8,64,384]{3,2,1,0:T(8,128)(2,1)S(1)}, bf16[2,4,128,384]{3,2,1,0:T(8,128)(2,1)S(1)}) custom-call(bf16[256,128]{1,0:T(8,128)(2,1)S(1)} %pad_maximum_fusion.2.both, bf16[128,128]{1,0:T(8,128)(2,1)S(1)} %get-tuple-element.23.prev1, ...), custom_call_target="tpu_custom_call" | custom-call | flops 6000000000 | bytes 6000000 | tf_op jit(solution)/shard_map/projection/pallas_call | solution.py:602
  26.9 6.1 %first_part.1 = (bf16[2,3,128,384]{3,2,1,0:T(8,128)(2,1)S(1)}, bf16[4,5,64,384]{3,2,1,0:T(8,128)(2,1)S(1)}, bf16[4,5,64,384]{3,2,1,0:T(8,128)(2,1)S(1)}) custom-call(bf16[4,512,768]{2,1,0:T(8,128)(2,1)S(1)} %get-tuple-element.28.hs, bf16[4,8,64,384]{3,2,1,0:T(8,128)(2,1)S(1)} %get-tuple-element.29.v2, bf16[4,8,64,384]{3,2,1,0:T(8,128)(2,1)S(1)} %get-tuple-element.30.v3, ...), custom_call_target="tpu_custom_call" | custom-call | flops 8000000000 | bytes 8000000 | tf_op jit(solution)/shard_map/first_part/pallas_call | solution.py:620
  33.0 1.3 %collective-permute-start.6 = (bf16[2,3,128,384]{3,2,1,0:T(8,128)(2,1)S(1)}, bf16[2,3,128,384]{3,2,1,0:T(8,128)(2,1)S(1)}, u32[]{:S(2)}, u32[]{:S(2)}) collective-permute-start(bf16[2,3,128,384]{3,2,1,0:T(8,128)(2,1)S(1)} %get-tuple-element.33.n2a), channel_id=1, source_target_pairs={{0,4},{4,8},{8,12},{12,16},{16,20},{20,24},{24,28},{1,5},{5,9},{9,... | collective-permute-start | bytes 1769480 | tf_op jit(solution)/shard_map/ppermute | solution.py:17
  34.3 0.0 slice-start
  34.3 0.0 copy-start.9
  34.4 6.0 %second_part.1.n2b = bf16[2,3,128,384]{3,2,1,0:T(8,128)(2,1)S(1)} custom-call(bf16[4,512,768]{2,1,0:T(8,128)(2,1)S(1)} %get-tuple-element.28.hs, bf16[4,5,64,384]{3,2,1,0:T(8,128)(2,1)S(1)} %get-tuple-element.34.v0, bf16[4,5,64,384]{3,2,1,0:T(8,128)(2,1)S(1)} %get-tuple-element.35.v1, bf16[4,8,64,384]{3,2,1,0:T(8,128)(2,1)S(1)} %get-tuple-element.29.v2, ...), custom_call_target="tpu_custom_call" | custom-call | flops 200000000 | bytes 200000 | tf_op jit(solution)/shard_map/second_part/pallas_call | solution.py:637
  40.4 1.6 %collective-permute-start.7 = (bf16[2,3,128,384]{3,2,1,0:T(8,128)(2,1)S(1)}, bf16[2,3,128,384]{3,2,1,0:T(8,128)(2,1)S(1)}, u32[]{:S(2)}, u32[]{:S(2)}) collective-permute-start(bf16[2,3,128,384]{3,2,1,0:T(8,128)(2,1)S(1)} %second_part.1.n2b), channel_id=1, source_target_pairs={{0,4},{4,8},{8,12},{12,16},{16,20},{20,24},{24,28},{1,5},{5,9},{9,... | collective-permute-start | bytes 1769480 | tf_op jit(solution)/shard_map/ppermute | solution.py:17
  42.0 1.8 %summed_kernels.1.u = bf16[2,9,384,384]{3,2,1,0:T(8,128)(2,1)S(1)} custom-call(bf16[9,3,384,384]{3,2,1,0:T(8,128)(2,1)S(1)} %bitcast.11), custom_call_target="tpu_custom_call" | custom-call | flops 7962624 | bytes 13271040 | tf_op jit(solution)/shard_map/summed_kernels/pallas_call | solution.py:228
  43.9 4.1 %own_frames.1 = (f32[2,4,128,384]{3,2,1,0:T(8,128)S(1)}, bf16[4,3,64,384]{3,2,1,0:T(8,128)(2,1)S(1)}, bf16[4,3,64,384]{3,2,1,0:T(8,128)(2,1)S(1)}) custom-call(bf16[2,3,128,384]{3,2,1,0:T(8,128)(2,1)S(1)} %get-tuple-element.33.n2a, bf16[2,3,128,384]{3,2,1,0:T(8,128)(2,1)S(1)} %second_part.1.n2b, bf16[2,3,128,384]{3,2,1,0:T(8,128)(2,1)S(1)} %collective-permute-done.6.earlier, ...), custom_call_target="tpu_custom_call" | custom-call | flops 4000000000 | bytes 4000000 | tf_op jit(solution)/shard_map/own_frames/pallas_call | solution.py:656
  48.0 5.1 %earlier_frames.1 = bf16[2,4,128,384]{3,2,1,0:T(8,128)(2,1)} custom-call(bf16[4,3,64,384]{3,2,1,0:T(8,128)(2,1)S(1)} %get-tuple-element.38.ve0, bf16[4,3,64,384]{3,2,1,0:T(8,128)(2,1)S(1)} %get-tuple-element.39.ve1, bf16[2,3,128,384]{3,2,1,0:T(8,128)(2,1)S(1)} %collective-permute-done.7.earlier, bf16[2,4,128,384]{3,2,1,0:T(8,128)(2,1)S(1)} %get-tuple-element.36.placed, ...), custom_call_target="tpu_custom_call" | custom-call | flops 4000000000 | bytes 4000000 | tf_op jit(solution)/shard_map/earlier_frames/pallas_call | solution.py:674
  (32 shorter events, 0.1 us)
Async XLA Ops:
  0.0 12.8 %copy-start.4 = (bf16[2,4,128,16]{2,3,1,0:T(8,128)(2,1)S(1)}, bf16[2,4,128,16]{2,3,1,0:T(8,128)(2,1)}, u32[]{:S(2)}) copy-start(bf16[2,4,128,16]{2,3,1,0:T(8,128)(2,1)} %param.12) | copy-start | bytes 98308
  0.0 12.8 %copy-start.3 = (bf16[2,4,128,16]{2,3,1,0:T(8,128)(2,1)S(1)}, bf16[2,4,128,16]{2,3,1,0:T(8,128)(2,1)}, u32[]{:S(2)}) copy-start(bf16[2,4,128,16]{2,3,1,0:T(8,128)(2,1)} %param.13) | copy-start | bytes 98308
  0.0 12.9 %collective-permute-start = (bf16[128,128]{1,0:T(8,128)(2,1)}, bf16[128,128]{1,0:T(8,128)(2,1)S(1)}, u32[]{:S(2)}, u32[]{:S(2)}) collective-permute-start(bf16[128,128]{1,0:T(8,128)(2,1)} %bitcast.21), channel_id=1, source_target_pairs={{0,4},{4,8},{8,12},{12,16},{16,20},{20,24},{24,28},{1,5},{5,9},{9,... | collective-permute-start | bytes 98312 | tf_op jit(solution)/shard_map/ppermute | solution.py:17
  2.5 10.5 %collective-permute-start.1 = (bf16[128,128]{1,0:T(8,128)(2,1)}, bf16[128,128]{1,0:T(8,128)(2,1)S(1)}, u32[]{:S(2)}, u32[]{:S(2)}) collective-permute-start(bf16[128,128]{1,0:T(8,128)(2,1)} %bitcast.22), channel_id=1, source_target_pairs={{0,8},{4,12},{8,16},{12,20},{16,24},{20,28},{1,9},{5,13},{9,17},{1... | collective-permute-start | bytes 98312 | tf_op jit(solution)/shard_map/ppermute | solution.py:17
  9.3 17.6 %collective-permute-start.4 = (bf16[2,3,128,384]{3,2,1,0:T(8,128)(2,1)S(1)}, bf16[2,3,128,384]{3,2,1,0:T(8,128)(2,1)S(1)}, u32[]{:S(2)}, u32[]{:S(2)}) collective-permute-start(bf16[2,3,128,384]{3,2,1,0:T(8,128)(2,1)S(1)} %pad_maximum_fusion), channel_id=1, source_target_pairs={{0,1},{1,2},{2,3}} | collective-permute-start | bytes 1769480 | tf_op jit(solution)/shard_map/ppermute | solution.py:22
  12.8 6.7 %slice-start.2 = ((s8[7962624]{0:T(1024)(128)(4,1)}), s8[4194304]{0:T(1024)(128)(4,1)S(1)}, s32[]{:S(2)}) async-start(s8[7962624]{0:T(1024)(128)(4,1)} %bitcast.14), calls=%async_computation.2 | async-start | bytes 8388608
  12.8 6.6 %copy-start.5 = (f32[384]{0:T(512)S(1)}, f32[384]{0:T(512)}, u32[]{:S(2)}) copy-start(f32[384]{0:T(512)} %param.17) | copy-start | bytes 4612
  12.9 6.6 %copy-start.6 = (f32[384]{0:T(512)S(1)}, f32[384]{0:T(512)}, u32[]{:S(2)}) copy-start(f32[384]{0:T(512)} %param.18) | copy-start | bytes 4612
  12.9 6.6 %copy-start.7 = (f32[384]{0:T(512)S(1)}, f32[384]{0:T(512)}, u32[]{:S(2)}) copy-start(f32[384]{0:T(512)} %param.20) | copy-start | bytes 4612
  12.9 6.6 %copy-start.8 = (f32[384]{0:T(512)S(1)}, f32[384]{0:T(512)}, u32[]{:S(2)}) copy-start(f32[384]{0:T(512)} %param.21) | copy-start | bytes 4612
  12.9 6.6 %slice-start.3 = ((s8[7962624]{0:T(1024)(128)(4,1)}), s8[3768320]{0:T(1024)(128)(4,1)S(1)}, s32[]{:S(2)}) async-start(s8[7962624]{0:T(1024)(128)(4,1)} %bitcast.14), calls=%async_computation.3 | async-start | bytes 7536640
  12.9 6.6 %copy-start = (bf16[2,4,128,384]{3,2,1,0:T(8,128)(2,1)S(1)}, bf16[2,4,128,384]{3,2,1,0:T(8,128)(2,1)}, u32[]{:S(2)}) copy-start(bf16[2,4,128,384]{3,2,1,0:T(8,128)(2,1)} %cache_one.1) | copy-start | bytes 2359300
  12.9 6.6 %copy-start.1 = (bf16[2,4,128,384]{3,2,1,0:T(8,128)(2,1)S(1)}, bf16[2,4,128,384]{3,2,1,0:T(8,128)(2,1)}, u32[]{:S(2)}) copy-start(bf16[2,4,128,384]{3,2,1,0:T(8,128)(2,1)} %cache_two.1) | copy-start | bytes 2359300
  12.9 6.6 %copy-start.2 = (bf16[3,3,3,16,384]{4,3,2,1,0:T(8,128)(2,1)S(1)}, bf16[3,3,3,16,384]{4,3,2,1,0:T(8,128)(2,1)}, u32[]{:S(2)}) copy-start(bf16[3,3,3,16,384]{4,3,2,1,0:T(8,128)(2,1)} %param.16) | copy-start | bytes 995332
  13.0 9.1 %collective-permute-start.2 = (bf16[288,128]{1,0:T(8,128)(2,1)S(1)}, bf16[288,128]{1,0:T(8,128)(2,1)S(1)}, u32[]{:S(2)}, u32[]{:S(2)}) collective-permute-start(bf16[288,128]{1,0:T(8,128)(2,1)S(1)} %get-tuple-element.25), channel_id=1, source_target_pairs={{0,1},{1,2},{2,3},{4,5},{5,6},{6,7},{8,9},{9,10},{10,11},{12,13},{... | collective-permute-start | bytes 221192 | tf_op jit(solution)/shard_map/ppermute | solution.py:17
  16.7 6.2 %collective-permute-start.3 = (bf16[288,128]{1,0:T(8,128)(2,1)S(1)}, bf16[288,128]{1,0:T(8,128)(2,1)S(1)}, u32[]{:S(2)}, u32[]{:S(2)}) collective-permute-start(bf16[288,128]{1,0:T(8,128)(2,1)S(1)} %get-tuple-element.26), channel_id=1, source_target_pairs={{1,0},{2,1},{3,2},{5,4},{6,5},{7,6},{9,8},{10,9},{11,10},{13,12},{... | collective-permute-start | bytes 221192 | tf_op jit(solution)/shard_map/ppermute | solution.py:17
  18.1 16.2 %collective-permute-start.5 = (bf16[2,3,128,384]{3,2,1,0:T(8,128)(2,1)S(1)}, bf16[2,3,128,384]{3,2,1,0:T(8,128)(2,1)S(1)}, u32[]{:S(2)}, u32[]{:S(2)}) collective-permute-start(bf16[2,3,128,384]{3,2,1,0:T(8,128)(2,1)S(1)} %pad_maximum_fusion.1), channel_id=1, source_target_pairs={{1,0},{2,1},{3,2}} | collective-permute-start | bytes 1769480 | tf_op jit(solution)/shard_map/ppermute | solution.py:22
  33.0 10.9 %collective-permute-start.6 = (bf16[2,3,128,384]{3,2,1,0:T(8,128)(2,1)S(1)}, bf16[2,3,128,384]{3,2,1,0:T(8,128)(2,1)S(1)}, u32[]{:S(2)}, u32[]{:S(2)}) collective-permute-start(bf16[2,3,128,384]{3,2,1,0:T(8,128)(2,1)S(1)} %get-tuple-element.33.n2a), channel_id=1, source_target_pairs={{0,4},{4,8},{8,12},{12,16},{16,20},{20,24},{24,28},{1,5},{5,9},{9,... | collective-permute-start | bytes 1769480 | tf_op jit(solution)/shard_map/ppermute | solution.py:17
  34.3 7.6 %slice-start = ((s8[7962624]{0:T(1024)(128)(4,1)}), s8[4194304]{0:T(1024)(128)(4,1)S(1)}, s32[]{:S(2)}) async-start(s8[7962624]{0:T(1024)(128)(4,1)} %bitcast.9), calls=%async_computation | async-start | bytes 8388608
  34.3 7.6 %copy-start.9 = (f32[384]{0:T(512)S(1)}, f32[384]{0:T(512)}, u32[]{:S(2)}) copy-start(f32[384]{0:T(512)} %param.23) | copy-start | bytes 4612
  34.4 7.6 %slice-start.1 = ((s8[7962624]{0:T(1024)(128)(4,1)}), s8[3768320]{0:T(1024)(128)(4,1)S(1)}, s32[]{:S(2)}) async-start(s8[7962624]{0:T(1024)(128)(4,1)} %bitcast.9), calls=%async_computation.1 | async-start | bytes 7536640
  40.4 7.6 %collective-permute-start.7 = (bf16[2,3,128,384]{3,2,1,0:T(8,128)(2,1)S(1)}, bf16[2,3,128,384]{3,2,1,0:T(8,128)(2,1)S(1)}, u32[]{:S(2)}, u32[]{:S(2)}) collective-permute-start(bf16[2,3,128,384]{3,2,1,0:T(8,128)(2,1)S(1)} %second_part.1.n2b), channel_id=1, source_target_pairs={{0,4},{4,8},{8,12},{12,16},{16,20},{20,24},{24,28},{1,5},{5,9},{9,... | collective-permute-start | bytes 1769480 | tf_op jit(solution)/shard_map/ppermute | solution.py:17

commit v7 on v6

--- a/solution.py
+++ b/solution.py
@@ -48,7 +48,7 @@
     )
     odd_before, odd = odd_before.astype(BF), odd.astype(BF)
     even, even_after = even.astype(BF), even_after.astype(BF)
-    return odd_before - odd, even + odd, odd - even, even - even_after
+    return odd_before - odd, 0.5 * (even + odd), 0.5 * (odd - even), even - even_after
 
 
 def dot(a, b):
@@ -167,8 +167,8 @@
 
 
 def sum_taps(w, u, i):
-    s = 0.5 * (w[i, 0].astype(F32) + w[i, 2].astype(F32))
-    h = 0.5 * w[i, 1].astype(F32)
+    s = w[i, 0].astype(F32) + w[i, 2].astype(F32)
+    h = w[i, 1].astype(F32)
     u[0, i] = (s + h).astype(BF)
     u[1, i] = (s - h).astype(BF)
 

time: 53.6 us -> 53.7 us (level)
  Pallas kernels: 29.6 us -> 29 us
  transfers between devices with their start and end apart: 8 -> 8, of which waited for: 1 -> 1; matrix products, arithmetic and copies ran while one was open for 5% -> 5% of each run, Pallas kernels for 46% -> 45%
where the time goes in v7:
time: 53.7 us; the launch traced here: 52.8 us
  Pallas kernels  29 us (54%)
  starting transfers between devices  19.6 us (36%)
  local copies, waits for them, and re-layouts  2.38 us (4%)
  waiting for transfers between devices  1.29 us (2%)
    ppermute x6, starting transfers between devices, shifted(): lax.ppermute(x, axis, [(i, i + by) for i in range(count) if 0 <= i + by <...  14.8 us
    pallas_call x1, Pallas kernels, on_device(): pl.pallas_call(functools.partial(first_part_body, tiles), out_shape=[norm...  6.12 us
    pallas_call x1, Pallas kernels, on_device(): pl.pallas_call(functools.partial(second_part_body, tiles), out_shape=norm...  6.01 us
    pallas_call x1, Pallas kernels, on_device(): pl.pallas_call(earlier_frames_body, out_shape=jax.ShapeDtypeStruct((2, ro...  5.09 us
    ppermute x2, starting transfers between devices, first_frames_only(): lax.ppermute(x, ('tm', 'tile'), [(i, i + by) for i in range(rows) if 0 <=...  4.81 us
    pallas_call x1, Pallas kernels, on_device(): pl.pallas_call(own_frames_body, out_shape=[jax.ShapeDtypeStruct((2, rows,...  4.15 us
    pallas_call x1, Pallas kernels, on_device(): pl.pallas_call(functools.partial(projection_body, tiles), out_shape=[jax....  3.95 us
    slice x2, local copies, waits for them, and re-layouts, on_device(): caches = jnp.concatenate([cache_one[:, :2], cache_two[:, :1]], 1)  2.27 us
  transfers between devices with their start and end apart: 8, of which 1 were waited for; matrix products, arithmetic and copies ran while one was open for 5% of the time, Pallas kernels for 45%

profile of v7, /device:TPU:0, one launch (start us, length us, event | category | flops | bytes accessed | tf_op | source)
XLA Modules:
  0.0 52.8 jit_solution(16990563626007009912)
XLA Ops:
  0.0 2.5 %collective-permute-start = (bf16[128,128]{1,0:T(8,128)(2,1)}, bf16[128,128]{1,0:T(8,128)(2,1)S(1)}, u32[]{:S(2)}, u32[]{:S(2)}) collective-permute-start(bf16[128,128]{1,0:T(8,128)(2,1)} %bitcast.21), channel_id=1, source_target_pairs={{0,4},{4,8},{8,12},{12,16},{16,20},{20,24},{24,28},{1,5},{5,9},{9,... | collective-permute-start | bytes 98312 | tf_op jit(solution)/shard_map/ppermute | solution.py:17
  2.5 4.4 %collective-permute-start.1 = (bf16[128,128]{1,0:T(8,128)(2,1)}, bf16[128,128]{1,0:T(8,128)(2,1)S(1)}, u32[]{:S(2)}, u32[]{:S(2)}) collective-permute-start(bf16[128,128]{1,0:T(8,128)(2,1)} %bitcast.22), channel_id=1, source_target_pairs={{0,8},{4,12},{8,16},{12,20},{16,24},{20,28},{1,9},{5,13},{9,17},{1... | collective-permute-start | bytes 98312 | tf_op jit(solution)/shard_map/ppermute | solution.py:17
  6.9 1.1 %fusion.1 = (bf16[2,1,128,384]{3,2,1,0:T(8,128)(2,1)S(1)}, bf16[2,1,128,384]{3,2,1,0:T(8,128)(2,1)S(1)}) fusion(bf16[2,4,128,384]{3,2,1,0:T(8,128)(2,1)} %cache_two.1), kind=kLoop, calls=%fused_computation.4 | loop fusion | bytes 786432 | tf_op jit(solution)/shard_map/slice | solution.py:591
  8.0 1.2 %fusion = (bf16[2,2,128,384]{3,2,1,0:T(8,128)(2,1)S(1)}, bf16[2,2,128,384]{3,2,1,0:T(8,128)(2,1)S(1)}) fusion(bf16[2,4,128,384]{3,2,1,0:T(8,128)(2,1)} %cache_one.1), kind=kLoop, calls=%fused_computation.3 | loop fusion | bytes 1572864 | tf_op jit(solution)/shard_map/slice | solution.py:591
  9.2 0.1 pad_maximum_fusion
  9.3 3.5 %collective-permute-start.4 = (bf16[2,3,128,384]{3,2,1,0:T(8,128)(2,1)S(1)}, bf16[2,3,128,384]{3,2,1,0:T(8,128)(2,1)S(1)}, u32[]{:S(2)}, u32[]{:S(2)}) collective-permute-start(bf16[2,3,128,384]{3,2,1,0:T(8,128)(2,1)S(1)} %pad_maximum_fusion), channel_id=1, source_target_pairs={{0,1},{1,2},{2,3}} | collective-permute-start | bytes 1769480 | tf_op jit(solution)/shard_map/ppermute | solution.py:22
  12.8 0.0 slice-start.2
  12.8 0.0 copy-start.5
  12.9 0.0 copy-start.6
  12.9 0.0 copy-start.7
  12.9 0.0 copy-start.8
  12.9 0.0 slice-start.3
  12.9 0.0 copy-start
  12.9 0.0 copy-start.1
  12.9 0.0 copy-start.2
  13.0 3.7 %collective-permute-start.2 = (bf16[288,128]{1,0:T(8,128)(2,1)S(1)}, bf16[288,128]{1,0:T(8,128)(2,1)S(1)}, u32[]{:S(2)}, u32[]{:S(2)}) collective-permute-start(bf16[288,128]{1,0:T(8,128)(2,1)S(1)} %get-tuple-element.25), channel_id=1, source_target_pairs={{0,1},{1,2},{2,3},{4,5},{5,6},{6,7},{8,9},{9,10},{10,11},{12,13},{... | collective-permute-start | bytes 221192 | tf_op jit(solution)/shard_map/ppermute | solution.py:17
  16.7 1.3 %collective-permute-start.3 = (bf16[288,128]{1,0:T(8,128)(2,1)S(1)}, bf16[288,128]{1,0:T(8,128)(2,1)S(1)}, u32[]{:S(2)}, u32[]{:S(2)}) collective-permute-start(bf16[288,128]{1,0:T(8,128)(2,1)S(1)} %get-tuple-element.26), channel_id=1, source_target_pairs={{1,0},{2,1},{3,2},{5,4},{6,5},{7,6},{9,8},{10,9},{11,10},{13,12},{... | collective-permute-start | bytes 221192 | tf_op jit(solution)/shard_map/ppermute | solution.py:17
  18.0 0.1 pad_maximum_fusion.1
  18.1 1.3 %collective-permute-start.5 = (bf16[2,3,128,384]{3,2,1,0:T(8,128)(2,1)S(1)}, bf16[2,3,128,384]{3,2,1,0:T(8,128)(2,1)S(1)}, u32[]{:S(2)}, u32[]{:S(2)}) collective-permute-start(bf16[2,3,128,384]{3,2,1,0:T(8,128)(2,1)S(1)} %pad_maximum_fusion.1), channel_id=1, source_target_pairs={{1,0},{2,1},{3,2}} | collective-permute-start | bytes 1769480 | tf_op jit(solution)/shard_map/ppermute | solution.py:22
  19.5 2.1 %first_kernels.1 = (bf16[2,9,384,384]{3,2,1,0:T(8,128)(2,1)S(1)}, bf16[768,768]{1,0:T(8,128)(2,1)S(1)}, bf16[2,4,128,384]{3,2,1,0:T(8,128)(2,1)S(1)}, bf16[2,4,128,384]{3,2,1,0:T(8,128)(2,1)S(1)}) custom-call(bf16[9,3,384,384]{3,2,1,0:T(8,128)(2,1)S(1)} %bitcast.16, bf16[432,384]{1,0:T(8,128)(2,1)S(1)} %bitcast.19, bf16[2,4,128,384]{3,2,1,0:T(8,128)(2,1)S(1)} %copy-done, ...), custom_call_target="tpu_custom_call" | custom-call | flops 7962624 | bytes 13271040 | tf_op jit(solution)/shard_map/first_kernels/pallas_call | solution.py:210
  21.7 0.0 collective-permute-done.2.up
  21.7 1.3 %collective-permute-done.3.dn = bf16[288,128]{1,0:T(8,128)(2,1)S(1)} collective-permute-done((bf16[288,128]{1,0:T(8,128)(2,1)S(1)}, bf16[288,128]{1,0:T(8,128)(2,1)S(1)}, u32[]{:S(2)}, u32[]{:S(2)}) %collective-permute-start.3) | collective-permute-done | bytes 73760 | tf_op jit(solution)/shard_map/ppermute | solution.py:17
  23.0 4.0 %projection.1 = (bf16[4,512,768]{2,1,0:T(8,128)(2,1)S(1)}, bf16[4,8,64,384]{3,2,1,0:T(8,128)(2,1)S(1)}, bf16[4,8,64,384]{3,2,1,0:T(8,128)(2,1)S(1)}, bf16[2,4,128,384]{3,2,1,0:T(8,128)(2,1)S(1)}) custom-call(bf16[256,128]{1,0:T(8,128)(2,1)S(1)} %pad_maximum_fusion.2.both, bf16[128,128]{1,0:T(8,128)(2,1)S(1)} %get-tuple-element.23.prev1, ...), custom_call_target="tpu_custom_call" | custom-call | flops 6000000000 | bytes 6000000 | tf_op jit(solution)/shard_map/projection/pallas_call | solution.py:602
  26.9 6.1 %first_part.1 = (bf16[2,3,128,384]{3,2,1,0:T(8,128)(2,1)S(1)}, bf16[4,5,64,384]{3,2,1,0:T(8,128)(2,1)S(1)}, bf16[4,5,64,384]{3,2,1,0:T(8,128)(2,1)S(1)}) custom-call(bf16[4,512,768]{2,1,0:T(8,128)(2,1)S(1)} %get-tuple-element.28.hs, bf16[4,8,64,384]{3,2,1,0:T(8,128)(2,1)S(1)} %get-tuple-element.29.v2, bf16[4,8,64,384]{3,2,1,0:T(8,128)(2,1)S(1)} %get-tuple-element.30.v3, ...), custom_call_target="tpu_custom_call" | custom-call | flops 8000000000 | bytes 8000000 | tf_op jit(solution)/shard_map/first_part/pallas_call | solution.py:620
  33.1 1.3 %collective-permute-start.6 = (bf16[2,3,128,384]{3,2,1,0:T(8,128)(2,1)S(1)}, bf16[2,3,128,384]{3,2,1,0:T(8,128)(2,1)S(1)}, u32[]{:S(2)}, u32[]{:S(2)}) collective-permute-start(bf16[2,3,128,384]{3,2,1,0:T(8,128)(2,1)S(1)} %get-tuple-element.33.n2a), channel_id=1, source_target_pairs={{0,4},{4,8},{8,12},{12,16},{16,20},{20,24},{24,28},{1,5},{5,9},{9,... | collective-permute-start | bytes 1769480 | tf_op jit(solution)/shard_map/ppermute | solution.py:17
  34.4 0.0 slice-start
  34.4 0.0 copy-start.9
  34.5 6.0 %second_part.1.n2b = bf16[2,3,128,384]{3,2,1,0:T(8,128)(2,1)S(1)} custom-call(bf16[4,512,768]{2,1,0:T(8,128)(2,1)S(1)} %get-tuple-element.28.hs, bf16[4,5,64,384]{3,2,1,0:T(8,128)(2,1)S(1)} %get-tuple-element.34.v0, bf16[4,5,64,384]{3,2,1,0:T(8,128)(2,1)S(1)} %get-tuple-element.35.v1, bf16[4,8,64,384]{3,2,1,0:T(8,128)(2,1)S(1)} %get-tuple-element.29.v2, ...), custom_call_target="tpu_custom_call" | custom-call | flops 200000000 | bytes 200000 | tf_op jit(solution)/shard_map/second_part/pallas_call | solution.py:637
  40.5 1.6 %collective-permute-start.7 = (bf16[2,3,128,384]{3,2,1,0:T(8,128)(2,1)S(1)}, bf16[2,3,128,384]{3,2,1,0:T(8,128)(2,1)S(1)}, u32[]{:S(2)}, u32[]{:S(2)}) collective-permute-start(bf16[2,3,128,384]{3,2,1,0:T(8,128)(2,1)S(1)} %second_part.1.n2b), channel_id=1, source_target_pairs={{0,4},{4,8},{8,12},{12,16},{16,20},{20,24},{24,28},{1,5},{5,9},{9,... | collective-permute-start | bytes 1769480 | tf_op jit(solution)/shard_map/ppermute | solution.py:17
  42.1 1.5 %summed_kernels.1.u = bf16[2,9,384,384]{3,2,1,0:T(8,128)(2,1)S(1)} custom-call(bf16[9,3,384,384]{3,2,1,0:T(8,128)(2,1)S(1)} %bitcast.11), custom_call_target="tpu_custom_call" | custom-call | flops 7962624 | bytes 13271040 | tf_op jit(solution)/shard_map/summed_kernels/pallas_call | solution.py:228
  43.6 4.1 %own_frames.1 = (f32[2,4,128,384]{3,2,1,0:T(8,128)S(1)}, bf16[4,3,64,384]{3,2,1,0:T(8,128)(2,1)S(1)}, bf16[4,3,64,384]{3,2,1,0:T(8,128)(2,1)S(1)}) custom-call(bf16[2,3,128,384]{3,2,1,0:T(8,128)(2,1)S(1)} %get-tuple-element.33.n2a, bf16[2,3,128,384]{3,2,1,0:T(8,128)(2,1)S(1)} %second_part.1.n2b, bf16[2,3,128,384]{3,2,1,0:T(8,128)(2,1)S(1)} %collective-permute-done.6.earlier, ...), custom_call_target="tpu_custom_call" | custom-call | flops 4000000000 | bytes 4000000 | tf_op jit(solution)/shard_map/own_frames/pallas_call | solution.py:656
  47.7 5.1 %earlier_frames.1 = bf16[2,4,128,384]{3,2,1,0:T(8,128)(2,1)} custom-call(bf16[4,3,64,384]{3,2,1,0:T(8,128)(2,1)S(1)} %get-tuple-element.38.ve0, bf16[4,3,64,384]{3,2,1,0:T(8,128)(2,1)S(1)} %get-tuple-element.39.ve1, bf16[2,3,128,384]{3,2,1,0:T(8,128)(2,1)S(1)} %collective-permute-done.7.earlier, bf16[2,4,128,384]{3,2,1,0:T(8,128)(2,1)S(1)} %get-tuple-element.36.placed, ...), custom_call_target="tpu_custom_call" | custom-call | flops 4000000000 | bytes 4000000 | tf_op jit(solution)/shard_map/earlier_frames/pallas_call | solution.py:674
  (32 shorter events, 0.1 us)
Async XLA Ops:
  0.0 12.8 %copy-start.4 = (bf16[2,4,128,16]{2,3,1,0:T(8,128)(2,1)S(1)}, bf16[2,4,128,16]{2,3,1,0:T(8,128)(2,1)}, u32[]{:S(2)}) copy-start(bf16[2,4,128,16]{2,3,1,0:T(8,128)(2,1)} %param.12) | copy-start | bytes 98308
  0.0 12.8 %copy-start.3 = (bf16[2,4,128,16]{2,3,1,0:T(8,128)(2,1)S(1)}, bf16[2,4,128,16]{2,3,1,0:T(8,128)(2,1)}, u32[]{:S(2)}) copy-start(bf16[2,4,128,16]{2,3,1,0:T(8,128)(2,1)} %param.13) | copy-start | bytes 98308
  0.0 12.9 %collective-permute-start = (bf16[128,128]{1,0:T(8,128)(2,1)}, bf16[128,128]{1,0:T(8,128)(2,1)S(1)}, u32[]{:S(2)}, u32[]{:S(2)}) collective-permute-start(bf16[128,128]{1,0:T(8,128)(2,1)} %bitcast.21), channel_id=1, source_target_pairs={{0,4},{4,8},{8,12},{12,16},{16,20},{20,24},{24,28},{1,5},{5,9},{9,... | collective-permute-start | bytes 98312 | tf_op jit(solution)/shard_map/ppermute | solution.py:17
  2.5 10.5 %collective-permute-start.1 = (bf16[128,128]{1,0:T(8,128)(2,1)}, bf16[128,128]{1,0:T(8,128)(2,1)S(1)}, u32[]{:S(2)}, u32[]{:S(2)}) collective-permute-start(bf16[128,128]{1,0:T(8,128)(2,1)} %bitcast.22), channel_id=1, source_target_pairs={{0,8},{4,12},{8,16},{12,20},{16,24},{20,28},{1,9},{5,13},{9,17},{1... | collective-permute-start | bytes 98312 | tf_op jit(solution)/shard_map/ppermute | solution.py:17
  9.3 17.7 %collective-permute-start.4 = (bf16[2,3,128,384]{3,2,1,0:T(8,128)(2,1)S(1)}, bf16[2,3,128,384]{3,2,1,0:T(8,128)(2,1)S(1)}, u32[]{:S(2)}, u32[]{:S(2)}) collective-permute-start(bf16[2,3,128,384]{3,2,1,0:T(8,128)(2,1)S(1)} %pad_maximum_fusion), channel_id=1, source_target_pairs={{0,1},{1,2},{2,3}} | collective-permute-start | bytes 1769480 | tf_op jit(solution)/shard_map/ppermute | solution.py:22
  12.8 6.7 %slice-start.2 = ((s8[7962624]{0:T(1024)(128)(4,1)}), s8[4194304]{0:T(1024)(128)(4,1)S(1)}, s32[]{:S(2)}) async-start(s8[7962624]{0:T(1024)(128)(4,1)} %bitcast.14), calls=%async_computation.2 | async-start | bytes 8388608
  12.8 6.6 %copy-start.5 = (f32[384]{0:T(512)S(1)}, f32[384]{0:T(512)}, u32[]{:S(2)}) copy-start(f32[384]{0:T(512)} %param.17) | copy-start | bytes 4612
  12.9 6.6 %copy-start.6 = (f32[384]{0:T(512)S(1)}, f32[384]{0:T(512)}, u32[]{:S(2)}) copy-start(f32[384]{0:T(512)} %param.18) | copy-start | bytes 4612
  12.9 6.6 %copy-start.7 = (f32[384]{0:T(512)S(1)}, f32[384]{0:T(512)}, u32[]{:S(2)}) copy-start(f32[384]{0:T(512)} %param.20) | copy-start | bytes 4612
  12.9 6.6 %copy-start.8 = (f32[384]{0:T(512)S(1)}, f32[384]{0:T(512)}, u32[]{:S(2)}) copy-start(f32[384]{0:T(512)} %param.21) | copy-start | bytes 4612
  12.9 6.6 %slice-start.3 = ((s8[7962624]{0:T(1024)(128)(4,1)}), s8[3768320]{0:T(1024)(128)(4,1)S(1)}, s32[]{:S(2)}) async-start(s8[7962624]{0:T(1024)(128)(4,1)} %bitcast.14), calls=%async_computation.3 | async-start | bytes 7536640
  12.9 6.6 %copy-start = (bf16[2,4,128,384]{3,2,1,0:T(8,128)(2,1)S(1)}, bf16[2,4,128,384]{3,2,1,0:T(8,128)(2,1)}, u32[]{:S(2)}) copy-start(bf16[2,4,128,384]{3,2,1,0:T(8,128)(2,1)} %cache_one.1) | copy-start | bytes 2359300
  12.9 6.6 %copy-start.1 = (bf16[2,4,128,384]{3,2,1,0:T(8,128)(2,1)S(1)}, bf16[2,4,128,384]{3,2,1,0:T(8,128)(2,1)}, u32[]{:S(2)}) copy-start(bf16[2,4,128,384]{3,2,1,0:T(8,128)(2,1)} %cache_two.1) | copy-start | bytes 2359300
  12.9 6.6 %copy-start.2 = (bf16[3,3,3,16,384]{4,3,2,1,0:T(8,128)(2,1)S(1)}, bf16[3,3,3,16,384]{4,3,2,1,0:T(8,128)(2,1)}, u32[]{:S(2)}) copy-start(bf16[3,3,3,16,384]{4,3,2,1,0:T(8,128)(2,1)} %param.16) | copy-start | bytes 995332
  13.0 8.7 %collective-permute-start.2 = (bf16[288,128]{1,0:T(8,128)(2,1)S(1)}, bf16[288,128]{1,0:T(8,128)(2,1)S(1)}, u32[]{:S(2)}, u32[]{:S(2)}) collective-permute-start(bf16[288,128]{1,0:T(8,128)(2,1)S(1)} %get-tuple-element.25), channel_id=1, source_target_pairs={{0,1},{1,2},{2,3},{4,5},{5,6},{6,7},{8,9},{9,10},{10,11},{12,13},{... | collective-permute-start | bytes 221192 | tf_op jit(solution)/shard_map/ppermute | solution.py:17
  16.7 6.2 %collective-permute-start.3 = (bf16[288,128]{1,0:T(8,128)(2,1)S(1)}, bf16[288,128]{1,0:T(8,128)(2,1)S(1)}, u32[]{:S(2)}, u32[]{:S(2)}) collective-permute-start(bf16[288,128]{1,0:T(8,128)(2,1)S(1)} %get-tuple-element.26), channel_id=1, source_target_pairs={{1,0},{2,1},{3,2},{5,4},{6,5},{7,6},{9,8},{10,9},{11,10},{13,12},{... | collective-permute-start | bytes 221192 | tf_op jit(solution)/shard_map/ppermute | solution.py:17
  18.1 16.3 %collective-permute-start.5 = (bf16[2,3,128,384]{3,2,1,0:T(8,128)(2,1)S(1)}, bf16[2,3,128,384]{3,2,1,0:T(8,128)(2,1)S(1)}, u32[]{:S(2)}, u32[]{:S(2)}) collective-permute-start(bf16[2,3,128,384]{3,2,1,0:T(8,128)(2,1)S(1)} %pad_maximum_fusion.1), channel_id=1, source_target_pairs={{1,0},{2,1},{3,2}} | collective-permute-start | bytes 1769480 | tf_op jit(solution)/shard_map/ppermute | solution.py:22
  33.1 10.5 %collective-permute-start.6 = (bf16[2,3,128,384]{3,2,1,0:T(8,128)(2,1)S(1)}, bf16[2,3,128,384]{3,2,1,0:T(8,128)(2,1)S(1)}, u32[]{:S(2)}, u32[]{:S(2)}) collective-permute-start(bf16[2,3,128,384]{3,2,1,0:T(8,128)(2,1)S(1)} %get-tuple-element.33.n2a), channel_id=1, source_target_pairs={{0,4},{4,8},{8,12},{12,16},{16,20},{20,24},{24,28},{1,5},{5,9},{9,... | collective-permute-start | bytes 1769480 | tf_op jit(solution)/shard_map/ppermute | solution.py:17
  34.4 7.7 %slice-start = ((s8[7962624]{0:T(1024)(128)(4,1)}), s8[4194304]{0:T(1024)(128)(4,1)S(1)}, s32[]{:S(2)}) async-start(s8[7962624]{0:T(1024)(128)(4,1)} %bitcast.9), calls=%async_computation | async-start | bytes 8388608
  34.4 7.6 %copy-start.9 = (f32[384]{0:T(512)S(1)}, f32[384]{0:T(512)}, u32[]{:S(2)}) copy-start(f32[384]{0:T(512)} %param.23) | copy-start | bytes 4612
  34.4 7.6 %slice-start.1 = ((s8[7962624]{0:T(1024)(128)(4,1)}), s8[3768320]{0:T(1024)(128)(4,1)S(1)}, s32[]{:S(2)}) async-start(s8[7962624]{0:T(1024)(128)(4,1)} %bitcast.9), calls=%async_computation.1 | async-start | bytes 7536640
  40.5 7.3 %collective-permute-start.7 = (bf16[2,3,128,384]{3,2,1,0:T(8,128)(2,1)S(1)}, bf16[2,3,128,384]{3,2,1,0:T(8,128)(2,1)S(1)}, u32[]{:S(2)}, u32[]{:S(2)}) collective-permute-start(bf16[2,3,128,384]{3,2,1,0:T(8,128)(2,1)S(1)} %second_part.1.n2b), channel_id=1, source_target_pairs={{0,4},{4,8},{8,12},{12,16},{16,20},{20,24},{24,28},{1,5},{5,9},{9,... | collective-permute-start | bytes 1769480 | tf_op jit(solution)/shard_map/ppermute | solution.py:17

commit v8 on v7

--- a/solution.py
+++ b/solution.py
@@ -178,7 +178,7 @@
         sum_taps(w, u, i)
         return 0
 
-    lax.fori_loop(0, w.shape[0], tap, 0)
+    lax.fori_loop(0, w.shape[0], tap, 0, unroll=3)
 
 
 def first_kernels_body(w, w_in, cache_one, cache_two, u, w_big, placed_one, placed_two):

time: 53.7 us -> 53.7 us (level)
  no operation moved by 1% of the time
where the time goes in v8:
time: 53.7 us; the launch traced here: 52.8 us
  Pallas kernels  28.9 us (54%)
  starting transfers between devices  19.6 us (36%)
  local copies, waits for them, and re-layouts  2.38 us (4%)
  waiting for transfers between devices  1.31 us (2%)
    ppermute x6, starting transfers between devices, shifted(): lax.ppermute(x, axis, [(i, i + by) for i in range(count) if 0 <= i + by <...  14.8 us
    pallas_call x1, Pallas kernels, on_device(): pl.pallas_call(functools.partial(first_part_body, tiles), out_shape=[norm...  6.12 us
    pallas_call x1, Pallas kernels, on_device(): pl.pallas_call(functools.partial(second_part_body, tiles), out_shape=norm...  6.01 us
    pallas_call x1, Pallas kernels, on_device(): pl.pallas_call(earlier_frames_body, out_shape=jax.ShapeDtypeStruct((2, ro...  5.09 us
    ppermute x2, starting transfers between devices, first_frames_only(): lax.ppermute(x, ('tm', 'tile'), [(i, i + by) for i in range(rows) if 0 <=...  4.81 us
    pallas_call x1, Pallas kernels, on_device(): pl.pallas_call(own_frames_body, out_shape=[jax.ShapeDtypeStruct((2, rows,...  4.14 us
    pallas_call x1, Pallas kernels, on_device(): pl.pallas_call(functools.partial(projection_body, tiles), out_shape=[jax....  3.95 us
    slice x2, local copies, waits for them, and re-layouts, on_device(): caches = jnp.concatenate([cache_one[:, :2], cache_two[:, :1]], 1)  2.27 us
  transfers between devices with their start and end apart: 8, of which 1 were waited for; matrix products, arithmetic and copies ran while one was open for 5% of the time, Pallas kernels for 45%

profile of v8, /device:TPU:0, one launch (start us, length us, event | category | flops | bytes accessed | tf_op | source)
XLA Modules:
  0.0 52.8 jit_solution(4658241555337963580)
XLA Ops:
  0.0 2.5 %collective-permute-start = (bf16[128,128]{1,0:T(8,128)(2,1)}, bf16[128,128]{1,0:T(8,128)(2,1)S(1)}, u32[]{:S(2)}, u32[]{:S(2)}) collective-permute-start(bf16[128,128]{1,0:T(8,128)(2,1)} %bitcast.21), channel_id=1, source_target_pairs={{0,4},{4,8},{8,12},{12,16},{16,20},{20,24},{24,28},{1,5},{5,9},{9,... | collective-permute-start | bytes 98312 | tf_op jit(solution)/shard_map/ppermute | solution.py:17
  2.5 4.4 %collective-permute-start.1 = (bf16[128,128]{1,0:T(8,128)(2,1)}, bf16[128,128]{1,0:T(8,128)(2,1)S(1)}, u32[]{:S(2)}, u32[]{:S(2)}) collective-permute-start(bf16[128,128]{1,0:T(8,128)(2,1)} %bitcast.22), channel_id=1, source_target_pairs={{0,8},{4,12},{8,16},{12,20},{16,24},{20,28},{1,9},{5,13},{9,17},{1... | collective-permute-start | bytes 98312 | tf_op jit(solution)/shard_map/ppermute | solution.py:17
  6.9 1.1 %fusion.1 = (bf16[2,1,128,384]{3,2,1,0:T(8,128)(2,1)S(1)}, bf16[2,1,128,384]{3,2,1,0:T(8,128)(2,1)S(1)}) fusion(bf16[2,4,128,384]{3,2,1,0:T(8,128)(2,1)} %cache_two.1), kind=kLoop, calls=%fused_computation.4 | loop fusion | bytes 786432 | tf_op jit(solution)/shard_map/slice | solution.py:591
  8.0 1.2 %fusion = (bf16[2,2,128,384]{3,2,1,0:T(8,128)(2,1)S(1)}, bf16[2,2,128,384]{3,2,1,0:T(8,128)(2,1)S(1)}) fusion(bf16[2,4,128,384]{3,2,1,0:T(8,128)(2,1)} %cache_one.1), kind=kLoop, calls=%fused_computation.3 | loop fusion | bytes 1572864 | tf_op jit(solution)/shard_map/slice | solution.py:591
  9.2 0.1 pad_maximum_fusion
  9.3 3.5 %collective-permute-start.4 = (bf16[2,3,128,384]{3,2,1,0:T(8,128)(2,1)S(1)}, bf16[2,3,128,384]{3,2,1,0:T(8,128)(2,1)S(1)}, u32[]{:S(2)}, u32[]{:S(2)}) collective-permute-start(bf16[2,3,128,384]{3,2,1,0:T(8,128)(2,1)S(1)} %pad_maximum_fusion), channel_id=1, source_target_pairs={{0,1},{1,2},{2,3}} | collective-permute-start | bytes 1769480 | tf_op jit(solution)/shard_map/ppermute | solution.py:22
  12.8 0.0 slice-start.2
  12.8 0.0 copy-start.5
  12.9 0.0 copy-start.6
  12.9 0.0 copy-start.7
  12.9 0.0 copy-start.8
  12.9 0.0 slice-start.3
  12.9 0.0 copy-start
  12.9 0.0 copy-start.1
  12.9 0.0 copy-start.2
  13.0 3.7 %collective-permute-start.2 = (bf16[288,128]{1,0:T(8,128)(2,1)S(1)}, bf16[288,128]{1,0:T(8,128)(2,1)S(1)}, u32[]{:S(2)}, u32[]{:S(2)}) collective-permute-start(bf16[288,128]{1,0:T(8,128)(2,1)S(1)} %get-tuple-element.25), channel_id=1, source_target_pairs={{0,1},{1,2},{2,3},{4,5},{5,6},{6,7},{8,9},{9,10},{10,11},{12,13},{... | collective-permute-start | bytes 221192 | tf_op jit(solution)/shard_map/ppermute | solution.py:17
  16.7 1.3 %collective-permute-start.3 = (bf16[288,128]{1,0:T(8,128)(2,1)S(1)}, bf16[288,128]{1,0:T(8,128)(2,1)S(1)}, u32[]{:S(2)}, u32[]{:S(2)}) collective-permute-start(bf16[288,128]{1,0:T(8,128)(2,1)S(1)} %get-tuple-element.26), channel_id=1, source_target_pairs={{1,0},{2,1},{3,2},{5,4},{6,5},{7,6},{9,8},{10,9},{11,10},{13,12},{... | collective-permute-start | bytes 221192 | tf_op jit(solution)/shard_map/ppermute | solution.py:17
  18.0 0.1 pad_maximum_fusion.1
  18.1 1.3 %collective-permute-start.5 = (bf16[2,3,128,384]{3,2,1,0:T(8,128)(2,1)S(1)}, bf16[2,3,128,384]{3,2,1,0:T(8,128)(2,1)S(1)}, u32[]{:S(2)}, u32[]{:S(2)}) collective-permute-start(bf16[2,3,128,384]{3,2,1,0:T(8,128)(2,1)S(1)} %pad_maximum_fusion.1), channel_id=1, source_target_pairs={{1,0},{2,1},{3,2}} | collective-permute-start | bytes 1769480 | tf_op jit(solution)/shard_map/ppermute | solution.py:22
  19.5 2.1 %first_kernels.1 = (bf16[2,9,384,384]{3,2,1,0:T(8,128)(2,1)S(1)}, bf16[768,768]{1,0:T(8,128)(2,1)S(1)}, bf16[2,4,128,384]{3,2,1,0:T(8,128)(2,1)S(1)}, bf16[2,4,128,384]{3,2,1,0:T(8,128)(2,1)S(1)}) custom-call(bf16[9,3,384,384]{3,2,1,0:T(8,128)(2,1)S(1)} %bitcast.16, bf16[432,384]{1,0:T(8,128)(2,1)S(1)} %bitcast.19, bf16[2,4,128,384]{3,2,1,0:T(8,128)(2,1)S(1)} %copy-done, ...), custom_call_target="tpu_custom_call" | custom-call | flops 7962624 | bytes 13271040 | tf_op jit(solution)/shard_map/first_kernels/pallas_call | solution.py:210
  21.7 0.0 collective-permute-done.2.up
  21.7 1.3 %collective-permute-done.3.dn = bf16[288,128]{1,0:T(8,128)(2,1)S(1)} collective-permute-done((bf16[288,128]{1,0:T(8,128)(2,1)S(1)}, bf16[288,128]{1,0:T(8,128)(2,1)S(1)}, u32[]{:S(2)}, u32[]{:S(2)}) %collective-permute-start.3) | collective-permute-done | bytes 73760 | tf_op jit(solution)/shard_map/ppermute | solution.py:17
  23.0 4.0 %projection.1 = (bf16[4,512,768]{2,1,0:T(8,128)(2,1)S(1)}, bf16[4,8,64,384]{3,2,1,0:T(8,128)(2,1)S(1)}, bf16[4,8,64,384]{3,2,1,0:T(8,128)(2,1)S(1)}, bf16[2,4,128,384]{3,2,1,0:T(8,128)(2,1)S(1)}) custom-call(bf16[256,128]{1,0:T(8,128)(2,1)S(1)} %pad_maximum_fusion.2.both, bf16[128,128]{1,0:T(8,128)(2,1)S(1)} %get-tuple-element.23.prev1, ...), custom_call_target="tpu_custom_call" | custom-call | flops 6000000000 | bytes 6000000 | tf_op jit(solution)/shard_map/projection/pallas_call | solution.py:602
  26.9 6.1 %first_part.1 = (bf16[2,3,128,384]{3,2,1,0:T(8,128)(2,1)S(1)}, bf16[4,5,64,384]{3,2,1,0:T(8,128)(2,1)S(1)}, bf16[4,5,64,384]{3,2,1,0:T(8,128)(2,1)S(1)}) custom-call(bf16[4,512,768]{2,1,0:T(8,128)(2,1)S(1)} %get-tuple-element.28.hs, bf16[4,8,64,384]{3,2,1,0:T(8,128)(2,1)S(1)} %get-tuple-element.29.v2, bf16[4,8,64,384]{3,2,1,0:T(8,128)(2,1)S(1)} %get-tuple-element.30.v3, ...), custom_call_target="tpu_custom_call" | custom-call | flops 8000000000 | bytes 8000000 | tf_op jit(solution)/shard_map/first_part/pallas_call | solution.py:620
  33.1 1.3 %collective-permute-start.6 = (bf16[2,3,128,384]{3,2,1,0:T(8,128)(2,1)S(1)}, bf16[2,3,128,384]{3,2,1,0:T(8,128)(2,1)S(1)}, u32[]{:S(2)}, u32[]{:S(2)}) collective-permute-start(bf16[2,3,128,384]{3,2,1,0:T(8,128)(2,1)S(1)} %get-tuple-element.33.n2a), channel_id=1, source_target_pairs={{0,4},{4,8},{8,12},{12,16},{16,20},{20,24},{24,28},{1,5},{5,9},{9,... | collective-permute-start | bytes 1769480 | tf_op jit(solution)/shard_map/ppermute | solution.py:17
  34.4 0.0 slice-start
  34.4 0.0 copy-start.9
  34.5 6.0 %second_part.1.n2b = bf16[2,3,128,384]{3,2,1,0:T(8,128)(2,1)S(1)} custom-call(bf16[4,512,768]{2,1,0:T(8,128)(2,1)S(1)} %get-tuple-element.28.hs, bf16[4,5,64,384]{3,2,1,0:T(8,128)(2,1)S(1)} %get-tuple-element.34.v0, bf16[4,5,64,384]{3,2,1,0:T(8,128)(2,1)S(1)} %get-tuple-element.35.v1, bf16[4,8,64,384]{3,2,1,0:T(8,128)(2,1)S(1)} %get-tuple-element.29.v2, ...), custom_call_target="tpu_custom_call" | custom-call | flops 200000000 | bytes 200000 | tf_op jit(solution)/shard_map/second_part/pallas_call | solution.py:637
  40.5 1.6 %collective-permute-start.7 = (bf16[2,3,128,384]{3,2,1,0:T(8,128)(2,1)S(1)}, bf16[2,3,128,384]{3,2,1,0:T(8,128)(2,1)S(1)}, u32[]{:S(2)}, u32[]{:S(2)}) collective-permute-start(bf16[2,3,128,384]{3,2,1,0:T(8,128)(2,1)S(1)} %second_part.1.n2b), channel_id=1, source_target_pairs={{0,4},{4,8},{8,12},{12,16},{16,20},{20,24},{24,28},{1,5},{5,9},{9,... | collective-permute-start | bytes 1769480 | tf_op jit(solution)/shard_map/ppermute | solution.py:17
  42.1 1.4 %summed_kernels.1.u = bf16[2,9,384,384]{3,2,1,0:T(8,128)(2,1)S(1)} custom-call(bf16[9,3,384,384]{3,2,1,0:T(8,128)(2,1)S(1)} %bitcast.11), custom_call_target="tpu_custom_call" | custom-call | flops 7962624 | bytes 13271040 | tf_op jit(solution)/shard_map/summed_kernels/pallas_call | solution.py:228
  43.6 4.1 %own_frames.1 = (f32[2,4,128,384]{3,2,1,0:T(8,128)S(1)}, bf16[4,3,64,384]{3,2,1,0:T(8,128)(2,1)S(1)}, bf16[4,3,64,384]{3,2,1,0:T(8,128)(2,1)S(1)}) custom-call(bf16[2,3,128,384]{3,2,1,0:T(8,128)(2,1)S(1)} %get-tuple-element.33.n2a, bf16[2,3,128,384]{3,2,1,0:T(8,128)(2,1)S(1)} %second_part.1.n2b, bf16[2,3,128,384]{3,2,1,0:T(8,128)(2,1)S(1)} %collective-permute-done.6.earlier, ...), custom_call_target="tpu_custom_call" | custom-call | flops 4000000000 | bytes 4000000 | tf_op jit(solution)/shard_map/own_frames/pallas_call | solution.py:656
  47.7 5.1 %earlier_frames.1 = bf16[2,4,128,384]{3,2,1,0:T(8,128)(2,1)} custom-call(bf16[4,3,64,384]{3,2,1,0:T(8,128)(2,1)S(1)} %get-tuple-element.38.ve0, bf16[4,3,64,384]{3,2,1,0:T(8,128)(2,1)S(1)} %get-tuple-element.39.ve1, bf16[2,3,128,384]{3,2,1,0:T(8,128)(2,1)S(1)} %collective-permute-done.7.earlier, bf16[2,4,128,384]{3,2,1,0:T(8,128)(2,1)S(1)} %get-tuple-element.36.placed, ...), custom_call_target="tpu_custom_call" | custom-call | flops 4000000000 | bytes 4000000 | tf_op jit(solution)/shard_map/earlier_frames/pallas_call | solution.py:674
  (32 shorter events, 0.1 us)
Async XLA Ops:
  0.0 12.8 %copy-start.4 = (bf16[2,4,128,16]{2,3,1,0:T(8,128)(2,1)S(1)}, bf16[2,4,128,16]{2,3,1,0:T(8,128)(2,1)}, u32[]{:S(2)}) copy-start(bf16[2,4,128,16]{2,3,1,0:T(8,128)(2,1)} %param.12) | copy-start | bytes 98308
  0.0 12.8 %copy-start.3 = (bf16[2,4,128,16]{2,3,1,0:T(8,128)(2,1)S(1)}, bf16[2,4,128,16]{2,3,1,0:T(8,128)(2,1)}, u32[]{:S(2)}) copy-start(bf16[2,4,128,16]{2,3,1,0:T(8,128)(2,1)} %param.13) | copy-start | bytes 98308
  0.0 12.9 %collective-permute-start = (bf16[128,128]{1,0:T(8,128)(2,1)}, bf16[128,128]{1,0:T(8,128)(2,1)S(1)}, u32[]{:S(2)}, u32[]{:S(2)}) collective-permute-start(bf16[128,128]{1,0:T(8,128)(2,1)} %bitcast.21), channel_id=1, source_target_pairs={{0,4},{4,8},{8,12},{12,16},{16,20},{20,24},{24,28},{1,5},{5,9},{9,... | collective-permute-start | bytes 98312 | tf_op jit(solution)/shard_map/ppermute | solution.py:17
  2.5 10.5 %collective-permute-start.1 = (bf16[128,128]{1,0:T(8,128)(2,1)}, bf16[128,128]{1,0:T(8,128)(2,1)S(1)}, u32[]{:S(2)}, u32[]{:S(2)}) collective-permute-start(bf16[128,128]{1,0:T(8,128)(2,1)} %bitcast.22), channel_id=1, source_target_pairs={{0,8},{4,12},{8,16},{12,20},{16,24},{20,28},{1,9},{5,13},{9,17},{1... | collective-permute-start | bytes 98312 | tf_op jit(solution)/shard_map/ppermute | solution.py:17
  9.3 17.7 %collective-permute-start.4 = (bf16[2,3,128,384]{3,2,1,0:T(8,128)(2,1)S(1)}, bf16[2,3,128,384]{3,2,1,0:T(8,128)(2,1)S(1)}, u32[]{:S(2)}, u32[]{:S(2)}) collective-permute-start(bf16[2,3,128,384]{3,2,1,0:T(8,128)(2,1)S(1)} %pad_maximum_fusion), channel_id=1, source_target_pairs={{0,1},{1,2},{2,3}} | collective-permute-start | bytes 1769480 | tf_op jit(solution)/shard_map/ppermute | solution.py:22
  12.8 6.7 %slice-start.2 = ((s8[7962624]{0:T(1024)(128)(4,1)}), s8[4194304]{0:T(1024)(128)(4,1)S(1)}, s32[]{:S(2)}) async-start(s8[7962624]{0:T(1024)(128)(4,1)} %bitcast.14), calls=%async_computation.2 | async-start | bytes 8388608
  12.8 6.6 %copy-start.5 = (f32[384]{0:T(512)S(1)}, f32[384]{0:T(512)}, u32[]{:S(2)}) copy-start(f32[384]{0:T(512)} %param.17) | copy-start | bytes 4612
  12.9 6.6 %copy-start.6 = (f32[384]{0:T(512)S(1)}, f32[384]{0:T(512)}, u32[]{:S(2)}) copy-start(f32[384]{0:T(512)} %param.18) | copy-start | bytes 4612
  12.9 6.6 %copy-start.7 = (f32[384]{0:T(512)S(1)}, f32[384]{0:T(512)}, u32[]{:S(2)}) copy-start(f32[384]{0:T(512)} %param.20) | copy-start | bytes 4612
  12.9 6.6 %copy-start.8 = (f32[384]{0:T(512)S(1)}, f32[384]{0:T(512)}, u32[]{:S(2)}) copy-start(f32[384]{0:T(512)} %param.21) | copy-start | bytes 4612
  12.9 6.6 %slice-start.3 = ((s8[7962624]{0:T(1024)(128)(4,1)}), s8[3768320]{0:T(1024)(128)(4,1)S(1)}, s32[]{:S(2)}) async-start(s8[7962624]{0:T(1024)(128)(4,1)} %bitcast.14), calls=%async_computation.3 | async-start | bytes 7536640
  12.9 6.6 %copy-start = (bf16[2,4,128,384]{3,2,1,0:T(8,128)(2,1)S(1)}, bf16[2,4,128,384]{3,2,1,0:T(8,128)(2,1)}, u32[]{:S(2)}) copy-start(bf16[2,4,128,384]{3,2,1,0:T(8,128)(2,1)} %cache_one.1) | copy-start | bytes 2359300
  12.9 6.6 %copy-start.1 = (bf16[2,4,128,384]{3,2,1,0:T(8,128)(2,1)S(1)}, bf16[2,4,128,384]{3,2,1,0:T(8,128)(2,1)}, u32[]{:S(2)}) copy-start(bf16[2,4,128,384]{3,2,1,0:T(8,128)(2,1)} %cache_two.1) | copy-start | bytes 2359300
  12.9 6.6 %copy-start.2 = (bf16[3,3,3,16,384]{4,3,2,1,0:T(8,128)(2,1)S(1)}, bf16[3,3,3,16,384]{4,3,2,1,0:T(8,128)(2,1)}, u32[]{:S(2)}) copy-start(bf16[3,3,3,16,384]{4,3,2,1,0:T(8,128)(2,1)} %param.16) | copy-start | bytes 995332
  13.0 8.7 %collective-permute-start.2 = (bf16[288,128]{1,0:T(8,128)(2,1)S(1)}, bf16[288,128]{1,0:T(8,128)(2,1)S(1)}, u32[]{:S(2)}, u32[]{:S(2)}) collective-permute-start(bf16[288,128]{1,0:T(8,128)(2,1)S(1)} %get-tuple-element.25), channel_id=1, source_target_pairs={{0,1},{1,2},{2,3},{4,5},{5,6},{6,7},{8,9},{9,10},{10,11},{12,13},{... | collective-permute-start | bytes 221192 | tf_op jit(solution)/shard_map/ppermute | solution.py:17
  16.7 6.2 %collective-permute-start.3 = (bf16[288,128]{1,0:T(8,128)(2,1)S(1)}, bf16[288,128]{1,0:T(8,128)(2,1)S(1)}, u32[]{:S(2)}, u32[]{:S(2)}) collective-permute-start(bf16[288,128]{1,0:T(8,128)(2,1)S(1)} %get-tuple-element.26), channel_id=1, source_target_pairs={{1,0},{2,1},{3,2},{5,4},{6,5},{7,6},{9,8},{10,9},{11,10},{13,12},{... | collective-permute-start | bytes 221192 | tf_op jit(solution)/shard_map/ppermute | solution.py:17
  18.1 16.3 %collective-permute-start.5 = (bf16[2,3,128,384]{3,2,1,0:T(8,128)(2,1)S(1)}, bf16[2,3,128,384]{3,2,1,0:T(8,128)(2,1)S(1)}, u32[]{:S(2)}, u32[]{:S(2)}) collective-permute-start(bf16[2,3,128,384]{3,2,1,0:T(8,128)(2,1)S(1)} %pad_maximum_fusion.1), channel_id=1, source_target_pairs={{1,0},{2,1},{3,2}} | collective-permute-start | bytes 1769480 | tf_op jit(solution)/shard_map/ppermute | solution.py:22
  33.1 10.5 %collective-permute-start.6 = (bf16[2,3,128,384]{3,2,1,0:T(8,128)(2,1)S(1)}, bf16[2,3,128,384]{3,2,1,0:T(8,128)(2,1)S(1)}, u32[]{:S(2)}, u32[]{:S(2)}) collective-permute-start(bf16[2,3,128,384]{3,2,1,0:T(8,128)(2,1)S(1)} %get-tuple-element.33.n2a), channel_id=1, source_target_pairs={{0,4},{4,8},{8,12},{12,16},{16,20},{20,24},{24,28},{1,5},{5,9},{9,... | collective-permute-start | bytes 1769480 | tf_op jit(solution)/shard_map/ppermute | solution.py:17
  34.4 7.7 %slice-start = ((s8[7962624]{0:T(1024)(128)(4,1)}), s8[4194304]{0:T(1024)(128)(4,1)S(1)}, s32[]{:S(2)}) async-start(s8[7962624]{0:T(1024)(128)(4,1)} %bitcast.9), calls=%async_computation | async-start | bytes 8388608
  34.4 7.6 %copy-start.9 = (f32[384]{0:T(512)S(1)}, f32[384]{0:T(512)}, u32[]{:S(2)}) copy-start(f32[384]{0:T(512)} %param.23) | copy-start | bytes 4612
  34.4 7.6 %slice-start.1 = ((s8[7962624]{0:T(1024)(128)(4,1)}), s8[3768320]{0:T(1024)(128)(4,1)S(1)}, s32[]{:S(2)}) async-start(s8[7962624]{0:T(1024)(128)(4,1)} %bitcast.9), calls=%async_computation.1 | async-start | bytes 7536640
  40.5 7.2 %collective-permute-start.7 = (bf16[2,3,128,384]{3,2,1,0:T(8,128)(2,1)S(1)}, bf16[2,3,128,384]{3,2,1,0:T(8,128)(2,1)S(1)}, u32[]{:S(2)}, u32[]{:S(2)}) collective-permute-start(bf16[2,3,128,384]{3,2,1,0:T(8,128)(2,1)S(1)} %second_part.1.n2b), channel_id=1, source_target_pairs={{0,4},{4,8},{8,12},{12,16},{16,20},{20,24},{24,28},{1,5},{5,9},{9,... | collective-permute-start | bytes 1769480 | tf_op jit(solution)/shard_map/ppermute | solution.py:17
